TPU v7x, 128 devices: a whole 4x4x4 slice. The times are simulated.
128 devices in a mesh: fsdp: 16 (over z, y), rep: 8 (over x, core).
Axes of the slice: x: 4, y: 4, z: 4, core: 2. Of those that a mesh axis runs over, the one named last changes fastest.
Arguments:
- gradient: bfloat16 [8192, 4096], P('fsdp', 'rep'), may hold values from -0.1875 to 0.1875
- first_moment: float32 [8192, 4096], P('fsdp', 'rep'), may hold values from -0.1875 to 0.1875
- second_moment: float32 [8192, 4096], P('fsdp', 'rep'), may hold values from 0.0001 to 0.004
- factors: float32 [256, 1024, 1024], P(('fsdp', 'rep')), may hold values from -0.125 to 0.125
- eigen_bases: bfloat16 [256, 1024, 1024], P(('fsdp', 'rep')), may hold values from -0.1875 to 0.1875
- owners: int32 [64], replicated, may hold values from 0 to 127, as said below
Outputs:
- update: float32 [8192, 4096], P('fsdp', 'rep')
- new_first: float32 [8192, 4096], P('fsdp', 'rep')
- new_second: float32 [8192, 4096], P('fsdp', 'rep')
- new_factors: float32 [256, 1024, 1024], P(('fsdp', 'rep'))
Inputs may be any that keep to these rules, and one draw needn't show every extreme that they name: `owners`: no device is named by more than 2 items, and in every draw some devices are named by exactly 2.
All inputs are finite; a program needn't handle non-finite values.
Results may differ from a plain program's by a relative error of at most 0.0041.
Values may be sent and summed in bfloat16 or wider, within the bound.
No kernel may reach another device: no remote copies, remote signals or barrier semaphores. Data moves between devices by JAX's collectives and lax.ppermute only.
A program may use at most 128 MiB of HBM per device.

v0:
```python
import functools

import jax
import jax.numpy as jnp
from jax import lax
from jax.experimental import pallas as pl
from jax.experimental.pallas import tpu as pltpu
from jax.sharding import PartitionSpec as P

beta_one = 0.9
beta_two = 0.95
shampoo_beta = 0.95
epsilon = 1e-08

SUB = 8
GB = 256
PAIRS = (
    ((0, 0), (0, 1), (0, 2), (0, 3), (1, 1)),
    ((1, 2), (1, 3), (2, 2), (2, 3), (3, 3)),
)
BOTH = ("fsdp", "rep")
PARAMS = pltpu.CompilerParams(vmem_limit_bytes=56 * 2**20)


def swap_neighbour(value, axis):
    pairs = [(source, source ^ 1) for source in range(lax.axis_size(axis))]
    return lax.ppermute(value, axis, pairs)


def dot_nn(left, right):
    return jnp.dot(left, right, preferred_element_type=jnp.float32)


def dot_tn(left, right):
    return lax.dot_general(
        left, right, (((0,), (0,)), ((), ())), preferred_element_type=jnp.float32
    )


def dot_nt(left, right):
    return lax.dot_general(
        left, right, (((1,), (1,)), ((), ())), preferred_element_type=jnp.float32
    )


def whole(memory_space=pltpu.VMEM):
    return pl.BlockSpec(memory_space=memory_space)


def interleave_kernel(src_ref, dst_ref):
    dst_ref[:, 0] = src_ref[0]


def interleave(bases, devices):
    slots, size, _ = bases.shape
    parts = bases.reshape(slots, devices, SUB, size)
    step = devices // 4
    return pl.pallas_call(
        interleave_kernel,
        grid=(4, slots),
        in_specs=[pl.BlockSpec((1, step, SUB, size), lambda p, s: (s, p, 0, 0))],
        out_specs=pl.BlockSpec((step, 1, SUB, size), lambda p, s: (p, s, 0, 0)),
        out_shape=jax.ShapeDtypeStruct((devices, slots, SUB, size), bases.dtype),
        compiler_params=PARAMS,
        name="interleave",
    )(parts)


def place_quads(row, col, quads, block_ref):
    half = quads[0].shape[0]
    for dr in range(2):
        for dc in range(2):
            at = (pl.multiple_of((row ^ dr) * half, half), pl.multiple_of((col ^ dc) * half, half))
            block_ref[pl.ds(at[0], half), pl.ds(at[1], half)] = quads[2 * dr + dc][...]


def gram_kernel(place_ref, own_ref, side_ref, below_ref, cross_ref, out_ref, block_ref):
    row = place_ref[0]
    col = place_ref[1]
    place_quads(row, col, (own_ref, side_ref, below_ref, cross_ref), block_ref)

    def emit(left_gram, which):
        for n, (first, second) in enumerate(PAIRS[which]):
            a = slice(first * GB, (first + 1) * GB)
            b = slice(second * GB, (second + 1) * GB)
            if left_gram:
                value = dot_nt(block_ref[a, :], block_ref[b, :])
            else:
                value = dot_tn(block_ref[:, a], block_ref[:, b])
            for half in range(2):
                tiles = value[:, half * 128 : (half + 1) * 128].reshape(GB // 8, 8, 128)
                tiles = tiles.astype(jnp.bfloat16)
                for r in (n // 2,) if n < 4 else (0, 1):
                    t = n % 2 if n < 4 else 2
                    out_ref[:, 2 * half + r, :, t * 128 : (t + 1) * 128] = tiles

    for left_gram in (True, False):
        for which in range(2):
            pl.when((col == (0 if left_gram else 1)) & (row == which))(
                functools.partial(emit, left_gram, which)
            )


def gram_pieces(place, quads):
    size = 2 * quads[0].shape[0]
    return pl.pallas_call(
        gram_kernel,
        in_specs=[whole(pltpu.SMEM)] + [whole()] * 4,
        out_specs=whole(),
        out_shape=jax.ShapeDtypeStruct((32, 4, 8, 384), jnp.bfloat16),
        scratch_shapes=[pltpu.VMEM((size, size), jnp.bfloat16)],
        compiler_params=PARAMS,
        cost_estimate=pl.CostEstimate(flops=7 * 10**8, bytes_accessed=3 * 10**6, transcendentals=0),
        name="gram_pieces",
    )(place, *quads)


def second_kernel(codes_ref, rows_ref, gram_ref, out_ref):
    out_ref[:, :, 768:] = gram_ref[...]

    @pl.loop(0, 32)
    def _(block):
        left = rows_ref[codes_ref[2 * block]]
        right = rows_ref[codes_ref[2 * block + 1]]
        base = (block // 4) * 16 + (block % 4) * 2
        for i in range(2):
            at = base + 8 * i
            out_ref[at, :, 0:512] = left[:, 512 * i : 512 * (i + 1)]
            out_ref[at, :, 512:768] = right[:, 0:256]
            out_ref[at + 1, :, 0:768] = right[:, 256:1024]


def second_operand(codes, rows, gram):
    return pl.pallas_call(
        second_kernel,
        in_specs=[whole(pltpu.SMEM), whole(), whole()],
        out_specs=whole(),
        out_shape=jax.ShapeDtypeStruct((128, SUB, 1152), jnp.bfloat16),
        compiler_params=PARAMS,
        cost_estimate=pl.CostEstimate(flops=0, bytes_accessed=8 * 10**6, transcendentals=0),
        name="second_operand",
    )(codes, rows, gram)


def third_kernel(codes_ref, place_ref, got_ref, out_ref):
    core = place_ref[1]

    @pl.loop(0, 64)
    def _(item):
        block = item // 2
        at = codes_ref[item]
        upper = (block // 4) * 16 + (block % 4) * 2 + item % 2
        lower = upper + 8
        out_ref[at, :, 0:256] = got_ref[upper, :, 0:256]
        out_ref[at, :, 256:512] = got_ref[lower, :, 0:256]
        out_ref[at, :, 512:640] = got_ref[upper + 8 * core, :, 256:384]


def third_operand(codes, place, got):
    return pl.pallas_call(
        third_kernel,
        grid=(1,),
        in_specs=[
            whole(pltpu.SMEM),
            whole(pltpu.SMEM),
            pl.BlockSpec((128, SUB, 384), lambda _: (0, 0, 2)),
        ],
        out_specs=pl.BlockSpec((256, SUB, 640), lambda _: (0, 0, 0)),
        out_shape=jax.ShapeDtypeStruct((256, SUB, 640), jnp.bfloat16),
        compiler_params=PARAMS,
        cost_estimate=pl.CostEstimate(flops=0, bytes_accessed=4 * 10**6, transcendentals=0),
        name="third_operand",
    )(codes, place, got)


def rotate_kernel(
    place_ref,
    own_ref,
    side_ref,
    below_ref,
    cross_ref,
    mine_ref,
    theirs_ref,
    first_ref,
    second_ref,
    new_first_ref,
    new_second_ref,
    direction_ref,
    block_ref,
    left_ref,
    right_ref,
):
    row = place_ref[0]
    col = place_ref[1]
    place_quads(row, col, (own_ref, side_ref, below_ref, cross_ref), block_ref)

    @pl.when(col == 0)
    def _():
        left_ref[...] = mine_ref[:, :, 0:512]
        right_ref[:, :, 0:256] = mine_ref[:, :, 512:768]
        right_ref[:, :, 256:512] = theirs_ref[:, :, 0:256]

    @pl.when(col == 1)
    def _():
        left_ref[...] = theirs_ref[:, :, 0:512]
        right_ref[...] = mine_ref[:, :, 256:768]

    left = left_ref[...].reshape(1024, 512)
    left_rot = dot_tn(left, block_ref[...]).astype(jnp.bfloat16)
    rotated = dot_nn(left_rot, right_ref[...].reshape(1024, 512))
    new_first = beta_one * first_ref[...] + (1.0 - beta_one) * rotated
    new_second = beta_two * second_ref[...] + (1.0 - beta_two) * rotated * rotated
    new_first_ref[...] = new_first
    new_second_ref[...] = new_second
    direction_ref[...] = (new_first / (jnp.sqrt(new_second) + epsilon)).astype(jnp.bfloat16)


def rotate(place, quads, mine, theirs, first, second):
    half = first.shape[0]
    return pl.pallas_call(
        rotate_kernel,
        grid=(1,),
        in_specs=[whole(pltpu.SMEM)]
        + [pl.BlockSpec((half, half), lambda _: (0, 0))] * 4
        + [pl.BlockSpec((128, SUB, 768), lambda _: (0, 0, 0))] * 2
        + [pl.BlockSpec((half, half), lambda _: (0, 0))] * 2,
        out_specs=[pl.BlockSpec((half, half), lambda _: (0, 0))] * 3,
        out_shape=[
            jax.ShapeDtypeStruct((half, half), jnp.float32),
            jax.ShapeDtypeStruct((half, half), jnp.float32),
            jax.ShapeDtypeStruct((half, half), jnp.bfloat16),
        ],
        scratch_shapes=[
            pltpu.VMEM((1024, 1024), jnp.bfloat16),
            pltpu.VMEM((128, SUB, 512), jnp.bfloat16),
            pltpu.VMEM((128, SUB, 512), jnp.bfloat16),
        ],
        compiler_params=PARAMS,
        cost_estimate=pl.CostEstimate(
            flops=16 * 10**8, bytes_accessed=10**7, transcendentals=10**6
        ),
        name="rotate",
    )(place, *quads, mine, theirs, first, second)


def back_kernel(
    place_ref,
    own_ref,
    side_ref,
    mine_ref,
    theirs_ref,
    keep_ref,
    give_ref,
    left_ref,
    right_ref,
    strip_ref,
):
    row = place_ref[0]
    col = place_ref[1]
    half = own_ref.shape[0]
    strip_ref[:, pl.ds(pl.multiple_of(col * half, half), half)] = own_ref[...]
    strip_ref[:, pl.ds(pl.multiple_of((1 - col) * half, half), half)] = side_ref[...]

    @pl.when(col == 0)
    def _():
        left_ref[...] = mine_ref[:, :, 0:512]
        right_ref[:, :, 0:256] = mine_ref[0:64, :, 512:768]
        right_ref[:, :, 256:1024] = theirs_ref[0:64]

    @pl.when(col == 1)
    def _():
        left_ref[...] = theirs_ref[:, :, 0:512]
        right_ref[:, :, 0:256] = theirs_ref[64:128, :, 512:768]
        right_ref[:, :, 256:1024] = mine_ref[64:128]

    half_back = dot_nt(strip_ref[...], right_ref[...].reshape(512, 1024)).astype(jnp.bfloat16)
    groups = half // SUB
    keep = left_ref[pl.ds(row * groups, groups)].reshape(half, 512)
    give = left_ref[pl.ds((1 - row) * groups, groups)].reshape(half, 512)
    keep_ref[...] = dot_nn(keep, half_back)
    give_ref[...] = dot_nn(give, half_back).astype(jnp.bfloat16)


def back(place, own, side, mine, theirs):
    half = own.shape[0]
    return pl.pallas_call(
        back_kernel,
        grid=(1,),
        in_specs=[whole(pltpu.SMEM)]
        + [pl.BlockSpec((half, half), lambda _: (0, 0))] * 2
        + [pl.BlockSpec((128, SUB, 768), lambda _: (0, 0, 0))] * 2,
        out_specs=[pl.BlockSpec((half, half), lambda _: (0, 0))] * 2,
        out_shape=[
            jax.ShapeDtypeStruct((half, half), jnp.float32),
            jax.ShapeDtypeStruct((half, half), jnp.bfloat16),
        ],
        scratch_shapes=[
            pltpu.VMEM((128, SUB, 512), jnp.bfloat16),
            pltpu.VMEM((64, SUB, 1024), jnp.bfloat16),
            pltpu.VMEM((half, 2 * half), jnp.bfloat16),
        ],
        compiler_params=PARAMS,
        cost_estimate=pl.CostEstimate(flops=11 * 10**8, bytes_accessed=6 * 10**6, transcendentals=0),
        name="back",
    )(place, own, side, mine, theirs)


def factor_kernel(live_ref, factor_ref, got_ref, out_ref):
    slot = pl.program_id(0)
    strip = pl.program_id(1)
    live = live_ref[slot] != 0

    def piece(first, second):
        which, n = next(
            (w, n) for w in range(2) for n in range(5) if PAIRS[w][n] == (first, second)
        )
        r = n // 2 if n < 4 else which
        lane = 2 * which + n % 2 if n < 4 else 4
        halves = [
            got_ref[:, 2 * h + r, slot, :, lane * 128 : (lane + 1) * 128]
            .astype(jnp.float32)
            .reshape(GB, 128)
            for h in range(2)
        ]
        return jnp.concatenate(halves, axis=1)

    def mix(row):
        for col in range(4):
            value = piece(row, col) if row <= col else piece(col, row).T
            at = slice(col * GB, (col + 1) * GB)
            out_ref[0, :, at] = (
                shampoo_beta * factor_ref[0, :, at] + (1.0 - shampoo_beta) * value
            )

    for row in range(4):
        pl.when(live & (strip == row))(functools.partial(mix, row))

    @pl.when(jnp.logical_not(live))
    def _():
        out_ref[...] = factor_ref[...]


def update_factors(live, factors, got):
    slots, size, _ = factors.shape
    got = got.reshape(32, 4, slots, SUB, 640)
    return pl.pallas_call(
        factor_kernel,
        grid=(slots, 4),
        in_specs=[
            whole(pltpu.SMEM),
            pl.BlockSpec((1, GB, size), lambda s, p: (s, p, 0)),
            whole(),
        ],
        out_specs=pl.BlockSpec((1, GB, size), lambda s, p: (s, p, 0)),
        out_shape=jax.ShapeDtypeStruct(factors.shape, factors.dtype),
        compiler_params=PARAMS,
        cost_estimate=pl.CostEstimate(
            flops=4 * 10**6, bytes_accessed=2 * 10**7, transcendentals=0
        ),
        name="update_factors",
    )(live, factors, got)


def shards(gradient, first_moment, second_moment, factors, eigen_bases, owners):
    devices = lax.axis_size("fsdp") * lax.axis_size("rep")
    slots = factors.shape[0]
    size = factors.shape[1]
    item_count = owners.shape[0]
    fsdp_index = lax.axis_index("fsdp")
    rep_index = lax.axis_index("rep")
    my_index = fsdp_index * lax.axis_size("rep") + rep_index
    place = jnp.stack([fsdp_index % 2, rep_index % 2]).astype(jnp.int32)

    first_parts = interleave(eigen_bases, devices)
    first_got = lax.all_to_all(first_parts, BOTH, 0, 0, tiled=True)

    item_index = jnp.arange(item_count, dtype=jnp.int32)
    earlier_same = (owners[:, None] == owners[None, :]) & (
        item_index[None, :] < item_index[:, None]
    )
    codes = slots * owners + jnp.sum(earlier_same.astype(jnp.int32), axis=1)
    my_codes = my_index * slots + jnp.arange(slots, dtype=jnp.int32)
    live = jnp.sum((codes[None, :] == my_codes[:, None]).astype(jnp.int32), axis=1)

    side = swap_neighbour(gradient, "rep")
    below = swap_neighbour(gradient, "fsdp")
    cross = swap_neighbour(below, "rep")
    quads = (gradient, side, below, cross)
    gram = gram_pieces(place, quads).reshape(devices, SUB, 384)

    second_parts = second_operand(codes, first_got.reshape(devices * slots, SUB, size), gram)
    mine = lax.all_to_all(second_parts, BOTH, 0, 0, tiled=True)
    theirs = swap_neighbour(mine[:, :, :768], "rep")

    third_parts = third_operand(codes, place, mine).reshape(devices, slots, SUB, 640)
    third_got = lax.all_to_all(third_parts, BOTH, 0, 0, tiled=True)

    new_first, new_second, direction = rotate(
        place, quads, mine, theirs, first_moment, second_moment
    )
    other = swap_neighbour(direction, "rep")
    keep, give = back(place, direction, other, mine, theirs)
    update = keep + swap_neighbour(give, "fsdp").astype(jnp.float32)
    new_factors = update_factors(live, factors, third_got)
    return (update, new_first, new_second, new_factors)


def solution(mesh):
    in_specs = (
        P("fsdp", "rep"),
        P("fsdp", "rep"),
        P("fsdp", "rep"),
        P(("fsdp", "rep"), None, None),
        P(("fsdp", "rep"), None, None),
        P(),
    )
    out_specs = (
        P("fsdp", "rep"),
        P("fsdp", "rep"),
        P("fsdp", "rep"),
        P(("fsdp", "rep"), None, None),
    )
    return jax.shard_map(shards, mesh=mesh, in_specs=in_specs, out_specs=out_specs, check_vma=False)
```

profile of v0, /device:TPU:1, one launch (start us, length us, event | category | flops | bytes accessed | tf_op | source)
XLA Modules:
  0.0 189.3 jit_solution(17061806531906363171)
XLA Ops:
  0.6 6.6 %interleave.1 = bf16[128,2,8,1024]{3,2,1,0:T(8,128)(2,1)} custom-call(bf16[2,128,8,1024]{3,2,1,0:T(8,128)(2,1)} %bitcast.9), custom_call_target="tpu_custom_call" | custom-call | tf_op jit(solution)/shard_map/interleave/pallas_call | solution.py:58
  7.2 12.0 %all-to-all-start = ((bf16[128,2,8,1024]{3,2,1,0:T(8,128)(2,1)}), bf16[128,2,8,1024]{3,2,1,0:T(8,128)(2,1)}, u32[]{:S(2)}, u32[]{:S(2)}) async-start(bf16[128,2,8,1024]{3,2,1,0:T(8,128)(2,1)} %interleave.1), calls=%async_computation | async-start | bytes 8388608 | tf_op jit(solution)/shard_map/all_to_all | solution.py:375
  19.2 1.5 collective-permute-start.1
  20.7 0.6 collective-permute-start
  21.3 55.1 %collective-permute-done.1.below_ref = bf16[512,512]{1,0:T(8,128)(2,1)S(1)} collective-permute-done((bf16[512,512]{1,0:T(8,128)(2,1)S(1)}, bf16[512,512]{1,0:T(8,128)(2,1)S(1)}, u32[]{:S(2)}, u32[]{:S(2)}) %collective-permute-start.1) | collective-permute-done | bytes 524320 | tf_op jit(solution)/shard_map/ppermute | solution.py:27
  76.4 0.9 collective-permute-start.2
  79.4 0.8 copy-done.5
  80.2 3.5 %gram_pieces.1 = bf16[32,4,8,384]{3,2,1,0:T(8,128)(2,1)} custom-call(s32[2]{0:T(128)} %pad_add_fusion.place_ref, bf16[512,512]{1,0:T(8,128)(2,1)} %own_ref.3, bf16[512,512]{1,0:T(8,128)(2,1)} %copy-done.4, bf16[512,512]{1,0:T(8,128)(2,1)} %copy-done.3, bf16[512,512]{1,0:T(8,128)(2,1)} %copy-done.5), custom_call_target="tpu_custom_call" | custom-call | flops 700000000 | bytes 3000000 | tf_op jit(solution)/shard_map/gram_pieces/pallas_call | solution.py:106
  83.7 4.3 %second_operand.1 = bf16[128,8,1152]{2,1,0:T(8,128)(2,1)} custom-call(s32[64]{0:T(128)} %multiply_add_fusion.codes_ref, bf16[256,8,1024]{2,1,0:T(8,128)(2,1)} %bitcast.3.rows_ref, bf16[128,8,384]{2,1,0:T(8,128)(2,1)} %bitcast.10), custom_call_target="tpu_custom_call" | custom-call | bytes 8000000 | tf_op jit(solution)/shard_map/second_operand/pallas_call | solution.py:134
  88.0 42.3 %all_to_all.15.mine_ref.got_ref = bf16[128,8,1152]{2,1,0:T(8,128)(2,1)S(1)} all-to-all(bf16[128,8,1152]{2,1,0:T(8,128)(2,1)} %second_operand.1), channel_id=1, replica_groups=mesh['fsdp'=16,'rep'=8] {'fsdp','rep'}, dimensions={0} | all-to-all | bytes 4718592 | tf_op jit(solution)/shard_map/all_to_all | solution.py:392
  130.4 1.3 slice.4
  131.7 1.0 collective-permute-start.3
  132.7 3.7 %third_operand.1 = bf16[256,8,640]{2,1,0:T(8,128)(2,1)} custom-call(s32[64]{0:T(128)} %multiply_add_fusion.codes_ref, s32[2]{0:T(128)} %pad_add_fusion.place_ref, bf16[128,8,1152]{2,1,0:T(8,128)(2,1)} %copy-done), custom_call_target="tpu_custom_call" | custom-call | bytes 4000000 | tf_op jit(solution)/shard_map/third_operand/pallas_call | solution.py:160
  136.5 4.0 %all-to-all-start.2 = ((bf16[128,2,8,640]{3,2,1,0:T(8,128)(2,1)}), bf16[128,2,8,640]{3,2,1,0:T(8,128)(2,1)S(1)}, u32[]{:S(2)}, u32[]{:S(2)}) async-start(bf16[128,2,8,640]{3,2,1,0:T(8,128)(2,1)} %bitcast.7), calls=%async_computation.2 | async-start | bytes 5242880 | tf_op jit(solution)/shard_map/all_to_all | solution.py:396
  140.5 7.2 %rotate.1 = (f32[512,512]{1,0:T(8,128)}, f32[512,512]{1,0:T(8,128)}, bf16[512,512]{1,0:T(8,128)(2,1)}) custom-call(s32[2]{0:T(128)} %pad_add_fusion.place_ref, bf16[512,512]{1,0:T(8,128)(2,1)} %own_ref.3, bf16[512,512]{1,0:T(8,128)(2,1)} %copy-done.4, bf16[512,512]{1,0:T(8,128)(2,1)} %copy-done.3, bf16[512,512]{1,0:T(8,128)(2,1)} %copy-done.5, ...), custom_call_target="tpu_custom_call" | custom-call | flops 1600000000 | bytes 10000000 | tf_op jit(solution)/shard_map/rotate/pallas_call | solution.py:220
  147.7 1.2 collective-permute-start.4
  148.9 1.7 collective-permute-done.4.side_ref
  150.7 0.8 copy-done.7
  151.5 4.7 %back.1 = (f32[512,512]{1,0:T(8,128)}, bf16[512,512]{1,0:T(8,128)(2,1)}) custom-call(s32[2]{0:T(128)} %pad_add_fusion.place_ref, bf16[512,512]{1,0:T(8,128)(2,1)} %get-tuple-element.9.own_ref, bf16[512,512]{1,0:T(8,128)(2,1)} %copy-done.7, bf16[128,8,1152]{2,1,0:T(8,128)(2,1)} %copy-done, bf16[128,8,768]{2,1,0:T(8,128)(2,1)} %collective-permute-done.3.theirs_ref), custom_call_target="tpu_custom_call" | custom-call | flops 1100000000 | bytes 6000000 | tf_op jit(solution)/shard_map/back/pallas_call | solution.py:286
  156.8 0.7 fusion.1.live_ref
  157.5 19.2 %all-to-all-done.2 = bf16[128,2,8,640]{3,2,1,0:T(8,128)(2,1)S(1)} async-done(((bf16[128,2,8,640]{3,2,1,0:T(8,128)(2,1)}), bf16[128,2,8,640]{3,2,1,0:T(8,128)(2,1)S(1)}, u32[]{:S(2)}, u32[]{:S(2)}) %all-to-all-start.2) | async-done | bytes 2621472 | tf_op jit(solution)/shard_map/all_to_all | solution.py:396
  176.6 1.5 copy-done.1
  178.1 10.0 %update_factors.1 = f32[2,1024,1024]{2,1,0:T(8,128)} custom-call(s32[2]{0:T(128)} %fusion.1.live_ref, f32[2,1024,1024]{2,1,0:T(8,128)} %factor_ref.1, bf16[32,4,2,8,640]{4,3,2,1,0:T(8,128)(2,1)} %bitcast.8), custom_call_target="tpu_custom_call" | custom-call | flops 4000000 | bytes 20000000 | tf_op jit(solution)/shard_map/update_factors/pallas_call | solution.py:346
  188.1 1.1 convert_add_fusion
  (27 shorter events, 2.8 us)
Async XLA Ops:
  7.2 12.0 %copy-start.2 = (bf16[512,512]{1,0:T(8,128)(2,1)S(1)}, bf16[512,512]{1,0:T(8,128)(2,1)}, u32[]{:S(2)}) copy-start(bf16[512,512]{1,0:T(8,128)(2,1)} %own_ref.3) | copy-start | bytes 1572868
  7.2 70.7 %copy-start.9 = (s32[64]{0:T(128)S(1)}, s32[64]{0:T(128)}, u32[]{:S(2)}) copy-start(s32[64]{0:T(128)} %param.11) | copy-start | bytes 772
  7.2 76.5 %all-to-all-start = ((bf16[128,2,8,1024]{3,2,1,0:T(8,128)(2,1)}), bf16[128,2,8,1024]{3,2,1,0:T(8,128)(2,1)}, u32[]{:S(2)}, u32[]{:S(2)}) async-start(bf16[128,2,8,1024]{3,2,1,0:T(8,128)(2,1)} %interleave.1), calls=%async_computation | async-start | bytes 8388608 | tf_op jit(solution)/shard_map/all_to_all | solution.py:375
  19.2 57.2 %collective-permute-start.1 = (bf16[512,512]{1,0:T(8,128)(2,1)S(1)}, bf16[512,512]{1,0:T(8,128)(2,1)S(1)}, u32[]{:S(2)}, u32[]{:S(2)}) collective-permute-start(bf16[512,512]{1,0:T(8,128)(2,1)S(1)} %copy-done.2), channel_id=1, source_target_pairs={{0,8},{8,0},{16,24},{24,16},{32,40},{40,32},{48,56},{56,48},{64,72... | collective-permute-start | bytes 1572872 | tf_op jit(solution)/shard_map/ppermute | solution.py:27
  20.7 57.9 %collective-permute-start = (bf16[512,512]{1,0:T(8,128)(2,1)S(1)}, bf16[512,512]{1,0:T(8,128)(2,1)S(1)}, u32[]{:S(2)}, u32[]{:S(2)}) collective-permute-start(bf16[512,512]{1,0:T(8,128)(2,1)S(1)} %copy-done.2), channel_id=1, source_target_pairs={{0,1},{1,0},{2,3},{3,2},{4,5},{5,4},{6,7},{7,6},{8,9},{9,8},{10,11... | collective-permute-start | bytes 1572872 | tf_op jit(solution)/shard_map/ppermute | solution.py:27
  76.4 2.4 %copy-start.3 = (bf16[512,512]{1,0:T(8,128)(2,1)}, bf16[512,512]{1,0:T(8,128)(2,1)S(1)}, u32[]{:S(2)}) copy-start(bf16[512,512]{1,0:T(8,128)(2,1)S(1)} %collective-permute-done.1.below_ref) | copy-start | bytes 1572868
  76.4 2.4 %collective-permute-start.2 = (bf16[512,512]{1,0:T(8,128)(2,1)S(1)}, bf16[512,512]{1,0:T(8,128)(2,1)S(1)}, u32[]{:S(2)}, u32[]{:S(2)}) collective-permute-start(bf16[512,512]{1,0:T(8,128)(2,1)S(1)} %collective-permute-done.1.below_ref), channel_id=1, source_target_pairs={{0,1},{1,0},{2,3},{3,2},{4,5},{5,4},{6,7},{7,6},{8,9},{9,8},{10,11... | collective-permute-start | bytes 1572872 | tf_op jit(solution)/shard_map/ppermute | solution.py:27
  78.6 0.8 copy-start.4
  79.4 0.8 copy-start.5
  130.4 2.4 %copy-start = (bf16[128,8,1152]{2,1,0:T(8,128)(2,1)}, bf16[128,8,1152]{2,1,0:T(8,128)(2,1)S(1)}, u32[]{:S(2)}) copy-start(bf16[128,8,1152]{2,1,0:T(8,128)(2,1)S(1)} %all_to_all.15.mine_ref.got_ref) | copy-start | bytes 7077892
  131.7 8.8 %collective-permute-start.3 = (bf16[128,8,768]{2,1,0:T(8,128)(2,1)}, bf16[128,8,768]{2,1,0:T(8,128)(2,1)}, u32[]{:S(2)}, u32[]{:S(2)}) collective-permute-start(bf16[128,8,768]{2,1,0:T(8,128)(2,1)} %slice.4), channel_id=1, source_target_pairs={{0,1},{1,0},{2,3},{3,2},{4,5},{5,4},{6,7},{7,6},{8,9},{9,8},{10,11... | collective-permute-start | bytes 4718600 | tf_op jit(solution)/shard_map/ppermute | solution.py:27
  136.5 40.2 %all-to-all-start.2 = ((bf16[128,2,8,640]{3,2,1,0:T(8,128)(2,1)}), bf16[128,2,8,640]{3,2,1,0:T(8,128)(2,1)S(1)}, u32[]{:S(2)}, u32[]{:S(2)}) async-start(bf16[128,2,8,640]{3,2,1,0:T(8,128)(2,1)} %bitcast.7), calls=%async_computation.2 | async-start | bytes 5242880 | tf_op jit(solution)/shard_map/all_to_all | solution.py:396
  147.7 9.1 %copy-start.8 = (s32[64]{0:T(128)S(1)}, s32[64]{0:T(128)}, u32[]{:S(2)}) copy-start(s32[64]{0:T(128)} %multiply_add_fusion.codes_ref) | copy-start | bytes 772
  147.7 3.0 %collective-permute-start.4 = (bf16[512,512]{1,0:T(8,128)(2,1)}, bf16[512,512]{1,0:T(8,128)(2,1)S(1)}, u32[]{:S(2)}, u32[]{:S(2)}) collective-permute-start(bf16[512,512]{1,0:T(8,128)(2,1)} %get-tuple-element.9.own_ref), channel_id=1, source_target_pairs={{0,1},{1,0},{2,3},{3,2},{4,5},{5,4},{6,7},{7,6},{8,9},{9,8},{10,11... | collective-permute-start | bytes 1572872 | tf_op jit(solution)/shard_map/ppermute | solution.py:27
  150.7 0.8 copy-start.7
  156.2 32.0 %collective-permute-start.5 = (bf16[512,512]{1,0:T(8,128)(2,1)}, bf16[512,512]{1,0:T(8,128)(2,1)S(1)}, u32[]{:S(2)}, u32[]{:S(2)}) collective-permute-start(bf16[512,512]{1,0:T(8,128)(2,1)} %get-tuple-element.11), channel_id=1, source_target_pairs={{0,8},{8,0},{16,24},{24,16},{32,40},{40,32},{48,56},{56,48},{64,72... | collective-permute-start | bytes 1572872 | tf_op jit(solution)/shard_map/ppermute | solution.py:27
  176.6 1.5 copy-start.1
  178.1 10.0 %copy-start.6 = (f32[512,512]{1,0:T(8,128)S(1)}, f32[512,512]{1,0:T(8,128)}, u32[]{:S(2)}) copy-start(f32[512,512]{1,0:T(8,128)} %get-tuple-element.10) | copy-start | bytes 3145732
where the time goes:
time: 190 us; the launch traced here: 189 us
  waiting for transfers between devices  76.2 us (40%)
  blocking collectives  42.3 us (22%)
  Pallas kernels  40 us (21%)
  starting transfers between devices  21.8 us (11%)
  local copies, waits for them, and re-layouts  5.07 us (3%)
  other arithmetic  3.14 us (2%)
    ppermute x6, waiting for transfers between devices, swap_neighbour(): return lax.ppermute(value, axis, pairs)  57 us
    all_to_all x1, blocking collectives, shards(): mine = lax.all_to_all(second_parts, BOTH, 0, 0, tiled=True)  42.3 us
    all_to_all x1, waiting for transfers between devices, shards(): third_got = lax.all_to_all(third_parts, BOTH, 0, 0, tiled=True)  19.2 us
    all_to_all x1, starting transfers between devices, shards(): first_got = lax.all_to_all(first_parts, BOTH, 0, 0, tiled=True)  12 us
    pallas_call x1, Pallas kernels, update_factors(): pl.pallas_call(factor_kernel, grid=(slots, 4), in_specs=[whole(pltpu.SMEM...  10 us
    pallas_call x1, Pallas kernels, rotate(): pl.pallas_call(rotate_kernel, grid=(1,), in_specs=[whole(pltpu.SMEM)] + [...  7.2 us
    pallas_call x1, Pallas kernels, interleave(): pl.pallas_call(interleave_kernel, grid=(4, slots), in_specs=[pl.BlockSpec...  6.6 us
    ppermute x6, starting transfers between devices, swap_neighbour(): return lax.ppermute(value, axis, pairs)  5.82 us
  transfers between devices with their start and end apart: 8, of which 4 were waited for; matrix products, arithmetic and copies ran while one was open for 1% of the time, Pallas kernels for 15%

commit v1 on v0

--- a/solution.py
+++ b/solution.py
@@ -14,12 +14,10 @@
 
 SUB = 8
 GB = 256
-PAIRS = (
-    ((0, 0), (0, 1), (0, 2), (0, 3), (1, 1)),
-    ((1, 2), (1, 3), (2, 2), (2, 3), (3, 3)),
-)
+ABOVE = (((0, 1), (0, 2), (0, 3)), ((1, 2), (1, 3), (2, 3)))
+WIDTH = 2 * 128
 BOTH = ("fsdp", "rep")
-PARAMS = pltpu.CompilerParams(vmem_limit_bytes=56 * 2**20)
+PARAMS = pltpu.CompilerParams(vmem_limit_bytes=24 * 2**20)
 
 
 def swap_neighbour(value, axis):
@@ -47,23 +45,39 @@
     return pl.BlockSpec(memory_space=memory_space)
 
 
-def interleave_kernel(src_ref, dst_ref):
-    dst_ref[:, 0] = src_ref[0]
+def interleave_kernel(src_ref, dst_ref, held_ref, sems):
+    slots, devices = held_ref.shape[0], held_ref.shape[1]
+    stores = []
+    loads = []
+    for n in range(2 * slots):
+        slot, span = n % slots, pl.ds(n // slots * (devices // 2), devices // 2)
+        held = held_ref.at[slot, span]
+        loads.append(pltpu.make_async_copy(src_ref.at[slot, span], held, sems.at[0, n]))
+        stores.append(pltpu.make_async_copy(held, dst_ref.at[span, slot], sems.at[1, n]))
+        loads[n].start()
+    for load, store in zip(loads, stores):
+        load.wait()
+        store.start()
+    for store in stores:
+        store.wait()
 
 
 def interleave(bases, devices):
     slots, size, _ = bases.shape
     parts = bases.reshape(slots, devices, SUB, size)
-    step = devices // 4
     return pl.pallas_call(
         interleave_kernel,
-        grid=(4, slots),
-        in_specs=[pl.BlockSpec((1, step, SUB, size), lambda p, s: (s, p, 0, 0))],
-        out_specs=pl.BlockSpec((step, 1, SUB, size), lambda p, s: (p, s, 0, 0)),
-        out_shape=jax.ShapeDtypeStruct((devices, slots, SUB, size), bases.dtype),
-        compiler_params=PARAMS,
+        in_specs=[whole(pl.ANY)],
+        out_specs=whole(pl.ANY),
+        out_shape=pltpu.HBM((devices, slots, SUB, size), bases.dtype),
+        scratch_shapes=[
+            pltpu.VMEM(parts.shape, bases.dtype),
+            pltpu.SemaphoreType.DMA((2, 2 * slots)),
+        ],
+        compiler_params=pltpu.CompilerParams(vmem_limit_bytes=8 * 2**20),
+        cost_estimate=pl.CostEstimate(flops=0, bytes_accessed=8 * 10**6, transcendentals=0),
         name="interleave",
-    )(parts)
+    )(pltpu.with_memory_space_constraint(parts, pltpu.HBM))
 
 
 def place_quads(row, col, quads, block_ref):
@@ -74,25 +88,43 @@
             block_ref[pl.ds(at[0], half), pl.ds(at[1], half)] = quads[2 * dr + dc][...]
 
 
-def gram_kernel(place_ref, own_ref, side_ref, below_ref, cross_ref, out_ref, block_ref):
+def grid_positions():
+    shape = (GB, GB)
+    return lax.broadcasted_iota(jnp.int32, shape, 0), lax.broadcasted_iota(jnp.int32, shape, 1)
+
+
+def gram_kernel(
+    place_ref, own_ref, side_ref, below_ref, cross_ref, out_ref, diagonal_ref, block_ref
+):
     row = place_ref[0]
     col = place_ref[1]
     place_quads(row, col, (own_ref, side_ref, below_ref, cross_ref), block_ref)
 
     def emit(left_gram, which):
-        for n, (first, second) in enumerate(PAIRS[which]):
+        def product(first, second):
             a = slice(first * GB, (first + 1) * GB)
             b = slice(second * GB, (second + 1) * GB)
             if left_gram:
-                value = dot_nt(block_ref[a, :], block_ref[b, :])
+                return dot_nt(block_ref[a, :], block_ref[b, :])
+            return dot_tn(block_ref[:, a], block_ref[:, b])
+
+        r, c = grid_positions()
+        upper = product(2 * which, 2 * which)
+        lower = product(2 * which + 1, 2 * which + 1)
+        diagonal = jnp.sum(jnp.where(r == c, lower, 0.0), axis=0, keepdims=True)
+        tile_row = lax.broadcasted_iota(jnp.int32, (SUB, 128), 0)
+        diagonal_ref[...] = jnp.where(
+            tile_row == 0, diagonal[:, :128], jnp.where(tile_row == 1, diagonal[:, 128:], 0.0)
+        ).astype(jnp.bfloat16)
+        for n in range(4):
+            if n < 3:
+                value = product(*ABOVE[which][n])
             else:
-                value = dot_tn(block_ref[:, a], block_ref[:, b])
+                value = jnp.where(r <= c, upper, lower)
             for half in range(2):
-                tiles = value[:, half * 128 : (half + 1) * 128].reshape(GB // 8, 8, 128)
-                tiles = tiles.astype(jnp.bfloat16)
-                for r in (n // 2,) if n < 4 else (0, 1):
-                    t = n % 2 if n < 4 else 2
-                    out_ref[:, 2 * half + r, :, t * 128 : (t + 1) * 128] = tiles
+                tiles = value[:, half * 128 : (half + 1) * 128].reshape(GB // SUB, SUB, 128)
+                span = slice(n % 2 * 128, (n % 2 + 1) * 128)
+                out_ref[:, 2 * half + n // 2, :, span] = tiles.astype(jnp.bfloat16)
 
     for left_gram in (True, False):
         for which in range(2):
@@ -106,71 +138,141 @@
     return pl.pallas_call(
         gram_kernel,
         in_specs=[whole(pltpu.SMEM)] + [whole()] * 4,
-        out_specs=whole(),
-        out_shape=jax.ShapeDtypeStruct((32, 4, 8, 384), jnp.bfloat16),
+        out_specs=[whole()] * 2,
+        out_shape=[
+            jax.ShapeDtypeStruct((32, 4, SUB, WIDTH), jnp.bfloat16),
+            jax.ShapeDtypeStruct((SUB, 128), jnp.bfloat16),
+        ],
         scratch_shapes=[pltpu.VMEM((size, size), jnp.bfloat16)],
         compiler_params=PARAMS,
-        cost_estimate=pl.CostEstimate(flops=7 * 10**8, bytes_accessed=3 * 10**6, transcendentals=0),
+        cost_estimate=pl.CostEstimate(
+            flops=36 * 10**9, bytes_accessed=3 * 10**6, transcendentals=0
+        ),
         name="gram_pieces",
     )(place, *quads)
 
 
-def second_kernel(codes_ref, rows_ref, gram_ref, out_ref):
-    out_ref[:, :, 768:] = gram_ref[...]
-
-    @pl.loop(0, 32)
-    def _(block):
-        left = rows_ref[codes_ref[2 * block]]
-        right = rows_ref[codes_ref[2 * block + 1]]
-        base = (block // 4) * 16 + (block % 4) * 2
-        for i in range(2):
-            at = base + 8 * i
-            out_ref[at, :, 0:512] = left[:, 512 * i : 512 * (i + 1)]
-            out_ref[at, :, 512:768] = right[:, 0:256]
-            out_ref[at + 1, :, 0:768] = right[:, 256:1024]
+GROUPS = 4
+
+
+def second_kernel(codes_ref, rows_ref, gram_ref, out_ref, live_ref, arranged_ref, sems):
+    items = live_ref.shape[0] // GROUPS
+    dests = arranged_ref.shape[0] // GROUPS
+    pieces = pltpu.make_async_copy(gram_ref, arranged_ref.at[:, :, 768:1024], sems.at[2 * GROUPS])
+    for group in range(GROUPS):
+
+        @pl.loop(items * group, items * (group + 1))
+        def _(item, group=group):
+            pltpu.make_async_copy(
+                rows_ref.at[codes_ref[item]], live_ref.at[item], sems.at[group]
+            ).start()
+
+    pieces.start()
+    stores = []
+    for group in range(GROUPS):
+        pltpu.make_async_copy(
+            rows_ref.at[0:items], live_ref.at[items * group : items * (group + 1)], sems.at[group]
+        ).wait()
+
+        @pl.loop(items // 2 * group, items // 2 * (group + 1))
+        def _(block):
+            left = live_ref[2 * block]
+            right = live_ref[2 * block + 1]
+            base = (block // 4) * 16 + (block % 4) * 2
+            for i in range(2):
+                at = base + 8 * i
+                arranged_ref[at, :, 0:512] = left[:, 512 * i : 512 * (i + 1)]
+                arranged_ref[at, :, 512:768] = right[:, 0:256]
+                arranged_ref[at + 1, :, 0:768] = right[:, 256:1024]
+
+        if group == 0:
+            pieces.wait()
+        span = slice(dests * group, dests * (group + 1))
+        store = pltpu.make_async_copy(
+            arranged_ref.at[span], out_ref.at[span], sems.at[GROUPS + group]
+        )
+        store.start()
+        stores.append(store)
+    for store in stores:
+        store.wait()
 
 
 def second_operand(codes, rows, gram):
     return pl.pallas_call(
         second_kernel,
-        in_specs=[whole(pltpu.SMEM), whole(), whole()],
-        out_specs=whole(),
-        out_shape=jax.ShapeDtypeStruct((128, SUB, 1152), jnp.bfloat16),
-        compiler_params=PARAMS,
+        in_specs=[whole(pltpu.SMEM), whole(pl.ANY), whole(pl.ANY)],
+        out_specs=whole(pl.ANY),
+        out_shape=jax.ShapeDtypeStruct((128, SUB, 1024), jnp.bfloat16),
+        scratch_shapes=[
+            pltpu.VMEM((64, SUB, 1024), jnp.bfloat16),
+            pltpu.VMEM((128, SUB, 1024), jnp.bfloat16),
+            pltpu.SemaphoreType.DMA((2 * GROUPS + 1,)),
+        ],
+        compiler_params=pltpu.CompilerParams(vmem_limit_bytes=8 * 2**20),
         cost_estimate=pl.CostEstimate(flops=0, bytes_accessed=8 * 10**6, transcendentals=0),
         name="second_operand",
     )(codes, rows, gram)
 
 
-def third_kernel(codes_ref, place_ref, got_ref, out_ref):
-    core = place_ref[1]
-
-    @pl.loop(0, 64)
-    def _(item):
-        block = item // 2
-        at = codes_ref[item]
-        upper = (block // 4) * 16 + (block % 4) * 2 + item % 2
-        lower = upper + 8
-        out_ref[at, :, 0:256] = got_ref[upper, :, 0:256]
-        out_ref[at, :, 256:512] = got_ref[lower, :, 0:256]
-        out_ref[at, :, 512:640] = got_ref[upper + 8 * core, :, 256:384]
-
-
-def third_operand(codes, place, got):
+def third_kernel(
+    codes_ref, mine_ref, got_ref, diagonal_ref, out_ref, held_ref, packed_ref, sems
+):
+    items = packed_ref.shape[0] // GROUPS
+    sources = held_ref.shape[0] // GROUPS
+    loads = []
+    for group in range(GROUPS):
+        span = slice(sources * group, sources * (group + 1))
+        load = pltpu.make_async_copy(
+            got_ref.at[span, :, 768:1024], held_ref.at[span], sems.at[group]
+        )
+        load.start()
+        loads.append(load)
+    apart = pltpu.make_async_copy(
+        diagonal_ref,
+        out_ref.at[codes_ref[mine_ref[0]] // 2, :, 4 * WIDTH : 4 * WIDTH + 128],
+        sems.at[2 * GROUPS],
+    )
+    apart.start()
+    for group in range(GROUPS):
+        loads[group].wait()
+
+        @pl.loop(items * group, items * (group + 1))
+        def _(item, group=group):
+            block = item // 2
+            upper = (block // 4) * 16 + (block % 4) * 2 + item % 2
+            packed_ref[item, :, 0:WIDTH] = held_ref[upper]
+            packed_ref[item, :, WIDTH:] = held_ref[upper + 8]
+            code = codes_ref[item]
+            lane = pl.multiple_of(code % 2 * (2 * WIDTH), 2 * WIDTH)
+            pltpu.make_async_copy(
+                packed_ref.at[item],
+                out_ref.at[code // 2, :, pl.ds(lane, 2 * WIDTH)],
+                sems.at[GROUPS + group],
+            ).start()
+
+    for group in range(GROUPS):
+        span = slice(items * group, items * (group + 1))
+        pltpu.make_async_copy(
+            packed_ref.at[span], out_ref.at[span, :, 0 : 2 * WIDTH], sems.at[GROUPS + group]
+        ).wait()
+    apart.wait()
+
+
+def third_operand(codes, my_item, got, diagonal):
     return pl.pallas_call(
         third_kernel,
-        grid=(1,),
-        in_specs=[
-            whole(pltpu.SMEM),
-            whole(pltpu.SMEM),
-            pl.BlockSpec((128, SUB, 384), lambda _: (0, 0, 2)),
-        ],
-        out_specs=pl.BlockSpec((256, SUB, 640), lambda _: (0, 0, 0)),
-        out_shape=jax.ShapeDtypeStruct((256, SUB, 640), jnp.bfloat16),
-        compiler_params=PARAMS,
+        in_specs=[whole(pltpu.SMEM), whole(pltpu.SMEM), whole(pl.ANY), whole(pl.ANY)],
+        out_specs=whole(pl.ANY),
+        out_shape=pltpu.HBM((128, SUB, 4 * WIDTH + 128), jnp.bfloat16),
+        scratch_shapes=[
+            pltpu.VMEM((128, SUB, WIDTH), jnp.bfloat16),
+            pltpu.VMEM((64, SUB, 2 * WIDTH), jnp.bfloat16),
+            pltpu.SemaphoreType.DMA((2 * GROUPS + 1,)),
+        ],
+        compiler_params=pltpu.CompilerParams(vmem_limit_bytes=8 * 2**20),
         cost_estimate=pl.CostEstimate(flops=0, bytes_accessed=4 * 10**6, transcendentals=0),
         name="third_operand",
-    )(codes, place, got)
+    )(codes, my_item, got, diagonal)
 
 
 def rotate_kernel(
@@ -305,60 +407,93 @@
     )(place, own, side, mine, theirs)
 
 
-def factor_kernel(live_ref, factor_ref, got_ref, out_ref):
-    slot = pl.program_id(0)
-    strip = pl.program_id(1)
-    live = live_ref[slot] != 0
-
-    def piece(first, second):
-        which, n = next(
-            (w, n) for w in range(2) for n in range(5) if PAIRS[w][n] == (first, second)
-        )
-        r = n // 2 if n < 4 else which
-        lane = 2 * which + n % 2 if n < 4 else 4
+def factor_kernel(
+    items_ref, live_ref, factor_ref, got_ref, out_ref, strips_ref, held_ref, sems
+):
+    slots = factor_ref.shape[0]
+    count = 4 * slots
+
+    def at(n):
+        return (n // 4, slice(GB * (n % 4), GB * (n % 4 + 1)))
+
+    pieces = pltpu.make_async_copy(got_ref, held_ref, sems.at[2 * count])
+    loads = [
+        pltpu.make_async_copy(factor_ref.at[at(n)], strips_ref.at[n], sems.at[n])
+        for n in range(count)
+    ]
+    stores = [
+        pltpu.make_async_copy(strips_ref.at[n], out_ref.at[at(n)], sems.at[count + n])
+        for n in range(count)
+    ]
+    loads[0].start()
+    pieces.start()
+    for n in range(1, count):
+        loads[n].start()
+
+    def piece(slot, which, n):
+        lane = 2 * WIDTH * slot + (2 * which + n % 2) * 128
         halves = [
-            got_ref[:, 2 * h + r, slot, :, lane * 128 : (lane + 1) * 128]
+            held_ref[:, 2 * h + n // 2, :, lane : lane + 128]
             .astype(jnp.float32)
             .reshape(GB, 128)
             for h in range(2)
         ]
         return jnp.concatenate(halves, axis=1)
 
-    def mix(row):
+    def sub_block(slot, row, col):
+        if row != col:
+            pair = (min(row, col), max(row, col))
+            which = 0 if pair in ABOVE[0] else 1
+            value = piece(slot, which, ABOVE[which].index(pair))
+            return value if row < col else value.T
+        value = piece(slot, row // 2, 3)
+        r, c = grid_positions()
+        if row % 2 == 0:
+            return jnp.where(r <= c, value, value.T)
+        item = items_ref[slot]
+        block = item // 2
+        source = (block // 4 * 2 + row // 2) * 8 + block % 4 * 2 + item % 2
+        tile = held_ref[source // 4, source % 4, :, 4 * WIDTH :].astype(jnp.float32)
+        diagonal = jnp.concatenate([tile[0:1], tile[1:2]], axis=1)
+        return jnp.where(r > c, value, jnp.where(r < c, value.T, diagonal))
+
+    def mix(n):
+        slot, row = n // 4, n % 4
         for col in range(4):
-            value = piece(row, col) if row <= col else piece(col, row).T
-            at = slice(col * GB, (col + 1) * GB)
-            out_ref[0, :, at] = (
-                shampoo_beta * factor_ref[0, :, at] + (1.0 - shampoo_beta) * value
-            )
-
-    for row in range(4):
-        pl.when(live & (strip == row))(functools.partial(mix, row))
-
-    @pl.when(jnp.logical_not(live))
-    def _():
-        out_ref[...] = factor_ref[...]
-
-
-def update_factors(live, factors, got):
+            span = slice(col * GB, (col + 1) * GB)
+            strips_ref[n, :, span] = shampoo_beta * strips_ref[n, :, span] + (
+                1.0 - shampoo_beta
+            ) * sub_block(slot, row, col)
+
+    for n in range(count):
+        loads[n].wait()
+        if n == 0:
+            pieces.wait()
+        pl.when(live_ref[n // 4] != 0)(functools.partial(mix, n))
+        stores[n].start()
+    for n in range(count):
+        stores[n].wait()
+
+
+def update_factors(items, live, factors, got):
     slots, size, _ = factors.shape
-    got = got.reshape(32, 4, slots, SUB, 640)
+    got = got.reshape(32, 4, SUB, got.shape[2])
     return pl.pallas_call(
         factor_kernel,
-        grid=(slots, 4),
-        in_specs=[
-            whole(pltpu.SMEM),
-            pl.BlockSpec((1, GB, size), lambda s, p: (s, p, 0)),
-            whole(),
-        ],
-        out_specs=pl.BlockSpec((1, GB, size), lambda s, p: (s, p, 0)),
+        in_specs=[whole(pltpu.SMEM)] * 2 + [whole(pl.ANY)] * 2,
+        out_specs=whole(pl.ANY),
         out_shape=jax.ShapeDtypeStruct(factors.shape, factors.dtype),
-        compiler_params=PARAMS,
+        scratch_shapes=[
+            pltpu.VMEM((4 * slots, GB, size), jnp.float32),
+            pltpu.VMEM(got.shape, got.dtype),
+            pltpu.SemaphoreType.DMA((8 * slots + 1,)),
+        ],
+        compiler_params=pltpu.CompilerParams(vmem_limit_bytes=20 * 2**20),
         cost_estimate=pl.CostEstimate(
             flops=4 * 10**6, bytes_accessed=2 * 10**7, transcendentals=0
         ),
         name="update_factors",
-    )(live, factors, got)
+    )(items, live, pltpu.with_memory_space_constraint(factors, pltpu.HBM), got)
 
 
 def shards(gradient, first_moment, second_moment, factors, eigen_bases, owners):
@@ -369,8 +504,10 @@
     fsdp_index = lax.axis_index("fsdp")
     rep_index = lax.axis_index("rep")
     my_index = fsdp_index * lax.axis_size("rep") + rep_index
+    my_item = (fsdp_index // 2 * 8 + rep_index).reshape(1).astype(jnp.int32)
     place = jnp.stack([fsdp_index % 2, rep_index % 2]).astype(jnp.int32)
 
+    below = swap_neighbour(gradient, "fsdp")
     first_parts = interleave(eigen_bases, devices)
     first_got = lax.all_to_all(first_parts, BOTH, 0, 0, tiled=True)
 
@@ -380,19 +517,21 @@
     )
     codes = slots * owners + jnp.sum(earlier_same.astype(jnp.int32), axis=1)
     my_codes = my_index * slots + jnp.arange(slots, dtype=jnp.int32)
-    live = jnp.sum((codes[None, :] == my_codes[:, None]).astype(jnp.int32), axis=1)
+    hits = (codes[None, :] == my_codes[:, None]).astype(jnp.int32)
+    live = jnp.sum(hits, axis=1)
+    items = jnp.sum(hits * item_index[None, :], axis=1)
 
     side = swap_neighbour(gradient, "rep")
-    below = swap_neighbour(gradient, "fsdp")
     cross = swap_neighbour(below, "rep")
     quads = (gradient, side, below, cross)
-    gram = gram_pieces(place, quads).reshape(devices, SUB, 384)
+    gram, diagonal = gram_pieces(place, quads)
+    gram = gram.reshape(devices, SUB, WIDTH)
 
     second_parts = second_operand(codes, first_got.reshape(devices * slots, SUB, size), gram)
     mine = lax.all_to_all(second_parts, BOTH, 0, 0, tiled=True)
-    theirs = swap_neighbour(mine[:, :, :768], "rep")
-
-    third_parts = third_operand(codes, place, mine).reshape(devices, slots, SUB, 640)
+    theirs = swap_neighbour(mine, "rep")
+
+    third_parts = third_operand(codes, my_item, mine, diagonal)
     third_got = lax.all_to_all(third_parts, BOTH, 0, 0, tiled=True)
 
     new_first, new_second, direction = rotate(
@@ -401,7 +540,7 @@
     other = swap_neighbour(direction, "rep")
     keep, give = back(place, direction, other, mine, theirs)
     update = keep + swap_neighbour(give, "fsdp").astype(jnp.float32)
-    new_factors = update_factors(live, factors, third_got)
+    new_factors = update_factors(items, live, factors, third_got)
     return (update, new_first, new_second, new_factors)
 
 

time: 190 us -> 157 us (0.83)
  Pallas kernels: 40 us -> 27.1 us
  waiting for transfers between devices: 76.2 us -> 65.7 us
  blocking collectives: 42.3 us -> 34.4 us
    ppermute x6, waiting for transfers between devices: 57 us -> 3.45 us  [swap_neighbour(): return lax.ppermute(value, axis, pairs)]
    all_to_all x1, waiting for transfers between devices: 0.01 us -> 47.5 us  [shards(): first_got = lax.all_to_all(first_parts, BOTH, 0, 0, tiled=True)]
    pallas_call x4, Pallas kernels: 24.7 us -> 16.1 us  [the longest x1 7.91 us: update_factors(): pl.pallas_call(factor_kernel, in_specs=[whole(pltpu.SMEM)] * 2 + [whole(p...]
    all_to_all x1, blocking collectives: 42.3 us -> 34.4 us  [shards(): mine = lax.all_to_all(second_parts, BOTH, 0, 0, tiled=True)]
    all_to_all x1, waiting for transfers between devices: 19.2 us -> 14.8 us  [shards(): third_got = lax.all_to_all(third_parts, BOTH, 0, 0, tiled=True)]
    unnamed x20 -> x22, local copies, waits for them, and re-layouts: 3.73 us -> 5.41 us
  transfers between devices with their start and end apart: 8 -> 8, of which waited for: 4 -> 5; matrix products, arithmetic and copies ran while one was open for 1% -> 0% of each run, Pallas kernels for 15% -> 16%
where the time goes in v1:
time: 157 us
  waiting for transfers between devices  65.7 us (42%)
  blocking collectives  34.4 us (22%)
  Pallas kernels  27.1 us (17%)
  starting transfers between devices  21.9 us (14%)
  local copies, waits for them, and re-layouts  5.41 us (3%)
  other arithmetic  1.57 us (1%)
    all_to_all x1, waiting for transfers between devices, shards(): first_got = lax.all_to_all(first_parts, BOTH, 0, 0, tiled=True)  47.5 us
    all_to_all x1, blocking collectives, shards(): mine = lax.all_to_all(second_parts, BOTH, 0, 0, tiled=True)  34.4 us
    all_to_all x1, waiting for transfers between devices, shards(): third_got = lax.all_to_all(third_parts, BOTH, 0, 0, tiled=True)  14.8 us
    all_to_all x1, starting transfers between devices, shards(): first_got = lax.all_to_all(first_parts, BOTH, 0, 0, tiled=True)  11.1 us
    pallas_call x1, Pallas kernels, update_factors(): pl.pallas_call(factor_kernel, in_specs=[whole(pltpu.SMEM)] * 2 + [whole(p...  7.91 us
    ppermute x6, starting transfers between devices, swap_neighbour(): return lax.ppermute(value, axis, pairs)  6.08 us
    unnamed x22, local copies, waits for them, and re-layouts  5.41 us
    pallas_call x1, Pallas kernels, rotate(): pl.pallas_call(rotate_kernel, grid=(1,), in_specs=[whole(pltpu.SMEM)] + [...  5.41 us
  transfers between devices with their start and end apart: 8, of which 5 were waited for; matrix products, arithmetic and copies ran while one was open for 0% of the time, Pallas kernels for 16%

profile of v1, /device:TPU:1, one launch (start us, length us, event | category | flops | bytes accessed | tf_op | source)
XLA Modules:
  0.0 156.8 jit_solution(14948699973982159700)
XLA Ops:
  0.6 2.2 %collective-permute-start.1 = (bf16[512,512]{1,0:T(8,128)(2,1)}, bf16[512,512]{1,0:T(8,128)(2,1)S(1)}, u32[]{:S(2)}, u32[]{:S(2)}) collective-permute-start(bf16[512,512]{1,0:T(8,128)(2,1)} %own_ref.3), channel_id=1, source_target_pairs={{0,8},{8,0},{16,24},{24,16},{32,40},{40,32},{48,56},{56,48},{64,72... | collective-permute-start | bytes 1572872 | tf_op jit(solution)/shard_map/ppermute | solution.py:25
  2.8 3.3 %interleave.1 = bf16[128,2,8,1024]{3,2,1,0:T(8,128)(2,1)} custom-call(bf16[2,128,8,1024]{3,2,1,0:T(8,128)(2,1)} %bitcast.8), custom_call_target="tpu_custom_call" | custom-call | bytes 8000000 | tf_op jit(solution)/shard_map/interleave/pallas_call | solution.py:68
  6.2 11.1 %all-to-all-start = ((bf16[128,2,8,1024]{3,2,1,0:T(8,128)(2,1)}), bf16[128,2,8,1024]{3,2,1,0:T(8,128)(2,1)}, u32[]{:S(2)}, u32[]{:S(2)}) async-start(bf16[128,2,8,1024]{3,2,1,0:T(8,128)(2,1)} %interleave.1), calls=%async_computation | async-start | bytes 8388608 | tf_op jit(solution)/shard_map/all_to_all | solution.py:512
  17.3 1.2 collective-permute-start
  18.9 1.2 collective-permute-done.side_ref
  20.8 1.6 %gram_pieces.1 = (bf16[32,4,8,256]{3,2,1,0:T(8,128)(2,1)S(1)}, bf16[8,128]{1,0:T(8,128)(2,1)S(1)}) custom-call(s32[2]{0:T(128)S(1)} %pad_add_fusion.place_ref, bf16[512,512]{1,0:T(8,128)(2,1)S(1)} %copy-done.2, bf16[512,512]{1,0:T(8,128)(2,1)S(1)} %collective-permute-done.side_ref, bf16[512,512]{1,0:T(8,128)(2,1)S(1)} %collective-permute-done.1.below_ref, ...), custom_call_target="tpu_custom_call" | custom-call | flops 35999997952 | bytes 3000000 | tf_op jit(solution)/shard_map/gram_pieces/pallas_call | solution.py:138
  22.5 47.5 %all-to-all-done = bf16[128,2,8,1024]{3,2,1,0:T(8,128)(2,1)} async-done(((bf16[128,2,8,1024]{3,2,1,0:T(8,128)(2,1)}), bf16[128,2,8,1024]{3,2,1,0:T(8,128)(2,1)}, u32[]{:S(2)}, u32[]{:S(2)}) %all-to-all-start) | async-done | bytes 4194336 | tf_op jit(solution)/shard_map/all_to_all | solution.py:512
  69.9 2.1 %second_operand.1 = bf16[128,8,1024]{2,1,0:T(8,128)(2,1)S(1)} custom-call(s32[64]{0:T(128)S(1)} %multiply_add_fusion.codes_ref, bf16[256,8,1024]{2,1,0:T(8,128)(2,1)} %bitcast.3.rows_ref, bf16[128,8,256]{2,1,0:T(8,128)(2,1)S(1)} %bitcast.7), custom_call_target="tpu_custom_call" | custom-call | bytes 8000000 | tf_op jit(solution)/shard_map/second_operand/pallas_call | solution.py:201
  72.0 34.4 %all_to_all.15.mine_ref.got_ref = bf16[128,8,1024]{2,1,0:T(8,128)(2,1)S(1)} all-to-all(bf16[128,8,1024]{2,1,0:T(8,128)(2,1)S(1)} %second_operand.1), channel_id=1, replica_groups=mesh['fsdp'=16,'rep'=8] {'fsdp','rep'}, dimensions={0} | all-to-all | bytes 4194304 | tf_op jit(solution)/shard_map/all_to_all | solution.py:531
  106.4 0.9 collective-permute-start.3
  107.4 2.8 %third_operand.1 = bf16[128,8,1152]{2,1,0:T(8,128)(2,1)} custom-call(s32[64]{0:T(128)S(1)} %multiply_add_fusion.codes_ref, s32[1]{0:T(128)} %bitcast.5.mine_ref, bf16[128,8,1024]{2,1,0:T(8,128)(2,1)S(1)} %all_to_all.15.mine_ref.got_ref, bf16[8,128]{1,0:T(8,128)(2,1)S(1)} %get-tuple-element.17.diagonal_ref), custom_call_target="tpu_custom_call" | custom-call | bytes 4000000 | tf_op jit(solution)/shard_map/third_operand/pallas_call | solution.py:262
  110.2 4.7 %all-to-all-start.2 = ((bf16[128,8,1152]{2,1,0:T(8,128)(2,1)}), bf16[128,8,1152]{2,1,0:T(8,128)(2,1)}, u32[]{:S(2)}, u32[]{:S(2)}) async-start(bf16[128,8,1152]{2,1,0:T(8,128)(2,1)} %third_operand.1), calls=%async_computation.2 | async-start | bytes 4718592 | tf_op jit(solution)/shard_map/all_to_all | solution.py:535
  114.9 1.2 copy-done.1
  116.1 1.0 copy-done.3
  117.2 1.0 copy-done.5
  118.2 1.0 copy-done.7
  119.2 1.0 copy-done.9
  120.3 5.4 %rotate.1 = (f32[512,512]{1,0:T(8,128)}, f32[512,512]{1,0:T(8,128)}, bf16[512,512]{1,0:T(8,128)(2,1)S(1)}) custom-call(s32[2]{0:T(128)S(1)} %pad_add_fusion.place_ref, bf16[512,512]{1,0:T(8,128)(2,1)S(1)} %copy-done.3, bf16[512,512]{1,0:T(8,128)(2,1)S(1)} %copy-done.7, bf16[512,512]{1,0:T(8,128)(2,1)S(1)} %copy-done.5, bf16[512,512]{1,0:T(8,128)(2,1)S(1)} %copy-done.9, ...), custom_call_target="tpu_custom_call" | custom-call | flops 1600000000 | bytes 10000000 | tf_op jit(solution)/shard_map/rotate/pallas_call | solution.py:322
  125.7 1.1 collective-permute-start.4
  126.8 1.5 collective-permute-done.4.side_ref
  128.3 3.9 %back.1 = (f32[512,512]{1,0:T(8,128)S(1)}, bf16[512,512]{1,0:T(8,128)(2,1)}) custom-call(s32[2]{0:T(128)S(1)} %pad_add_fusion.place_ref, bf16[512,512]{1,0:T(8,128)(2,1)S(1)} %get-tuple-element.12.own_ref, bf16[512,512]{1,0:T(8,128)(2,1)S(1)} %collective-permute-done.4.side_ref, bf16[128,8,1024]{2,1,0:T(8,128)(2,1)S(1)} %all_to_all.15.mine_ref.got_ref, ...), custom_call_target="tpu_custom_call" | custom-call | flops 1100000000 | bytes 6000000 | tf_op jit(solution)/shard_map/back/pallas_call | solution.py:388
  132.9 14.8 %all-to-all-done.2 = bf16[128,8,1152]{2,1,0:T(8,128)(2,1)} async-done(((bf16[128,8,1152]{2,1,0:T(8,128)(2,1)}), bf16[128,8,1152]{2,1,0:T(8,128)(2,1)}, u32[]{:S(2)}, u32[]{:S(2)}) %all-to-all-start.2) | async-done | bytes 2359328 | tf_op jit(solution)/shard_map/all_to_all | solution.py:535
  147.8 7.9 %update_factors.1 = f32[2,1024,1024]{2,1,0:T(8,128)} custom-call(s32[2]{0:T(128)S(1)} %get-tuple-element.19.items_ref, s32[2]{0:T(128)S(1)} %get-tuple-element.18.live_ref, f32[2,1024,1024]{2,1,0:T(8,128)} %factor_ref.1, bf16[32,4,8,1152]{3,2,1,0:T(8,128)(2,1)} %bitcast.6.got_ref), custom_call_target="tpu_custom_call" | custom-call | flops 4000000 | bytes 20000000 | tf_op jit(solution)/shard_map/update_factors/pallas_call | solution.py:481
  155.7 1.1 convert_add_fusion
  (28 shorter events, 1.9 us)
Async XLA Ops:
  0.6 17.9 %collective-permute-start.1 = (bf16[512,512]{1,0:T(8,128)(2,1)}, bf16[512,512]{1,0:T(8,128)(2,1)S(1)}, u32[]{:S(2)}, u32[]{:S(2)}) collective-permute-start(bf16[512,512]{1,0:T(8,128)(2,1)} %own_ref.3), channel_id=1, source_target_pairs={{0,8},{8,0},{16,24},{24,16},{32,40},{40,32},{48,56},{56,48},{64,72... | collective-permute-start | bytes 1572872 | tf_op jit(solution)/shard_map/ppermute | solution.py:25
  6.1 11.2 %copy-start.2 = (bf16[512,512]{1,0:T(8,128)(2,1)S(1)}, bf16[512,512]{1,0:T(8,128)(2,1)}, u32[]{:S(2)}) copy-start(bf16[512,512]{1,0:T(8,128)(2,1)} %own_ref.3) | copy-start | bytes 1572868
  6.2 12.6 %copy-start.10 = (s32[64]{0:T(128)S(1)}, s32[64]{0:T(128)}, u32[]{:S(2)}) copy-start(s32[64]{0:T(128)} %param.11) | copy-start | bytes 772
  6.2 63.8 %all-to-all-start = ((bf16[128,2,8,1024]{3,2,1,0:T(8,128)(2,1)}), bf16[128,2,8,1024]{3,2,1,0:T(8,128)(2,1)}, u32[]{:S(2)}, u32[]{:S(2)}) async-start(bf16[128,2,8,1024]{3,2,1,0:T(8,128)(2,1)} %interleave.1), calls=%async_computation | async-start | bytes 8388608 | tf_op jit(solution)/shard_map/all_to_all | solution.py:512
  17.3 2.8 %collective-permute-start = (bf16[512,512]{1,0:T(8,128)(2,1)S(1)}, bf16[512,512]{1,0:T(8,128)(2,1)S(1)}, u32[]{:S(2)}, u32[]{:S(2)}) collective-permute-start(bf16[512,512]{1,0:T(8,128)(2,1)S(1)} %copy-done.2), channel_id=1, source_target_pairs={{0,1},{1,0},{2,3},{3,2},{4,5},{5,4},{6,7},{7,6},{8,9},{9,8},{10,11... | collective-permute-start | bytes 1572872 | tf_op jit(solution)/shard_map/ppermute | solution.py:25
  18.5 3.9 %copy-start.4 = (bf16[512,512]{1,0:T(8,128)(2,1)}, bf16[512,512]{1,0:T(8,128)(2,1)S(1)}, u32[]{:S(2)}) copy-start(bf16[512,512]{1,0:T(8,128)(2,1)S(1)} %collective-permute-done.1.below_ref) | copy-start | bytes 1572868
  18.5 2.3 %collective-permute-start.2 = (bf16[512,512]{1,0:T(8,128)(2,1)S(1)}, bf16[512,512]{1,0:T(8,128)(2,1)S(1)}, u32[]{:S(2)}, u32[]{:S(2)}) collective-permute-start(bf16[512,512]{1,0:T(8,128)(2,1)S(1)} %collective-permute-done.1.below_ref), channel_id=1, source_target_pairs={{0,1},{1,0},{2,3},{3,2},{4,5},{5,4},{6,7},{7,6},{8,9},{9,8},{10,11... | collective-permute-start | bytes 1572872 | tf_op jit(solution)/shard_map/ppermute | solution.py:25
  20.1 2.4 %copy-start.6 = (bf16[512,512]{1,0:T(8,128)(2,1)}, bf16[512,512]{1,0:T(8,128)(2,1)S(1)}, u32[]{:S(2)}) copy-start(bf16[512,512]{1,0:T(8,128)(2,1)S(1)} %collective-permute-done.side_ref) | copy-start | bytes 1572868
  20.8 1.7 %copy-start.8 = (bf16[512,512]{1,0:T(8,128)(2,1)}, bf16[512,512]{1,0:T(8,128)(2,1)S(1)}, u32[]{:S(2)}) copy-start(bf16[512,512]{1,0:T(8,128)(2,1)S(1)} %collective-permute-done.2.cross_ref) | copy-start | bytes 1572868
  106.4 8.4 %collective-permute-start.3 = (bf16[128,8,1024]{2,1,0:T(8,128)(2,1)S(1)}, bf16[128,8,1024]{2,1,0:T(8,128)(2,1)}, u32[]{:S(2)}, u32[]{:S(2)}) collective-permute-start(bf16[128,8,1024]{2,1,0:T(8,128)(2,1)S(1)} %all_to_all.15.mine_ref.got_ref), channel_id=1, source_target_pairs={{0,1},{1,0},{2,3},{3,2},{4,5},{5,4},{6,7},{7,6},{8,9},{9,8},{10,11... | collective-permute-start | bytes 6291464 | tf_op jit(solution)/shard_map/ppermute | solution.py:25
  107.4 7.5 %copy-start = (f32[512,512]{1,0:T(8,128)S(1)}, f32[512,512]{1,0:T(8,128)}, u32[]{:S(2)}) copy-start(f32[512,512]{1,0:T(8,128)} %first_ref.1) | copy-start | bytes 3145732
  110.2 37.6 %all-to-all-start.2 = ((bf16[128,8,1152]{2,1,0:T(8,128)(2,1)}), bf16[128,8,1152]{2,1,0:T(8,128)(2,1)}, u32[]{:S(2)}, u32[]{:S(2)}) async-start(bf16[128,8,1152]{2,1,0:T(8,128)(2,1)} %third_operand.1), calls=%async_computation.2 | async-start | bytes 4718592 | tf_op jit(solution)/shard_map/all_to_all | solution.py:535
  114.9 1.2 copy-start.1
  116.1 1.0 copy-start.3
  117.2 1.0 copy-start.5
  118.2 1.0 copy-start.7
  119.2 1.0 copy-start.9
  125.7 2.6 %collective-permute-start.4 = (bf16[512,512]{1,0:T(8,128)(2,1)S(1)}, bf16[512,512]{1,0:T(8,128)(2,1)S(1)}, u32[]{:S(2)}, u32[]{:S(2)}) collective-permute-start(bf16[512,512]{1,0:T(8,128)(2,1)S(1)} %get-tuple-element.12.own_ref), channel_id=1, source_target_pairs={{0,1},{1,0},{2,3},{3,2},{4,5},{5,4},{6,7},{7,6},{8,9},{9,8},{10,11... | collective-permute-start | bytes 1572872 | tf_op jit(solution)/shard_map/ppermute | solution.py:25
  132.2 23.5 %collective-permute-start.5 = (bf16[512,512]{1,0:T(8,128)(2,1)}, bf16[512,512]{1,0:T(8,128)(2,1)S(1)}, u32[]{:S(2)}, u32[]{:S(2)}) collective-permute-start(bf16[512,512]{1,0:T(8,128)(2,1)} %get-tuple-element.14), channel_id=1, source_target_pairs={{0,8},{8,0},{16,24},{24,16},{32,40},{40,32},{48,56},{56,48},{64,72... | collective-permute-start | bytes 1572872 | tf_op jit(solution)/shard_map/ppermute | solution.py:25

commit v2 on v1

--- a/solution.py
+++ b/solution.py
@@ -138,12 +138,12 @@
     return pl.pallas_call(
         gram_kernel,
         in_specs=[whole(pltpu.SMEM)] + [whole()] * 4,
-        out_specs=[whole()] * 2,
+        out_specs=[whole()] * 3,
         out_shape=[
             jax.ShapeDtypeStruct((32, 4, SUB, WIDTH), jnp.bfloat16),
             jax.ShapeDtypeStruct((SUB, 128), jnp.bfloat16),
-        ],
-        scratch_shapes=[pltpu.VMEM((size, size), jnp.bfloat16)],
+            pltpu.HBM((size, size), jnp.bfloat16),
+        ],
         compiler_params=PARAMS,
         cost_estimate=pl.CostEstimate(
             flops=36 * 10**9, bytes_accessed=3 * 10**6, transcendentals=0
@@ -155,10 +155,9 @@
 GROUPS = 4
 
 
-def second_kernel(codes_ref, rows_ref, gram_ref, out_ref, live_ref, arranged_ref, sems):
+def second_kernel(codes_ref, rows_ref, gram_ref, out_ref, live_ref, sems):
     items = live_ref.shape[0] // GROUPS
-    dests = arranged_ref.shape[0] // GROUPS
-    pieces = pltpu.make_async_copy(gram_ref, arranged_ref.at[:, :, 768:1024], sems.at[2 * GROUPS])
+    pieces = pltpu.make_async_copy(gram_ref, out_ref.at[:, :, 768:1024], sems.at[GROUPS])
     for group in range(GROUPS):
 
         @pl.loop(items * group, items * (group + 1))
@@ -168,7 +167,6 @@
             ).start()
 
     pieces.start()
-    stores = []
     for group in range(GROUPS):
         pltpu.make_async_copy(
             rows_ref.at[0:items], live_ref.at[items * group : items * (group + 1)], sems.at[group]
@@ -181,32 +179,22 @@
             base = (block // 4) * 16 + (block % 4) * 2
             for i in range(2):
                 at = base + 8 * i
-                arranged_ref[at, :, 0:512] = left[:, 512 * i : 512 * (i + 1)]
-                arranged_ref[at, :, 512:768] = right[:, 0:256]
-                arranged_ref[at + 1, :, 0:768] = right[:, 256:1024]
-
-        if group == 0:
-            pieces.wait()
-        span = slice(dests * group, dests * (group + 1))
-        store = pltpu.make_async_copy(
-            arranged_ref.at[span], out_ref.at[span], sems.at[GROUPS + group]
-        )
-        store.start()
-        stores.append(store)
-    for store in stores:
-        store.wait()
+                out_ref[at, :, 0:512] = left[:, 512 * i : 512 * (i + 1)]
+                out_ref[at, :, 512:768] = right[:, 0:256]
+                out_ref[at + 1, :, 0:768] = right[:, 256:1024]
+
+    pieces.wait()
 
 
 def second_operand(codes, rows, gram):
     return pl.pallas_call(
         second_kernel,
         in_specs=[whole(pltpu.SMEM), whole(pl.ANY), whole(pl.ANY)],
-        out_specs=whole(pl.ANY),
-        out_shape=jax.ShapeDtypeStruct((128, SUB, 1024), jnp.bfloat16),
+        out_specs=whole(),
+        out_shape=pltpu.VMEM((128, SUB, 1024), jnp.bfloat16),
         scratch_shapes=[
             pltpu.VMEM((64, SUB, 1024), jnp.bfloat16),
-            pltpu.VMEM((128, SUB, 1024), jnp.bfloat16),
-            pltpu.SemaphoreType.DMA((2 * GROUPS + 1,)),
+            pltpu.SemaphoreType.DMA((GROUPS + 1,)),
         ],
         compiler_params=pltpu.CompilerParams(vmem_limit_bytes=8 * 2**20),
         cost_estimate=pl.CostEstimate(flops=0, bytes_accessed=8 * 10**6, transcendentals=0),
@@ -214,47 +202,30 @@
     )(codes, rows, gram)
 
 
-def third_kernel(
-    codes_ref, mine_ref, got_ref, diagonal_ref, out_ref, held_ref, packed_ref, sems
-):
-    items = packed_ref.shape[0] // GROUPS
-    sources = held_ref.shape[0] // GROUPS
-    loads = []
-    for group in range(GROUPS):
-        span = slice(sources * group, sources * (group + 1))
-        load = pltpu.make_async_copy(
-            got_ref.at[span, :, 768:1024], held_ref.at[span], sems.at[group]
-        )
-        load.start()
-        loads.append(load)
+def third_kernel(codes_ref, mine_ref, got_ref, diagonal_ref, out_ref, sems):
     apart = pltpu.make_async_copy(
         diagonal_ref,
         out_ref.at[codes_ref[mine_ref[0]] // 2, :, 4 * WIDTH : 4 * WIDTH + 128],
-        sems.at[2 * GROUPS],
+        sems.at[0],
     )
     apart.start()
-    for group in range(GROUPS):
-        loads[group].wait()
-
-        @pl.loop(items * group, items * (group + 1))
-        def _(item, group=group):
-            block = item // 2
-            upper = (block // 4) * 16 + (block % 4) * 2 + item % 2
-            packed_ref[item, :, 0:WIDTH] = held_ref[upper]
-            packed_ref[item, :, WIDTH:] = held_ref[upper + 8]
-            code = codes_ref[item]
-            lane = pl.multiple_of(code % 2 * (2 * WIDTH), 2 * WIDTH)
-            pltpu.make_async_copy(
-                packed_ref.at[item],
-                out_ref.at[code // 2, :, pl.ds(lane, 2 * WIDTH)],
-                sems.at[GROUPS + group],
-            ).start()
-
-    for group in range(GROUPS):
-        span = slice(items * group, items * (group + 1))
-        pltpu.make_async_copy(
-            packed_ref.at[span], out_ref.at[span, :, 0 : 2 * WIDTH], sems.at[GROUPS + group]
-        ).wait()
+
+    @pl.loop(0, 32)
+    def _(block):
+        for side in range(2):
+            code = codes_ref[2 * block + side]
+            for half in range(2):
+                source = (block // 4) * 16 + (block % 4) * 2 + side + 8 * half
+                lane = pl.multiple_of(code % 2 * (2 * WIDTH) + half * WIDTH, WIDTH)
+                pltpu.make_async_copy(
+                    got_ref.at[source, :, 768:1024],
+                    out_ref.at[code // 2, :, pl.ds(lane, WIDTH)],
+                    sems.at[1],
+                ).start()
+
+    pltpu.make_async_copy(
+        got_ref.at[:, :, 768:1024], out_ref.at[:, :, 0:WIDTH], sems.at[1]
+    ).wait()
     apart.wait()
 
 
@@ -264,23 +235,16 @@
         in_specs=[whole(pltpu.SMEM), whole(pltpu.SMEM), whole(pl.ANY), whole(pl.ANY)],
         out_specs=whole(pl.ANY),
         out_shape=pltpu.HBM((128, SUB, 4 * WIDTH + 128), jnp.bfloat16),
-        scratch_shapes=[
-            pltpu.VMEM((128, SUB, WIDTH), jnp.bfloat16),
-            pltpu.VMEM((64, SUB, 2 * WIDTH), jnp.bfloat16),
-            pltpu.SemaphoreType.DMA((2 * GROUPS + 1,)),
-        ],
+        scratch_shapes=[pltpu.SemaphoreType.DMA((2,))],
         compiler_params=pltpu.CompilerParams(vmem_limit_bytes=8 * 2**20),
         cost_estimate=pl.CostEstimate(flops=0, bytes_accessed=4 * 10**6, transcendentals=0),
         name="third_operand",
-    )(codes, my_item, got, diagonal)
+    )(codes, my_item, pltpu.with_memory_space_constraint(got, pltpu.VMEM), diagonal)
 
 
 def rotate_kernel(
     place_ref,
-    own_ref,
-    side_ref,
-    below_ref,
-    cross_ref,
+    block_ref,
     mine_ref,
     theirs_ref,
     first_ref,
@@ -288,45 +252,71 @@
     new_first_ref,
     new_second_ref,
     direction_ref,
-    block_ref,
+    held_ref,
     left_ref,
     right_ref,
+    moment_ref,
+    sems,
 ):
-    row = place_ref[0]
     col = place_ref[1]
-    place_quads(row, col, (own_ref, side_ref, below_ref, cross_ref), block_ref)
+    to_left = left_ref
+    to_right = [right_ref.at[:, :, 256 * n : 256 * (n + 1)] for n in range(2)]
+
+    def load(source, target, n):
+        return pltpu.make_async_copy(source, target, sems.at[n])
 
     @pl.when(col == 0)
     def _():
-        left_ref[...] = mine_ref[:, :, 0:512]
-        right_ref[:, :, 0:256] = mine_ref[:, :, 512:768]
-        right_ref[:, :, 256:512] = theirs_ref[:, :, 0:256]
+        load(mine_ref.at[:, :, 0:512], to_left, 0).start()
+        load(mine_ref.at[:, :, 512:768], to_right[0], 1).start()
+        load(theirs_ref.at[:, :, 0:256], to_right[1], 2).start()
 
     @pl.when(col == 1)
     def _():
-        left_ref[...] = theirs_ref[:, :, 0:512]
-        right_ref[...] = mine_ref[:, :, 256:768]
-
-    left = left_ref[...].reshape(1024, 512)
-    left_rot = dot_tn(left, block_ref[...]).astype(jnp.bfloat16)
-    rotated = dot_nn(left_rot, right_ref[...].reshape(1024, 512))
-    new_first = beta_one * first_ref[...] + (1.0 - beta_one) * rotated
-    new_second = beta_two * second_ref[...] + (1.0 - beta_two) * rotated * rotated
-    new_first_ref[...] = new_first
-    new_second_ref[...] = new_second
-    direction_ref[...] = (new_first / (jnp.sqrt(new_second) + epsilon)).astype(jnp.bfloat16)
-
-
-def rotate(place, quads, mine, theirs, first, second):
+        load(theirs_ref.at[:, :, 0:512], to_left, 0).start()
+        load(mine_ref.at[:, :, 256:512], to_right[0], 1).start()
+        load(mine_ref.at[:, :, 512:768], to_right[1], 2).start()
+
+    load_block = load(block_ref, held_ref, 3)
+    load_block.start()
+    moments = [load(first_ref, moment_ref.at[0], 4), load(second_ref, moment_ref.at[1], 5)]
+    for moment in moments:
+        moment.start()
+    load(mine_ref.at[:, :, 0:512], to_left, 0).wait()
+    load_block.wait()
+    size = held_ref.shape[0]
+    left_rot = dot_tn(left_ref[...].reshape(size, 512), held_ref[...]).astype(jnp.bfloat16)
+    for n in range(2):
+        load(mine_ref.at[:, :, 0:256], to_right[n], 1 + n).wait()
+    for moment in moments:
+        moment.wait()
+    right = right_ref[...].reshape(size, 512)
+    stores = []
+    for part in range(4):
+        rows = slice(128 * part, 128 * (part + 1))
+        rotated = dot_nn(left_rot[rows], right)
+        new_first = beta_one * moment_ref[0, rows] + (1.0 - beta_one) * rotated
+        new_second = beta_two * moment_ref[1, rows] + (1.0 - beta_two) * rotated * rotated
+        direction_ref[rows] = (new_first / (jnp.sqrt(new_second) + epsilon)).astype(jnp.bfloat16)
+        moment_ref[0, rows] = new_first
+        moment_ref[1, rows] = new_second
+        for n, target in enumerate((new_first_ref, new_second_ref)):
+            store = load(moment_ref.at[n, rows], target.at[rows], 6 + 2 * part + n)
+            store.start()
+            stores.append(store)
+    for store in stores:
+        store.wait()
+
+
+def rotate(place, block, mine, theirs, first, second):
     half = first.shape[0]
+    block, first, second = (
+        pltpu.with_memory_space_constraint(value, pltpu.HBM) for value in (block, first, second)
+    )
     return pl.pallas_call(
         rotate_kernel,
-        grid=(1,),
-        in_specs=[whole(pltpu.SMEM)]
-        + [pl.BlockSpec((half, half), lambda _: (0, 0))] * 4
-        + [pl.BlockSpec((128, SUB, 768), lambda _: (0, 0, 0))] * 2
-        + [pl.BlockSpec((half, half), lambda _: (0, 0))] * 2,
-        out_specs=[pl.BlockSpec((half, half), lambda _: (0, 0))] * 3,
+        in_specs=[whole(pltpu.SMEM)] + [whole(pl.ANY)] * 5,
+        out_specs=[whole(pl.ANY), whole(pl.ANY), whole()],
         out_shape=[
             jax.ShapeDtypeStruct((half, half), jnp.float32),
             jax.ShapeDtypeStruct((half, half), jnp.float32),
@@ -336,13 +326,15 @@
             pltpu.VMEM((1024, 1024), jnp.bfloat16),
             pltpu.VMEM((128, SUB, 512), jnp.bfloat16),
             pltpu.VMEM((128, SUB, 512), jnp.bfloat16),
-        ],
-        compiler_params=PARAMS,
+            pltpu.VMEM((2, half, half), jnp.float32),
+            pltpu.SemaphoreType.DMA((14,)),
+        ],
+        compiler_params=pltpu.CompilerParams(vmem_limit_bytes=20 * 2**20),
         cost_estimate=pl.CostEstimate(
             flops=16 * 10**8, bytes_accessed=10**7, transcendentals=10**6
         ),
         name="rotate",
-    )(place, *quads, mine, theirs, first, second)
+    )(place, block, mine, theirs, first, second)
 
 
 def back_kernel(
@@ -407,28 +399,78 @@
     )(place, own, side, mine, theirs)
 
 
+def settle_kernel(factor_ref, out_ref, strips_ref, sems):
+    count = strips_ref.shape[0]
+    loads = [
+        pltpu.make_async_copy(factor_ref.at[strip_of(n)], strips_ref.at[n], sems.at[0, n])
+        for n in range(count)
+    ]
+    stores = [
+        pltpu.make_async_copy(strips_ref.at[n], out_ref.at[strip_of(n)], sems.at[1, n])
+        for n in range(count)
+    ]
+    for load in loads:
+        load.start()
+    for load, store in zip(loads, stores):
+        load.wait()
+        store.start()
+    for store in stores:
+        store.wait()
+
+
+def settle(factors):
+    slots, size, _ = factors.shape
+    return pl.pallas_call(
+        settle_kernel,
+        in_specs=[whole(pl.ANY)],
+        out_specs=whole(pl.ANY),
+        out_shape=pltpu.HBM(factors.shape, factors.dtype),
+        scratch_shapes=[
+            pltpu.VMEM((4 * slots, GB, size), jnp.float32),
+            pltpu.SemaphoreType.DMA((2, 4 * slots)),
+        ],
+        compiler_params=pltpu.CompilerParams(vmem_limit_bytes=12 * 2**20),
+        cost_estimate=pl.CostEstimate(
+            flops=0, bytes_accessed=16 * 10**6, transcendentals=0
+        ),
+        name="settle",
+    )(pltpu.with_memory_space_constraint(factors, pltpu.HBM))
+
+
+def strip_of(n):
+    return (n // 4, slice(GB * (n % 4), GB * (n % 4 + 1)))
+
+
 def factor_kernel(
     items_ref, live_ref, factor_ref, got_ref, out_ref, strips_ref, held_ref, sems
 ):
     slots = factor_ref.shape[0]
     count = 4 * slots
-
-    def at(n):
-        return (n // 4, slice(GB * (n % 4), GB * (n % 4 + 1)))
-
-    pieces = pltpu.make_async_copy(got_ref, held_ref, sems.at[2 * count])
+    spans = [slice(2 * WIDTH * slot, 2 * WIDTH * (slot + 1)) for slot in range(slots)]
+    spans.append(slice(2 * WIDTH * slots, got_ref.shape[3]))
+    pieces = [
+        pltpu.make_async_copy(
+            got_ref.at[:, :, :, span], held_ref.at[:, :, :, span], sems.at[2 * count + n]
+        )
+        for n, span in enumerate(spans)
+    ]
     loads = [
-        pltpu.make_async_copy(factor_ref.at[at(n)], strips_ref.at[n], sems.at[n])
+        pltpu.make_async_copy(out_ref.at[strip_of(n)], strips_ref.at[n], sems.at[n])
         for n in range(count)
     ]
     stores = [
-        pltpu.make_async_copy(strips_ref.at[n], out_ref.at[at(n)], sems.at[count + n])
+        pltpu.make_async_copy(strips_ref.at[n], out_ref.at[strip_of(n)], sems.at[count + n])
         for n in range(count)
     ]
-    loads[0].start()
-    pieces.start()
-    for n in range(1, count):
-        loads[n].start()
+    for slot in range(slots):
+
+        @pl.when(live_ref[slot] != 0)
+        def _(slot=slot):
+            pieces[slot].start()
+            if slot == 0:
+                pieces[slots].start()
+            for n in range(4 * slot, 4 * (slot + 1)):
+                loads[n].start()
 
     def piece(slot, which, n):
         lane = 2 * WIDTH * slot + (2 * which + n % 2) * 128
@@ -466,13 +508,19 @@
             ) * sub_block(slot, row, col)
 
     for n in range(count):
-        loads[n].wait()
-        if n == 0:
-            pieces.wait()
-        pl.when(live_ref[n // 4] != 0)(functools.partial(mix, n))
-        stores[n].start()
+
+        @pl.when(live_ref[n // 4] != 0)
+        def _(n=n):
+            if n % 4 == 0:
+                pieces[n // 4].wait()
+            if n == 0:
+                pieces[slots].wait()
+            loads[n].wait()
+            mix(n)
+            stores[n].start()
+
     for n in range(count):
-        stores[n].wait()
+        pl.when(live_ref[n // 4] != 0)(stores[n].wait)
 
 
 def update_factors(items, live, factors, got):
@@ -482,12 +530,13 @@
         factor_kernel,
         in_specs=[whole(pltpu.SMEM)] * 2 + [whole(pl.ANY)] * 2,
         out_specs=whole(pl.ANY),
-        out_shape=jax.ShapeDtypeStruct(factors.shape, factors.dtype),
+        out_shape=pltpu.HBM(factors.shape, factors.dtype),
         scratch_shapes=[
             pltpu.VMEM((4 * slots, GB, size), jnp.float32),
             pltpu.VMEM(got.shape, got.dtype),
-            pltpu.SemaphoreType.DMA((8 * slots + 1,)),
-        ],
+            pltpu.SemaphoreType.DMA((9 * slots + 1,)),
+        ],
+        input_output_aliases={2: 0},
         compiler_params=pltpu.CompilerParams(vmem_limit_bytes=20 * 2**20),
         cost_estimate=pl.CostEstimate(
             flops=4 * 10**6, bytes_accessed=2 * 10**7, transcendentals=0
@@ -524,7 +573,8 @@
     side = swap_neighbour(gradient, "rep")
     cross = swap_neighbour(below, "rep")
     quads = (gradient, side, below, cross)
-    gram, diagonal = gram_pieces(place, quads)
+    settled = settle(factors)
+    gram, diagonal, block = gram_pieces(place, quads)
     gram = gram.reshape(devices, SUB, WIDTH)
 
     second_parts = second_operand(codes, first_got.reshape(devices * slots, SUB, size), gram)
@@ -535,12 +585,12 @@
     third_got = lax.all_to_all(third_parts, BOTH, 0, 0, tiled=True)
 
     new_first, new_second, direction = rotate(
-        place, quads, mine, theirs, first_moment, second_moment
+        place, block, mine, theirs, first_moment, second_moment
     )
     other = swap_neighbour(direction, "rep")
     keep, give = back(place, direction, other, mine, theirs)
     update = keep + swap_neighbour(give, "fsdp").astype(jnp.float32)
-    new_factors = update_factors(items, live, factors, third_got)
+    new_factors = update_factors(items, live, settled, third_got)
     return (update, new_first, new_second, new_factors)
 
 

time: 157 us -> 156 us (level); the launches traced: 157 us -> 153 us
  local copies, waits for them, and re-layouts: 5.41 us -> 0.01 us
  Pallas kernels: 27.1 us -> 31.1 us
  waiting for transfers between devices: 65.7 us -> 63 us
    pallas_call x1 -> x2, Pallas kernels: 5.41 us -> 12.1 us  [the longest x1 6.42 us: settle(): pl.pallas_call(settle_kernel, in_specs=[whole(pl.ANY)], out_specs=whole(p...]
    unnamed x22 -> x4, local copies, waits for them, and re-layouts: 5.41 us -> 0.01 us
    pallas_call x1, Pallas kernels: 7.91 us -> 4.6 us  [update_factors(): pl.pallas_call(factor_kernel, in_specs=[whole(pltpu.SMEM)] * 2 + [whole(p...]
  transfers between devices with their start and end apart: 8 -> 8, of which waited for: 5 -> 5; matrix products, arithmetic and copies ran while one was open for 0% -> 0% of each run, Pallas kernels for 16% -> 19%
where the time goes in v2:
time: 156 us; the launch traced here: 153 us
  waiting for transfers between devices  63 us (40%)
  blocking collectives  34.4 us (22%)
  Pallas kernels  31.1 us (20%)
  starting transfers between devices  21.9 us (14%)
  other arithmetic  1.57 us (1%)
    all_to_all x1, waiting for transfers between devices, shards(): first_got = lax.all_to_all(first_parts, BOTH, 0, 0, tiled=True)  46.1 us
    all_to_all x1, blocking collectives, shards(): mine = lax.all_to_all(second_parts, BOTH, 0, 0, tiled=True)  34.4 us
    all_to_all x1, waiting for transfers between devices, shards(): third_got = lax.all_to_all(third_parts, BOTH, 0, 0, tiled=True)  13.5 us
    all_to_all x1, starting transfers between devices, shards(): first_got = lax.all_to_all(first_parts, BOTH, 0, 0, tiled=True)  11.1 us
    pallas_call x1, Pallas kernels, settle(): pl.pallas_call(settle_kernel, in_specs=[whole(pl.ANY)], out_specs=whole(p...  6.42 us
    ppermute x6, starting transfers between devices, swap_neighbour(): return lax.ppermute(value, axis, pairs)  6.16 us
    pallas_call x1, Pallas kernels, rotate(): pl.pallas_call(rotate_kernel, in_specs=[whole(pltpu.SMEM)] + [whole(pl.AN...  5.64 us
    all_to_all x1, starting transfers between devices, shards(): third_got = lax.all_to_all(third_parts, BOTH, 0, 0, tiled=True)  4.66 us
  transfers between devices with their start and end apart: 8, of which 5 were waited for; matrix products, arithmetic and copies ran while one was open for 0% of the time, Pallas kernels for 19%

profile of v2, /device:TPU:1, one launch (start us, length us, event | category | flops | bytes accessed | tf_op | source)
XLA Modules:
  0.0 152.8 jit_solution(4161111301892303456)
XLA Ops:
  0.6 2.2 %collective-permute-start.1 = (bf16[512,512]{1,0:T(8,128)(2,1)}, bf16[512,512]{1,0:T(8,128)(2,1)S(1)}, u32[]{:S(2)}, u32[]{:S(2)}) collective-permute-start(bf16[512,512]{1,0:T(8,128)(2,1)} %own_ref.1), channel_id=1, source_target_pairs={{0,8},{8,0},{16,24},{24,16},{32,40},{40,32},{48,56},{56,48},{64,72... | collective-permute-start | bytes 1572872 | tf_op jit(solution)/shard_map/ppermute | solution.py:25
  2.8 3.3 %interleave.1 = bf16[128,2,8,1024]{3,2,1,0:T(8,128)(2,1)} custom-call(bf16[2,128,8,1024]{3,2,1,0:T(8,128)(2,1)} %bitcast.8), custom_call_target="tpu_custom_call" | custom-call | bytes 8000000 | tf_op jit(solution)/shard_map/interleave/pallas_call | solution.py:68
  6.2 11.1 %all-to-all-start = ((bf16[128,2,8,1024]{3,2,1,0:T(8,128)(2,1)}), bf16[128,2,8,1024]{3,2,1,0:T(8,128)(2,1)}, u32[]{:S(2)}, u32[]{:S(2)}) async-start(bf16[128,2,8,1024]{3,2,1,0:T(8,128)(2,1)} %interleave.1), calls=%async_computation | async-start | bytes 8388608 | tf_op jit(solution)/shard_map/all_to_all | solution.py:561
  17.3 1.2 collective-permute-start
  18.7 0.2 convert_reduce_fusion
  18.9 1.2 collective-permute-done.side_ref
  20.1 0.7 collective-permute-done.2.cross_ref
  20.8 3.0 %gram_pieces.1 = (bf16[32,4,8,256]{3,2,1,0:T(8,128)(2,1)S(1)}, bf16[8,128]{1,0:T(8,128)(2,1)S(1)}, bf16[1024,1024]{1,0:T(8,128)(2,1)}) custom-call(s32[2]{0:T(128)S(1)} %pad_add_fusion.place_ref, bf16[512,512]{1,0:T(8,128)(2,1)S(1)} %copy-done, bf16[512,512]{1,0:T(8,128)(2,1)S(1)} %collective-permute-done.side_ref, ...), custom_call_target="tpu_custom_call" | custom-call | flops 35999997952 | bytes 3000000 | tf_op jit(solution)/shard_map/gram_pieces/pallas_call | solution.py:138
  23.8 46.1 %all-to-all-done = bf16[128,2,8,1024]{3,2,1,0:T(8,128)(2,1)} async-done(((bf16[128,2,8,1024]{3,2,1,0:T(8,128)(2,1)}), bf16[128,2,8,1024]{3,2,1,0:T(8,128)(2,1)}, u32[]{:S(2)}, u32[]{:S(2)}) %all-to-all-start) | async-done | bytes 4194336 | tf_op jit(solution)/shard_map/all_to_all | solution.py:561
  69.9 2.0 %second_operand.1 = bf16[128,8,1024]{2,1,0:T(8,128)(2,1)S(1)} custom-call(s32[64]{0:T(128)S(1)} %multiply_add_fusion.codes_ref, bf16[256,8,1024]{2,1,0:T(8,128)(2,1)} %bitcast.3.rows_ref, bf16[128,8,256]{2,1,0:T(8,128)(2,1)S(1)} %bitcast.7), custom_call_target="tpu_custom_call" | custom-call | bytes 8000000 | tf_op jit(solution)/shard_map/second_operand/pallas_call | solution.py:190
  71.9 34.4 %all_to_all.15.mine_ref.got_ref = bf16[128,8,1024]{2,1,0:T(8,128)(2,1)S(1)} all-to-all(bf16[128,8,1024]{2,1,0:T(8,128)(2,1)S(1)} %second_operand.1), channel_id=1, replica_groups=mesh['fsdp'=16,'rep'=8] {'fsdp','rep'}, dimensions={0} | all-to-all | bytes 4194304 | tf_op jit(solution)/shard_map/all_to_all | solution.py:581
  106.3 0.9 collective-permute-start.3
  107.2 2.2 %third_operand.1 = bf16[128,8,1152]{2,1,0:T(8,128)(2,1)} custom-call(s32[64]{0:T(128)S(1)} %multiply_add_fusion.codes_ref, s32[1]{0:T(128)} %bitcast.5.mine_ref, bf16[128,8,1024]{2,1,0:T(8,128)(2,1)S(1)} %all_to_all.15.mine_ref.got_ref, bf16[8,128]{1,0:T(8,128)(2,1)S(1)} %get-tuple-element.19.diagonal_ref), custom_call_target="tpu_custom_call" | custom-call | bytes 4000000 | tf_op jit(solution)/shard_map/third_operand/pallas_call | solution.py:233
  109.5 4.7 %all-to-all-start.2 = ((bf16[128,8,1152]{2,1,0:T(8,128)(2,1)}), bf16[128,8,1152]{2,1,0:T(8,128)(2,1)}, u32[]{:S(2)}, u32[]{:S(2)}) async-start(bf16[128,8,1152]{2,1,0:T(8,128)(2,1)} %third_operand.1), calls=%async_computation.2 | async-start | bytes 4718592 | tf_op jit(solution)/shard_map/all_to_all | solution.py:585
  114.1 5.6 %rotate.1 = (f32[512,512]{1,0:T(8,128)}, f32[512,512]{1,0:T(8,128)}, bf16[512,512]{1,0:T(8,128)(2,1)S(1)}) custom-call(s32[2]{0:T(128)S(1)} %pad_add_fusion.place_ref, bf16[1024,1024]{1,0:T(8,128)(2,1)} %get-tuple-element.12.block_ref, bf16[128,8,1024]{2,1,0:T(8,128)(2,1)S(1)} %all_to_all.15.mine_ref.got_ref, ...), custom_call_target="tpu_custom_call" | custom-call | flops 1600000000 | bytes 10000000 | tf_op jit(solution)/shard_map/rotate/pallas_call | solution.py:316
  119.8 1.2 collective-permute-start.4
  121.0 1.5 %collective-permute-done.4.side_ref = bf16[512,512]{1,0:T(8,128)(2,1)S(1)} collective-permute-done((bf16[512,512]{1,0:T(8,128)(2,1)S(1)}, bf16[512,512]{1,0:T(8,128)(2,1)S(1)}, u32[]{:S(2)}, u32[]{:S(2)}) %collective-permute-start.4) | collective-permute-done | bytes 524320 | tf_op jit(solution)/shard_map/ppermute | solution.py:25
  122.5 3.9 %back.1 = (f32[512,512]{1,0:T(8,128)S(1)}, bf16[512,512]{1,0:T(8,128)(2,1)}) custom-call(s32[2]{0:T(128)S(1)} %pad_add_fusion.place_ref, bf16[512,512]{1,0:T(8,128)(2,1)S(1)} %get-tuple-element.14.own_ref, bf16[512,512]{1,0:T(8,128)(2,1)S(1)} %collective-permute-done.4.side_ref, bf16[128,8,1024]{2,1,0:T(8,128)(2,1)S(1)} %all_to_all.15.mine_ref.got_ref, ...), custom_call_target="tpu_custom_call" | custom-call | flops 1100000000 | bytes 6000000 | tf_op jit(solution)/shard_map/back/pallas_call | solution.py:380
  126.4 0.5 collective-permute-start.5
  126.9 6.4 %settle.1.factor_ref = f32[2,1024,1024]{2,1,0:T(8,128)} custom-call(f32[2,1024,1024]{2,1,0:T(8,128)} %factor_ref.1), custom_call_target="tpu_custom_call" | custom-call | bytes 16000000 | tf_op jit(solution)/shard_map/settle/pallas_call | solution.py:423
  133.4 0.2 fusion.2
  133.6 13.5 %all-to-all-done.2 = bf16[128,8,1152]{2,1,0:T(8,128)(2,1)} async-done(((bf16[128,8,1152]{2,1,0:T(8,128)(2,1)}), bf16[128,8,1152]{2,1,0:T(8,128)(2,1)}, u32[]{:S(2)}, u32[]{:S(2)}) %all-to-all-start.2) | async-done | bytes 2359328 | tf_op jit(solution)/shard_map/all_to_all | solution.py:585
  147.0 4.6 %update_factors.1 = f32[2,1024,1024]{2,1,0:T(8,128)} custom-call(s32[2]{0:T(128)S(1)} %get-tuple-element.21.items_ref, s32[2]{0:T(128)S(1)} %get-tuple-element.20.live_ref, f32[2,1024,1024]{2,1,0:T(8,128)} %settle.1.factor_ref, bf16[32,4,8,1152]{3,2,1,0:T(8,128)(2,1)} %bitcast.6.got_ref), custom_call_target="tpu_custom_call", output_to_operand_aliasing={{}: (2, {})} | custom-call | flops 4000000 | bytes 20000000 | tf_op jit(solution)/shard_map/update_factors/pallas_call | solution.py:529
  151.6 1.1 convert_add_fusion
  (11 shorter events, 0.2 us)
Async XLA Ops:
  0.6 17.9 %collective-permute-start.1 = (bf16[512,512]{1,0:T(8,128)(2,1)}, bf16[512,512]{1,0:T(8,128)(2,1)S(1)}, u32[]{:S(2)}, u32[]{:S(2)}) collective-permute-start(bf16[512,512]{1,0:T(8,128)(2,1)} %own_ref.1), channel_id=1, source_target_pairs={{0,8},{8,0},{16,24},{24,16},{32,40},{40,32},{48,56},{56,48},{64,72... | collective-permute-start | bytes 1572872 | tf_op jit(solution)/shard_map/ppermute | solution.py:25
  6.1 11.2 %copy-start = (bf16[512,512]{1,0:T(8,128)(2,1)S(1)}, bf16[512,512]{1,0:T(8,128)(2,1)}, u32[]{:S(2)}) copy-start(bf16[512,512]{1,0:T(8,128)(2,1)} %own_ref.1) | copy-start | bytes 1572868
  6.2 12.6 %copy-start.1 = (s32[64]{0:T(128)S(1)}, s32[64]{0:T(128)}, u32[]{:S(2)}) copy-start(s32[64]{0:T(128)} %param.11) | copy-start | bytes 772
  6.2 63.8 %all-to-all-start = ((bf16[128,2,8,1024]{3,2,1,0:T(8,128)(2,1)}), bf16[128,2,8,1024]{3,2,1,0:T(8,128)(2,1)}, u32[]{:S(2)}, u32[]{:S(2)}) async-start(bf16[128,2,8,1024]{3,2,1,0:T(8,128)(2,1)} %interleave.1), calls=%async_computation | async-start | bytes 8388608 | tf_op jit(solution)/shard_map/all_to_all | solution.py:561
  17.3 2.8 %collective-permute-start = (bf16[512,512]{1,0:T(8,128)(2,1)S(1)}, bf16[512,512]{1,0:T(8,128)(2,1)S(1)}, u32[]{:S(2)}, u32[]{:S(2)}) collective-permute-start(bf16[512,512]{1,0:T(8,128)(2,1)S(1)} %copy-done), channel_id=1, source_target_pairs={{0,1},{1,0},{2,3},{3,2},{4,5},{5,4},{6,7},{7,6},{8,9},{9,8},{10,11... | collective-permute-start | bytes 1572872 | tf_op jit(solution)/shard_map/ppermute | solution.py:25
  18.5 2.3 %collective-permute-start.2 = (bf16[512,512]{1,0:T(8,128)(2,1)S(1)}, bf16[512,512]{1,0:T(8,128)(2,1)S(1)}, u32[]{:S(2)}, u32[]{:S(2)}) collective-permute-start(bf16[512,512]{1,0:T(8,128)(2,1)S(1)} %collective-permute-done.1.below_ref), channel_id=1, source_target_pairs={{0,1},{1,0},{2,3},{3,2},{4,5},{5,4},{6,7},{7,6},{8,9},{9,8},{10,11... | collective-permute-start | bytes 1572872 | tf_op jit(solution)/shard_map/ppermute | solution.py:25
  106.3 7.8 %collective-permute-start.3 = (bf16[128,8,1024]{2,1,0:T(8,128)(2,1)S(1)}, bf16[128,8,1024]{2,1,0:T(8,128)(2,1)}, u32[]{:S(2)}, u32[]{:S(2)}) collective-permute-start(bf16[128,8,1024]{2,1,0:T(8,128)(2,1)S(1)} %all_to_all.15.mine_ref.got_ref), channel_id=1, source_target_pairs={{0,1},{1,0},{2,3},{3,2},{4,5},{5,4},{6,7},{7,6},{8,9},{9,8},{10,11... | collective-permute-start | bytes 6291464 | tf_op jit(solution)/shard_map/ppermute | solution.py:25
  109.5 37.6 %all-to-all-start.2 = ((bf16[128,8,1152]{2,1,0:T(8,128)(2,1)}), bf16[128,8,1152]{2,1,0:T(8,128)(2,1)}, u32[]{:S(2)}, u32[]{:S(2)}) async-start(bf16[128,8,1152]{2,1,0:T(8,128)(2,1)} %third_operand.1), calls=%async_computation.2 | async-start | bytes 4718592 | tf_op jit(solution)/shard_map/all_to_all | solution.py:585
  119.8 2.7 %collective-permute-start.4 = (bf16[512,512]{1,0:T(8,128)(2,1)S(1)}, bf16[512,512]{1,0:T(8,128)(2,1)S(1)}, u32[]{:S(2)}, u32[]{:S(2)}) collective-permute-start(bf16[512,512]{1,0:T(8,128)(2,1)S(1)} %get-tuple-element.14.own_ref), channel_id=1, source_target_pairs={{0,1},{1,0},{2,3},{3,2},{4,5},{5,4},{6,7},{7,6},{8,9},{9,8},{10,11... | collective-permute-start | bytes 1572872 | tf_op jit(solution)/shard_map/ppermute | solution.py:25
  126.4 25.2 %collective-permute-start.5 = (bf16[512,512]{1,0:T(8,128)(2,1)}, bf16[512,512]{1,0:T(8,128)(2,1)S(1)}, u32[]{:S(2)}, u32[]{:S(2)}) collective-permute-start(bf16[512,512]{1,0:T(8,128)(2,1)} %get-tuple-element.16), channel_id=1, source_target_pairs={{0,8},{8,0},{16,24},{24,16},{32,40},{40,32},{48,56},{56,48},{64,72... | collective-permute-start | bytes 1572872 | tf_op jit(solution)/shard_map/ppermute | solution.py:25

commit v3 on v2

--- a/solution.py
+++ b/solution.py
@@ -16,6 +16,9 @@
 GB = 256
 ABOVE = (((0, 1), (0, 2), (0, 3)), ((1, 2), (1, 3), (2, 3)))
 WIDTH = 2 * 128
+CHIPS = 64
+ROW, COL, MINE, LIVE, NAMED = 64, 65, 66, 67, 69
+BASES = 512 + 1024
 BOTH = ("fsdp", "rep")
 PARAMS = pltpu.CompilerParams(vmem_limit_bytes=24 * 2**20)
 
@@ -94,7 +97,7 @@
 
 
 def gram_kernel(
-    place_ref, own_ref, side_ref, below_ref, cross_ref, out_ref, diagonal_ref, block_ref
+    place_ref, own_ref, side_ref, below_ref, cross_ref, keep_ref, give_ref, diagonal_ref, block_ref
 ):
     row = place_ref[0]
     col = place_ref[1]
@@ -124,7 +127,9 @@
             for half in range(2):
                 tiles = value[:, half * 128 : (half + 1) * 128].reshape(GB // SUB, SUB, 128)
                 span = slice(n % 2 * 128, (n % 2 + 1) * 128)
-                out_ref[:, 2 * half + n // 2, :, span] = tiles.astype(jnp.bfloat16)
+                kept = n // 2 == (0 if left_gram else 1)
+                target = keep_ref if kept else give_ref
+                target[:, half, :, span] = tiles.astype(jnp.bfloat16)
 
     for left_gram in (True, False):
         for which in range(2):
@@ -138,15 +143,16 @@
     return pl.pallas_call(
         gram_kernel,
         in_specs=[whole(pltpu.SMEM)] + [whole()] * 4,
-        out_specs=[whole()] * 3,
+        out_specs=[whole()] * 4,
         out_shape=[
-            jax.ShapeDtypeStruct((32, 4, SUB, WIDTH), jnp.bfloat16),
+            jax.ShapeDtypeStruct((32, 2, SUB, WIDTH), jnp.bfloat16),
+            jax.ShapeDtypeStruct((32, 2, SUB, WIDTH), jnp.bfloat16),
             jax.ShapeDtypeStruct((SUB, 128), jnp.bfloat16),
             pltpu.HBM((size, size), jnp.bfloat16),
         ],
         compiler_params=PARAMS,
         cost_estimate=pl.CostEstimate(
-            flops=36 * 10**9, bytes_accessed=3 * 10**6, transcendentals=0
+            flops=32 * 10**9, bytes_accessed=3 * 10**6, transcendentals=0
         ),
         name="gram_pieces",
     )(place, *quads)
@@ -155,91 +161,99 @@
 GROUPS = 4
 
 
-def second_kernel(codes_ref, rows_ref, gram_ref, out_ref, live_ref, sems):
+def second_kernel(facts_ref, rows_ref, keep_ref, other_ref, out_ref, live_ref, sems):
+    core = facts_ref[COL]
     items = live_ref.shape[0] // GROUPS
-    pieces = pltpu.make_async_copy(gram_ref, out_ref.at[:, :, 768:1024], sems.at[GROUPS])
+    pieces = []
+    for n, source in enumerate((keep_ref, other_ref)):
+        lane = pl.multiple_of(BASES + WIDTH * (core ^ n), WIDTH)
+        pieces.append(
+            pltpu.make_async_copy(
+                source, out_ref.at[:, :, pl.ds(lane, WIDTH)], sems.at[GROUPS + n]
+            )
+        )
     for group in range(GROUPS):
 
-        @pl.loop(items * group, items * (group + 1))
+        @pl.loop(items * group, items * (group + 1), unroll=True)
         def _(item, group=group):
             pltpu.make_async_copy(
-                rows_ref.at[codes_ref[item]], live_ref.at[item], sems.at[group]
+                rows_ref.at[facts_ref[item]], live_ref.at[item], sems.at[group]
             ).start()
 
-    pieces.start()
+    for piece in pieces:
+        piece.start()
     for group in range(GROUPS):
         pltpu.make_async_copy(
             rows_ref.at[0:items], live_ref.at[items * group : items * (group + 1)], sems.at[group]
         ).wait()
 
-        @pl.loop(items // 2 * group, items // 2 * (group + 1))
+        @pl.loop(items // 2 * group, items // 2 * (group + 1), unroll=True)
         def _(block):
             left = live_ref[2 * block]
             right = live_ref[2 * block + 1]
-            base = (block // 4) * 16 + (block % 4) * 2
             for i in range(2):
-                at = base + 8 * i
+                at = (block // 4) * 8 + block % 4 + 4 * i
                 out_ref[at, :, 0:512] = left[:, 512 * i : 512 * (i + 1)]
-                out_ref[at, :, 512:768] = right[:, 0:256]
-                out_ref[at + 1, :, 0:768] = right[:, 256:1024]
-
-    pieces.wait()
-
-
-def second_operand(codes, rows, gram):
+                out_ref[at, :, 512:BASES] = right
+
+    for piece in pieces:
+        piece.wait()
+
+
+def second_operand(facts, rows, keep, other):
     return pl.pallas_call(
         second_kernel,
-        in_specs=[whole(pltpu.SMEM), whole(pl.ANY), whole(pl.ANY)],
+        in_specs=[whole(pltpu.SMEM), whole(pl.ANY), whole(), whole()],
         out_specs=whole(),
-        out_shape=pltpu.VMEM((128, SUB, 1024), jnp.bfloat16),
+        out_shape=pltpu.VMEM((CHIPS, SUB, BASES + 2 * WIDTH), jnp.bfloat16),
         scratch_shapes=[
             pltpu.VMEM((64, SUB, 1024), jnp.bfloat16),
-            pltpu.SemaphoreType.DMA((GROUPS + 1,)),
+            pltpu.SemaphoreType.DMA((GROUPS + 2,)),
         ],
         compiler_params=pltpu.CompilerParams(vmem_limit_bytes=8 * 2**20),
         cost_estimate=pl.CostEstimate(flops=0, bytes_accessed=8 * 10**6, transcendentals=0),
         name="second_operand",
-    )(codes, rows, gram)
-
-
-def third_kernel(codes_ref, mine_ref, got_ref, diagonal_ref, out_ref, sems):
+    )(facts, rows, keep, other)
+
+
+def third_kernel(facts_ref, got_ref, diagonal_ref, out_ref, sems):
     apart = pltpu.make_async_copy(
         diagonal_ref,
-        out_ref.at[codes_ref[mine_ref[0]] // 2, :, 4 * WIDTH : 4 * WIDTH + 128],
+        out_ref.at[facts_ref[facts_ref[MINE]] // 2, :, 4 * WIDTH : 4 * WIDTH + 128],
         sems.at[0],
     )
     apart.start()
 
-    @pl.loop(0, 32)
+    @pl.loop(0, 32, unroll=True)
     def _(block):
         for side in range(2):
-            code = codes_ref[2 * block + side]
+            code = facts_ref[2 * block + side]
             for half in range(2):
-                source = (block // 4) * 16 + (block % 4) * 2 + side + 8 * half
+                source = (block // 4) * 8 + block % 4 + 4 * half
                 lane = pl.multiple_of(code % 2 * (2 * WIDTH) + half * WIDTH, WIDTH)
                 pltpu.make_async_copy(
-                    got_ref.at[source, :, 768:1024],
+                    got_ref.at[source, :, BASES + side * WIDTH : BASES + (side + 1) * WIDTH],
                     out_ref.at[code // 2, :, pl.ds(lane, WIDTH)],
                     sems.at[1],
                 ).start()
 
     pltpu.make_async_copy(
-        got_ref.at[:, :, 768:1024], out_ref.at[:, :, 0:WIDTH], sems.at[1]
+        got_ref.at[:, :, BASES:], out_ref.at[0:CHIPS, :, 0 : 2 * WIDTH], sems.at[1]
     ).wait()
     apart.wait()
 
 
-def third_operand(codes, my_item, got, diagonal):
+def third_operand(facts, got, diagonal):
     return pl.pallas_call(
         third_kernel,
-        in_specs=[whole(pltpu.SMEM), whole(pltpu.SMEM), whole(pl.ANY), whole(pl.ANY)],
+        in_specs=[whole(pltpu.SMEM), whole(pl.ANY), whole(pl.ANY)],
         out_specs=whole(pl.ANY),
         out_shape=pltpu.HBM((128, SUB, 4 * WIDTH + 128), jnp.bfloat16),
         scratch_shapes=[pltpu.SemaphoreType.DMA((2,))],
         compiler_params=pltpu.CompilerParams(vmem_limit_bytes=8 * 2**20),
         cost_estimate=pl.CostEstimate(flops=0, bytes_accessed=4 * 10**6, transcendentals=0),
         name="third_operand",
-    )(codes, my_item, pltpu.with_memory_space_constraint(got, pltpu.VMEM), diagonal)
+    )(facts, pltpu.with_memory_space_constraint(got, pltpu.VMEM), diagonal)
 
 
 def rotate_kernel(
@@ -259,35 +273,30 @@
     sems,
 ):
     col = place_ref[1]
-    to_left = left_ref
-    to_right = [right_ref.at[:, :, 256 * n : 256 * (n + 1)] for n in range(2)]
 
     def load(source, target, n):
         return pltpu.make_async_copy(source, target, sems.at[n])
 
-    @pl.when(col == 0)
-    def _():
-        load(mine_ref.at[:, :, 0:512], to_left, 0).start()
-        load(mine_ref.at[:, :, 512:768], to_right[0], 1).start()
-        load(theirs_ref.at[:, :, 0:256], to_right[1], 2).start()
-
-    @pl.when(col == 1)
-    def _():
-        load(theirs_ref.at[:, :, 0:512], to_left, 0).start()
-        load(mine_ref.at[:, :, 256:512], to_right[0], 1).start()
-        load(mine_ref.at[:, :, 512:768], to_right[1], 2).start()
-
+    lane = pl.multiple_of(512 + 512 * col, 512)
+    lefts = []
+    rights = []
+    for n, source in enumerate((mine_ref, theirs_ref)):
+        lefts.append(load(source.at[:, :, 0:512], left_ref.at[:, col ^ n], n))
+        rights.append(load(source.at[:, :, pl.ds(lane, 512)], right_ref.at[:, col ^ n], 14 + n))
+    for copy in lefts + rights:
+        copy.start()
     load_block = load(block_ref, held_ref, 3)
     load_block.start()
     moments = [load(first_ref, moment_ref.at[0], 4), load(second_ref, moment_ref.at[1], 5)]
     for moment in moments:
         moment.start()
-    load(mine_ref.at[:, :, 0:512], to_left, 0).wait()
+    for copy in lefts:
+        copy.wait()
     load_block.wait()
     size = held_ref.shape[0]
     left_rot = dot_tn(left_ref[...].reshape(size, 512), held_ref[...]).astype(jnp.bfloat16)
-    for n in range(2):
-        load(mine_ref.at[:, :, 0:256], to_right[n], 1 + n).wait()
+    for copy in rights:
+        copy.wait()
     for moment in moments:
         moment.wait()
     right = right_ref[...].reshape(size, 512)
@@ -324,10 +333,10 @@
         ],
         scratch_shapes=[
             pltpu.VMEM((1024, 1024), jnp.bfloat16),
-            pltpu.VMEM((128, SUB, 512), jnp.bfloat16),
-            pltpu.VMEM((128, SUB, 512), jnp.bfloat16),
+            pltpu.VMEM((CHIPS, 2, SUB, 512), jnp.bfloat16),
+            pltpu.VMEM((CHIPS, 2, SUB, 512), jnp.bfloat16),
             pltpu.VMEM((2, half, half), jnp.float32),
-            pltpu.SemaphoreType.DMA((14,)),
+            pltpu.SemaphoreType.DMA((16,)),
         ],
         compiler_params=pltpu.CompilerParams(vmem_limit_bytes=20 * 2**20),
         cost_estimate=pl.CostEstimate(
@@ -348,53 +357,60 @@
     left_ref,
     right_ref,
     strip_ref,
+    sems,
 ):
     row = place_ref[0]
     col = place_ref[1]
     half = own_ref.shape[0]
+    span = pl.ds(col * (CHIPS // 2), CHIPS // 2)
+    lefts = []
+    rights = []
+    for n, source in enumerate((mine_ref, theirs_ref)):
+        lefts.append(
+            pltpu.make_async_copy(
+                source.at[:, :, 0:512], left_ref.at[:, col ^ n], sems.at[n]
+            )
+        )
+        rights.append(
+            pltpu.make_async_copy(
+                source.at[span, :, 512:BASES], right_ref.at[:, col ^ n], sems.at[2 + n]
+            )
+        )
+    for copy in rights + lefts:
+        copy.start()
     strip_ref[:, pl.ds(pl.multiple_of(col * half, half), half)] = own_ref[...]
     strip_ref[:, pl.ds(pl.multiple_of((1 - col) * half, half), half)] = side_ref[...]
-
-    @pl.when(col == 0)
-    def _():
-        left_ref[...] = mine_ref[:, :, 0:512]
-        right_ref[:, :, 0:256] = mine_ref[0:64, :, 512:768]
-        right_ref[:, :, 256:1024] = theirs_ref[0:64]
-
-    @pl.when(col == 1)
-    def _():
-        left_ref[...] = theirs_ref[:, :, 0:512]
-        right_ref[:, :, 0:256] = theirs_ref[64:128, :, 512:768]
-        right_ref[:, :, 256:1024] = mine_ref[64:128]
-
-    half_back = dot_nt(strip_ref[...], right_ref[...].reshape(512, 1024)).astype(jnp.bfloat16)
-    groups = half // SUB
-    keep = left_ref[pl.ds(row * groups, groups)].reshape(half, 512)
-    give = left_ref[pl.ds((1 - row) * groups, groups)].reshape(half, 512)
+    for copy in rights:
+        copy.wait()
+    half_back = dot_nt(strip_ref[...], right_ref[...].reshape(half, 1024)).astype(jnp.bfloat16)
+    for copy in lefts:
+        copy.wait()
+    keep = left_ref[pl.ds(row * (CHIPS // 2), CHIPS // 2)].reshape(half, 512)
+    give = left_ref[pl.ds((1 - row) * (CHIPS // 2), CHIPS // 2)].reshape(half, 512)
+    give_ref[...] = dot_nn(give, half_back).astype(jnp.bfloat16)
     keep_ref[...] = dot_nn(keep, half_back)
-    give_ref[...] = dot_nn(give, half_back).astype(jnp.bfloat16)
 
 
 def back(place, own, side, mine, theirs):
     half = own.shape[0]
     return pl.pallas_call(
         back_kernel,
-        grid=(1,),
-        in_specs=[whole(pltpu.SMEM)]
-        + [pl.BlockSpec((half, half), lambda _: (0, 0))] * 2
-        + [pl.BlockSpec((128, SUB, 768), lambda _: (0, 0, 0))] * 2,
-        out_specs=[pl.BlockSpec((half, half), lambda _: (0, 0))] * 2,
+        in_specs=[whole(pltpu.SMEM), whole(), whole(), whole(pl.ANY), whole(pl.ANY)],
+        out_specs=[whole()] * 2,
         out_shape=[
             jax.ShapeDtypeStruct((half, half), jnp.float32),
             jax.ShapeDtypeStruct((half, half), jnp.bfloat16),
         ],
         scratch_shapes=[
-            pltpu.VMEM((128, SUB, 512), jnp.bfloat16),
-            pltpu.VMEM((64, SUB, 1024), jnp.bfloat16),
+            pltpu.VMEM((CHIPS, 2, SUB, 512), jnp.bfloat16),
+            pltpu.VMEM((CHIPS // 2, 2, SUB, 1024), jnp.bfloat16),
             pltpu.VMEM((half, 2 * half), jnp.bfloat16),
+            pltpu.SemaphoreType.DMA((4,)),
         ],
         compiler_params=PARAMS,
-        cost_estimate=pl.CostEstimate(flops=11 * 10**8, bytes_accessed=6 * 10**6, transcendentals=0),
+        cost_estimate=pl.CostEstimate(
+            flops=11 * 10**8, bytes_accessed=6 * 10**6, transcendentals=0
+        ),
         name="back",
     )(place, own, side, mine, theirs)
 
@@ -442,7 +458,7 @@
 
 
 def factor_kernel(
-    items_ref, live_ref, factor_ref, got_ref, out_ref, strips_ref, held_ref, sems
+    facts_ref, factor_ref, got_ref, out_ref, strips_ref, held_ref, sems
 ):
     slots = factor_ref.shape[0]
     count = 4 * slots
@@ -464,7 +480,7 @@
     ]
     for slot in range(slots):
 
-        @pl.when(live_ref[slot] != 0)
+        @pl.when(facts_ref[LIVE + slot] != 0)
         def _(slot=slot):
             pieces[slot].start()
             if slot == 0:
@@ -492,7 +508,7 @@
         r, c = grid_positions()
         if row % 2 == 0:
             return jnp.where(r <= c, value, value.T)
-        item = items_ref[slot]
+        item = facts_ref[NAMED + slot]
         block = item // 2
         source = (block // 4 * 2 + row // 2) * 8 + block % 4 * 2 + item % 2
         tile = held_ref[source // 4, source % 4, :, 4 * WIDTH :].astype(jnp.float32)
@@ -509,7 +525,7 @@
 
     for n in range(count):
 
-        @pl.when(live_ref[n // 4] != 0)
+        @pl.when(facts_ref[LIVE + n // 4] != 0)
         def _(n=n):
             if n % 4 == 0:
                 pieces[n // 4].wait()
@@ -520,15 +536,15 @@
             stores[n].start()
 
     for n in range(count):
-        pl.when(live_ref[n // 4] != 0)(stores[n].wait)
-
-
-def update_factors(items, live, factors, got):
+        pl.when(facts_ref[LIVE + n // 4] != 0)(stores[n].wait)
+
+
+def update_factors(facts, factors, got):
     slots, size, _ = factors.shape
     got = got.reshape(32, 4, SUB, got.shape[2])
     return pl.pallas_call(
         factor_kernel,
-        in_specs=[whole(pltpu.SMEM)] * 2 + [whole(pl.ANY)] * 2,
+        in_specs=[whole(pltpu.SMEM)] + [whole(pl.ANY)] * 2,
         out_specs=whole(pl.ANY),
         out_shape=pltpu.HBM(factors.shape, factors.dtype),
         scratch_shapes=[
@@ -536,13 +552,13 @@
             pltpu.VMEM(got.shape, got.dtype),
             pltpu.SemaphoreType.DMA((9 * slots + 1,)),
         ],
-        input_output_aliases={2: 0},
+        input_output_aliases={1: 0},
         compiler_params=pltpu.CompilerParams(vmem_limit_bytes=20 * 2**20),
         cost_estimate=pl.CostEstimate(
             flops=4 * 10**6, bytes_accessed=2 * 10**7, transcendentals=0
         ),
         name="update_factors",
-    )(items, live, pltpu.with_memory_space_constraint(factors, pltpu.HBM), got)
+    )(facts, pltpu.with_memory_space_constraint(factors, pltpu.HBM), got)
 
 
 def shards(gradient, first_moment, second_moment, factors, eigen_bases, owners):
@@ -569,19 +585,26 @@
     hits = (codes[None, :] == my_codes[:, None]).astype(jnp.int32)
     live = jnp.sum(hits, axis=1)
     items = jnp.sum(hits * item_index[None, :], axis=1)
+    facts = jnp.concatenate([codes, place, my_item, live, items]).astype(jnp.int32)
 
     side = swap_neighbour(gradient, "rep")
     cross = swap_neighbour(below, "rep")
     quads = (gradient, side, below, cross)
     settled = settle(factors)
-    gram, diagonal, block = gram_pieces(place, quads)
-    gram = gram.reshape(devices, SUB, WIDTH)
-
-    second_parts = second_operand(codes, first_got.reshape(devices * slots, SUB, size), gram)
-    mine = lax.all_to_all(second_parts, BOTH, 0, 0, tiled=True)
+    kept_gram, given_gram, diagonal, block = gram_pieces(place, quads)
+    other_gram = swap_neighbour(given_gram.reshape(CHIPS, SUB, WIDTH), "rep")
+    kept_gram = kept_gram.reshape(CHIPS, SUB, WIDTH)
+
+    second_parts = second_operand(
+        facts, first_got.reshape(devices * slots, SUB, size), kept_gram, other_gram
+    )
+    same_core = [[2 * chip + core for chip in range(CHIPS)] for core in range(2)]
+    mine = lax.all_to_all(
+        second_parts, BOTH, 0, 0, axis_index_groups=same_core, tiled=True
+    )
     theirs = swap_neighbour(mine, "rep")
 
-    third_parts = third_operand(codes, my_item, mine, diagonal)
+    third_parts = third_operand(facts, mine, diagonal)
     third_got = lax.all_to_all(third_parts, BOTH, 0, 0, tiled=True)
 
     new_first, new_second, direction = rotate(
@@ -590,7 +613,7 @@
     other = swap_neighbour(direction, "rep")
     keep, give = back(place, direction, other, mine, theirs)
     update = keep + swap_neighbour(give, "fsdp").astype(jnp.float32)
-    new_factors = update_factors(items, live, settled, third_got)
+    new_factors = update_factors(facts, settled, third_got)
     return (update, new_first, new_second, new_factors)
 
 

time: 156 us -> 155 us (level)
  Pallas kernels: 31.1 us -> 26.6 us
  waiting for transfers between devices: 63 us -> 66.4 us
  starting transfers between devices: 21.9 us -> 24.4 us
  blocking collectives: 34.4 us -> 32.4 us
    ppermute x6 -> x7, waiting for transfers between devices: 3.46 us -> 8.21 us  [swap_neighbour(): return lax.ppermute(value, axis, pairs)]
    pallas_call x3, Pallas kernels: 10.7 us -> 6.38 us  [the longest x1 3.73 us: back(): pl.pallas_call(back_kernel, in_specs=[whole(pltpu.SMEM), whole(), whole()...]
    ppermute x6 -> x7, starting transfers between devices: 6.16 us -> 8.33 us  [swap_neighbour(): return lax.ppermute(value, axis, pairs)]
    all_to_all x1, blocking collectives: 34.4 us -> 32.4 us  [shards(): lax.all_to_all(second_parts, BOTH, 0, 0, axis_index_groups=same_core, til...]
  transfers between devices with their start and end apart: 8 -> 9, of which waited for: 5 -> 7; matrix products, arithmetic and copies ran while one was open for 0% -> 0% of each run, Pallas kernels for 19% -> 16%
where the time goes in v3:
time: 155 us; the launch traced here: 152 us
  waiting for transfers between devices  66.4 us (43%)
  blocking collectives  32.4 us (21%)
  Pallas kernels  26.6 us (17%)
  starting transfers between devices  24.4 us (16%)
  other arithmetic  1.57 us (1%)
    all_to_all x1, waiting for transfers between devices, shards(): first_got = lax.all_to_all(first_parts, BOTH, 0, 0, tiled=True)  44.6 us
    all_to_all x1, blocking collectives, shards(): lax.all_to_all(second_parts, BOTH, 0, 0, axis_index_groups=same_core, til...  32.4 us
    all_to_all x1, waiting for transfers between devices, shards(): third_got = lax.all_to_all(third_parts, BOTH, 0, 0, tiled=True)  13.6 us
    all_to_all x1, starting transfers between devices, shards(): first_got = lax.all_to_all(first_parts, BOTH, 0, 0, tiled=True)  11.1 us
    ppermute x7, starting transfers between devices, swap_neighbour(): return lax.ppermute(value, axis, pairs)  8.33 us
    ppermute x7, waiting for transfers between devices, swap_neighbour(): return lax.ppermute(value, axis, pairs)  8.21 us
    pallas_call x1, Pallas kernels, settle(): pl.pallas_call(settle_kernel, in_specs=[whole(pl.ANY)], out_specs=whole(p...  6.42 us
    pallas_call x1, Pallas kernels, rotate(): pl.pallas_call(rotate_kernel, in_specs=[whole(pltpu.SMEM)] + [whole(pl.AN...  5.72 us
  transfers between devices with their start and end apart: 9, of which 7 were waited for; matrix products, arithmetic and copies ran while one was open for 0% of the time, Pallas kernels for 16%

profile of v3, /device:TPU:1, one launch (start us, length us, event | category | flops | bytes accessed | tf_op | source)
XLA Modules:
  0.0 152.1 jit_solution(3809182959462881765)
XLA Ops:
  0.6 2.2 %collective-permute-start.1 = (bf16[512,512]{1,0:T(8,128)(2,1)}, bf16[512,512]{1,0:T(8,128)(2,1)S(1)}, u32[]{:S(2)}, u32[]{:S(2)}) collective-permute-start(bf16[512,512]{1,0:T(8,128)(2,1)} %own_ref.1), channel_id=1, source_target_pairs={{0,8},{8,0},{16,24},{24,16},{32,40},{40,32},{48,56},{56,48},{64,72... | collective-permute-start | bytes 1572872 | tf_op jit(solution)/shard_map/ppermute | solution.py:28
  2.8 3.3 %interleave.1 = bf16[128,2,8,1024]{3,2,1,0:T(8,128)(2,1)} custom-call(bf16[2,128,8,1024]{3,2,1,0:T(8,128)(2,1)} %bitcast.10), custom_call_target="tpu_custom_call" | custom-call | bytes 8000000 | tf_op jit(solution)/shard_map/interleave/pallas_call | solution.py:71
  6.2 11.1 %all-to-all-start = ((bf16[128,2,8,1024]{3,2,1,0:T(8,128)(2,1)}), bf16[128,2,8,1024]{3,2,1,0:T(8,128)(2,1)}, u32[]{:S(2)}, u32[]{:S(2)}) async-start(bf16[128,2,8,1024]{3,2,1,0:T(8,128)(2,1)} %interleave.1), calls=%async_computation | async-start | bytes 8388608 | tf_op jit(solution)/shard_map/all_to_all | solution.py:577
  17.3 1.2 collective-permute-start
  18.9 1.2 collective-permute-done.side_ref
  20.1 0.7 collective-permute-done.2.cross_ref
  20.8 3.0 %gram_pieces.1 = (bf16[32,2,8,256]{3,2,1,0:T(8,128)(2,1)S(1)}, bf16[32,2,8,256]{3,2,1,0:T(8,128)(2,1)S(1)}, bf16[8,128]{1,0:T(8,128)(2,1)S(1)}, bf16[1024,1024]{1,0:T(8,128)(2,1)}) custom-call(s32[2]{0:T(128)S(1)} %pad_add_fusion.place_ref, bf16[512,512]{1,0:T(8,128)(2,1)S(1)} %copy-done, bf16[512,512]{1,0:T(8,128)(2,1)S(1)} %collective-permute-done.side_ref, ...), custom_call_target="tpu_custom_call" | custom-call | flops 32000000000 | bytes 3000000 | tf_op jit(solution)/shard_map/gram_pieces/pallas_call | solution.py:143
  24.4 0.9 collective-permute-done.3.other_ref
  25.4 44.6 %all-to-all-done = bf16[128,2,8,1024]{3,2,1,0:T(8,128)(2,1)} async-done(((bf16[128,2,8,1024]{3,2,1,0:T(8,128)(2,1)}), bf16[128,2,8,1024]{3,2,1,0:T(8,128)(2,1)}, u32[]{:S(2)}, u32[]{:S(2)}) %all-to-all-start) | async-done | bytes 4194336 | tf_op jit(solution)/shard_map/all_to_all | solution.py:577
  69.9 1.8 %second_operand.1 = bf16[64,8,2048]{2,1,0:T(8,128)(2,1)S(1)} custom-call(s32[71]{0:T(128)S(1)} %concatenate.4.facts_ref, bf16[256,8,1024]{2,1,0:T(8,128)(2,1)} %bitcast.4.rows_ref, bf16[64,8,256]{2,1,0:T(8,128)(2,1)S(1)} %bitcast.8, bf16[64,8,256]{2,1,0:T(8,128)(2,1)S(1)} %collective-permute-done.3.other_ref), custom_call_target="tpu_custom_call" | custom-call | bytes 8000000 | tf_op jit(solution)/shard_map/second_operand/pallas_call | solution.py:204
  71.7 32.4 %all_to_all.15.mine_ref.got_ref = bf16[64,8,2048]{2,1,0:T(8,128)(2,1)S(1)} all-to-all(bf16[64,8,2048]{2,1,0:T(8,128)(2,1)S(1)} %second_operand.1), channel_id=1, replica_groups={{0,2,4,6,8,10,12,14,16,18,20,22,24,26,28,30,32,34,36,38,40,42,44,46,48,..., dimensions={0} | all-to-all | bytes 4194304 | tf_op jit(solution)/shard_map/all_to_all | solution.py:602
  104.1 2.5 %collective-permute-start.4 = (bf16[64,8,2048]{2,1,0:T(8,128)(2,1)S(1)}, bf16[64,8,2048]{2,1,0:T(8,128)(2,1)}, u32[]{:S(2)}, u32[]{:S(2)}) collective-permute-start(bf16[64,8,2048]{2,1,0:T(8,128)(2,1)S(1)} %all_to_all.15.mine_ref.got_ref), channel_id=1, source_target_pairs={{0,1},{1,0},{2,3},{3,2},{4,5},{5,4},{6,7},{7,6},{8,9},{9,8},{10,11... | collective-permute-start | bytes 6291464 | tf_op jit(solution)/shard_map/ppermute | solution.py:28
  106.6 1.8 %third_operand.1 = bf16[128,8,1152]{2,1,0:T(8,128)(2,1)} custom-call(s32[71]{0:T(128)S(1)} %concatenate.4.facts_ref, bf16[64,8,2048]{2,1,0:T(8,128)(2,1)S(1)} %all_to_all.15.mine_ref.got_ref, bf16[8,128]{1,0:T(8,128)(2,1)S(1)} %get-tuple-element.21.diagonal_ref), custom_call_target="tpu_custom_call" | custom-call | bytes 4000000 | tf_op jit(solution)/shard_map/third_operand/pallas_call | solution.py:247
  108.4 4.9 %all-to-all-start.2 = ((bf16[128,8,1152]{2,1,0:T(8,128)(2,1)}), bf16[128,8,1152]{2,1,0:T(8,128)(2,1)}, u32[]{:S(2)}, u32[]{:S(2)}) async-start(bf16[128,8,1152]{2,1,0:T(8,128)(2,1)} %third_operand.1), calls=%async_computation.2 | async-start | bytes 4718592 | tf_op jit(solution)/shard_map/all_to_all | solution.py:608
  113.4 5.7 %rotate.1 = (f32[512,512]{1,0:T(8,128)}, f32[512,512]{1,0:T(8,128)}, bf16[512,512]{1,0:T(8,128)(2,1)S(1)}) custom-call(s32[2]{0:T(128)S(1)} %pad_add_fusion.place_ref, bf16[1024,1024]{1,0:T(8,128)(2,1)} %get-tuple-element.13.block_ref, bf16[64,8,2048]{2,1,0:T(8,128)(2,1)S(1)} %all_to_all.15.mine_ref.got_ref, ...), custom_call_target="tpu_custom_call" | custom-call | flops 1600000000 | bytes 10000000 | tf_op jit(solution)/shard_map/rotate/pallas_call | solution.py:325
  119.1 1.2 collective-permute-start.5
  120.3 1.5 %collective-permute-done.5.side_ref = bf16[512,512]{1,0:T(8,128)(2,1)S(1)} collective-permute-done((bf16[512,512]{1,0:T(8,128)(2,1)S(1)}, bf16[512,512]{1,0:T(8,128)(2,1)S(1)}, u32[]{:S(2)}, u32[]{:S(2)}) %collective-permute-start.5) | collective-permute-done | bytes 524320 | tf_op jit(solution)/shard_map/ppermute | solution.py:28
  121.9 3.7 %back.1 = (f32[512,512]{1,0:T(8,128)S(1)}, bf16[512,512]{1,0:T(8,128)(2,1)}) custom-call(s32[2]{0:T(128)S(1)} %pad_add_fusion.place_ref, bf16[512,512]{1,0:T(8,128)(2,1)S(1)} %get-tuple-element.16.own_ref, bf16[512,512]{1,0:T(8,128)(2,1)S(1)} %collective-permute-done.5.side_ref, bf16[64,8,2048]{2,1,0:T(8,128)(2,1)S(1)} %all_to_all.15.mine_ref.got_ref, ...), custom_call_target="tpu_custom_call" | custom-call | flops 1100000000 | bytes 6000000 | tf_op jit(solution)/shard_map/back/pallas_call | solution.py:396
  125.6 0.7 collective-permute-start.6
  126.3 6.4 %settle.1.factor_ref = f32[2,1024,1024]{2,1,0:T(8,128)} custom-call(f32[2,1024,1024]{2,1,0:T(8,128)} %factor_ref.1), custom_call_target="tpu_custom_call" | custom-call | bytes 16000000 | tf_op jit(solution)/shard_map/settle/pallas_call | solution.py:439
  132.7 13.6 %all-to-all-done.2 = bf16[128,8,1152]{2,1,0:T(8,128)(2,1)} async-done(((bf16[128,8,1152]{2,1,0:T(8,128)(2,1)}), bf16[128,8,1152]{2,1,0:T(8,128)(2,1)}, u32[]{:S(2)}, u32[]{:S(2)}) %all-to-all-start.2) | async-done | bytes 2359328 | tf_op jit(solution)/shard_map/all_to_all | solution.py:608
  146.3 0.8 update_factors.1
  147.1 3.8 %collective-permute-done.6 = bf16[512,512]{1,0:T(8,128)(2,1)S(1)} collective-permute-done((bf16[512,512]{1,0:T(8,128)(2,1)}, bf16[512,512]{1,0:T(8,128)(2,1)S(1)}, u32[]{:S(2)}, u32[]{:S(2)}) %collective-permute-start.6) | collective-permute-done | bytes 524320 | tf_op jit(solution)/shard_map/ppermute | solution.py:28
  151.0 1.1 convert_add_fusion
  (14 shorter events, 1.0 us)
Async XLA Ops:
  0.6 17.9 %collective-permute-start.1 = (bf16[512,512]{1,0:T(8,128)(2,1)}, bf16[512,512]{1,0:T(8,128)(2,1)S(1)}, u32[]{:S(2)}, u32[]{:S(2)}) collective-permute-start(bf16[512,512]{1,0:T(8,128)(2,1)} %own_ref.1), channel_id=1, source_target_pairs={{0,8},{8,0},{16,24},{24,16},{32,40},{40,32},{48,56},{56,48},{64,72... | collective-permute-start | bytes 1572872 | tf_op jit(solution)/shard_map/ppermute | solution.py:28
  6.1 11.2 %copy-start = (bf16[512,512]{1,0:T(8,128)(2,1)S(1)}, bf16[512,512]{1,0:T(8,128)(2,1)}, u32[]{:S(2)}) copy-start(bf16[512,512]{1,0:T(8,128)(2,1)} %own_ref.1) | copy-start | bytes 1572868
  6.2 12.6 %copy-start.1 = (s32[64]{0:T(128)S(1)}, s32[64]{0:T(128)}, u32[]{:S(2)}) copy-start(s32[64]{0:T(128)} %param.11) | copy-start | bytes 772
  6.2 63.8 %all-to-all-start = ((bf16[128,2,8,1024]{3,2,1,0:T(8,128)(2,1)}), bf16[128,2,8,1024]{3,2,1,0:T(8,128)(2,1)}, u32[]{:S(2)}, u32[]{:S(2)}) async-start(bf16[128,2,8,1024]{3,2,1,0:T(8,128)(2,1)} %interleave.1), calls=%async_computation | async-start | bytes 8388608 | tf_op jit(solution)/shard_map/all_to_all | solution.py:577
  17.3 2.8 %collective-permute-start = (bf16[512,512]{1,0:T(8,128)(2,1)S(1)}, bf16[512,512]{1,0:T(8,128)(2,1)S(1)}, u32[]{:S(2)}, u32[]{:S(2)}) collective-permute-start(bf16[512,512]{1,0:T(8,128)(2,1)S(1)} %copy-done), channel_id=1, source_target_pairs={{0,1},{1,0},{2,3},{3,2},{4,5},{5,4},{6,7},{7,6},{8,9},{9,8},{10,11... | collective-permute-start | bytes 1572872 | tf_op jit(solution)/shard_map/ppermute | solution.py:28
  18.5 2.3 %collective-permute-start.2 = (bf16[512,512]{1,0:T(8,128)(2,1)S(1)}, bf16[512,512]{1,0:T(8,128)(2,1)S(1)}, u32[]{:S(2)}, u32[]{:S(2)}) collective-permute-start(bf16[512,512]{1,0:T(8,128)(2,1)S(1)} %collective-permute-done.1.below_ref), channel_id=1, source_target_pairs={{0,1},{1,0},{2,3},{3,2},{4,5},{5,4},{6,7},{7,6},{8,9},{9,8},{10,11... | collective-permute-start | bytes 1572872 | tf_op jit(solution)/shard_map/ppermute | solution.py:28
  23.8 1.5 %collective-permute-start.3 = (bf16[64,8,256]{2,1,0:T(8,128)(2,1)S(1)}, bf16[64,8,256]{2,1,0:T(8,128)(2,1)S(1)}, u32[]{:S(2)}, u32[]{:S(2)}) collective-permute-start(bf16[64,8,256]{2,1,0:T(8,128)(2,1)S(1)} %bitcast.9), channel_id=1, source_target_pairs={{0,1},{1,0},{2,3},{3,2},{4,5},{5,4},{6,7},{7,6},{8,9},{9,8},{10,11... | collective-permute-start | bytes 786440 | tf_op jit(solution)/shard_map/ppermute | solution.py:28
  104.1 9.3 %collective-permute-start.4 = (bf16[64,8,2048]{2,1,0:T(8,128)(2,1)S(1)}, bf16[64,8,2048]{2,1,0:T(8,128)(2,1)}, u32[]{:S(2)}, u32[]{:S(2)}) collective-permute-start(bf16[64,8,2048]{2,1,0:T(8,128)(2,1)S(1)} %all_to_all.15.mine_ref.got_ref), channel_id=1, source_target_pairs={{0,1},{1,0},{2,3},{3,2},{4,5},{5,4},{6,7},{7,6},{8,9},{9,8},{10,11... | collective-permute-start | bytes 6291464 | tf_op jit(solution)/shard_map/ppermute | solution.py:28
  108.4 37.9 %all-to-all-start.2 = ((bf16[128,8,1152]{2,1,0:T(8,128)(2,1)}), bf16[128,8,1152]{2,1,0:T(8,128)(2,1)}, u32[]{:S(2)}, u32[]{:S(2)}) async-start(bf16[128,8,1152]{2,1,0:T(8,128)(2,1)} %third_operand.1), calls=%async_computation.2 | async-start | bytes 4718592 | tf_op jit(solution)/shard_map/all_to_all | solution.py:608
  119.1 2.8 %collective-permute-start.5 = (bf16[512,512]{1,0:T(8,128)(2,1)S(1)}, bf16[512,512]{1,0:T(8,128)(2,1)S(1)}, u32[]{:S(2)}, u32[]{:S(2)}) collective-permute-start(bf16[512,512]{1,0:T(8,128)(2,1)S(1)} %get-tuple-element.16.own_ref), channel_id=1, source_target_pairs={{0,1},{1,0},{2,3},{3,2},{4,5},{5,4},{6,7},{7,6},{8,9},{9,8},{10,11... | collective-permute-start | bytes 1572872 | tf_op jit(solution)/shard_map/ppermute | solution.py:28
  125.6 25.4 %collective-permute-start.6 = (bf16[512,512]{1,0:T(8,128)(2,1)}, bf16[512,512]{1,0:T(8,128)(2,1)S(1)}, u32[]{:S(2)}, u32[]{:S(2)}) collective-permute-start(bf16[512,512]{1,0:T(8,128)(2,1)} %get-tuple-element.18), channel_id=1, source_target_pairs={{0,8},{8,0},{16,24},{24,16},{32,40},{40,32},{48,56},{56,48},{64,72... | collective-permute-start | bytes 1572872 | tf_op jit(solution)/shard_map/ppermute | solution.py:28

commit v4 on v3

--- a/solution.py
+++ b/solution.py
@@ -19,6 +19,7 @@
 CHIPS = 64
 ROW, COL, MINE, LIVE, NAMED = 64, 65, 66, 67, 69
 BASES = 512 + 1024
+SPARE = BASES + 2 * WIDTH
 BOTH = ("fsdp", "rep")
 PARAMS = pltpu.CompilerParams(vmem_limit_bytes=24 * 2**20)
 
@@ -161,7 +162,9 @@
 GROUPS = 4
 
 
-def second_kernel(facts_ref, rows_ref, keep_ref, other_ref, out_ref, live_ref, sems):
+def second_kernel(
+    facts_ref, rows_ref, keep_ref, other_ref, diagonal_ref, out_ref, live_ref, sems
+):
     core = facts_ref[COL]
     items = live_ref.shape[0] // GROUPS
     pieces = []
@@ -172,6 +175,12 @@
                 source, out_ref.at[:, :, pl.ds(lane, WIDTH)], sems.at[GROUPS + n]
             )
         )
+    owner = facts_ref[facts_ref[MINE]] // 4
+    pieces.append(
+        pltpu.make_async_copy(
+            diagonal_ref, out_ref.at[owner, :, SPARE : SPARE + 128], sems.at[GROUPS + 2]
+        )
+    )
     for group in range(GROUPS):
 
         @pl.loop(items * group, items * (group + 1), unroll=True)
@@ -200,30 +209,23 @@
         piece.wait()
 
 
-def second_operand(facts, rows, keep, other):
+def second_operand(facts, rows, keep, other, diagonal):
     return pl.pallas_call(
         second_kernel,
-        in_specs=[whole(pltpu.SMEM), whole(pl.ANY), whole(), whole()],
+        in_specs=[whole(pltpu.SMEM), whole(pl.ANY), whole(), whole(), whole()],
         out_specs=whole(),
-        out_shape=pltpu.VMEM((CHIPS, SUB, BASES + 2 * WIDTH), jnp.bfloat16),
+        out_shape=pltpu.VMEM((CHIPS, SUB, SPARE + 128), jnp.bfloat16),
         scratch_shapes=[
             pltpu.VMEM((64, SUB, 1024), jnp.bfloat16),
-            pltpu.SemaphoreType.DMA((GROUPS + 2,)),
+            pltpu.SemaphoreType.DMA((GROUPS + 3,)),
         ],
         compiler_params=pltpu.CompilerParams(vmem_limit_bytes=8 * 2**20),
         cost_estimate=pl.CostEstimate(flops=0, bytes_accessed=8 * 10**6, transcendentals=0),
         name="second_operand",
-    )(facts, rows, keep, other)
-
-
-def third_kernel(facts_ref, got_ref, diagonal_ref, out_ref, sems):
-    apart = pltpu.make_async_copy(
-        diagonal_ref,
-        out_ref.at[facts_ref[facts_ref[MINE]] // 2, :, 4 * WIDTH : 4 * WIDTH + 128],
-        sems.at[0],
-    )
-    apart.start()
-
+    )(facts, rows, keep, other, diagonal)
+
+
+def third_kernel(facts_ref, got_ref, out_ref, sems):
     @pl.loop(0, 32, unroll=True)
     def _(block):
         for side in range(2):
@@ -234,30 +236,29 @@
                 pltpu.make_async_copy(
                     got_ref.at[source, :, BASES + side * WIDTH : BASES + (side + 1) * WIDTH],
                     out_ref.at[code // 2, :, pl.ds(lane, WIDTH)],
-                    sems.at[1],
+                    sems.at[0],
                 ).start()
 
     pltpu.make_async_copy(
-        got_ref.at[:, :, BASES:], out_ref.at[0:CHIPS, :, 0 : 2 * WIDTH], sems.at[1]
+        got_ref.at[:, :, BASES:SPARE], out_ref.at[0:CHIPS, :, 0 : 2 * WIDTH], sems.at[0]
     ).wait()
-    apart.wait()
-
-
-def third_operand(facts, got, diagonal):
+
+
+def third_operand(facts, got):
     return pl.pallas_call(
         third_kernel,
-        in_specs=[whole(pltpu.SMEM), whole(pl.ANY), whole(pl.ANY)],
+        in_specs=[whole(pltpu.SMEM), whole(pl.ANY)],
         out_specs=whole(pl.ANY),
-        out_shape=pltpu.HBM((128, SUB, 4 * WIDTH + 128), jnp.bfloat16),
-        scratch_shapes=[pltpu.SemaphoreType.DMA((2,))],
+        out_shape=pltpu.HBM((128, SUB, 4 * WIDTH), jnp.bfloat16),
+        scratch_shapes=[pltpu.SemaphoreType.DMA((1,))],
         compiler_params=pltpu.CompilerParams(vmem_limit_bytes=8 * 2**20),
         cost_estimate=pl.CostEstimate(flops=0, bytes_accessed=4 * 10**6, transcendentals=0),
         name="third_operand",
-    )(facts, pltpu.with_memory_space_constraint(got, pltpu.VMEM), diagonal)
+    )(facts, pltpu.with_memory_space_constraint(got, pltpu.VMEM))
 
 
 def rotate_kernel(
-    place_ref,
+    facts_ref,
     block_ref,
     mine_ref,
     theirs_ref,
@@ -266,16 +267,28 @@
     new_first_ref,
     new_second_ref,
     direction_ref,
+    spare_ref,
     held_ref,
     left_ref,
     right_ref,
     moment_ref,
     sems,
 ):
-    col = place_ref[1]
+    col = facts_ref[COL]
 
     def load(source, target, n):
         return pltpu.make_async_copy(source, target, sems.at[n])
+
+    def spare(source, n):
+        item = facts_ref[NAMED + n // 2]
+        block = item // 2
+        chip = (block // 4 * 2 + n % 2) * 4 + block % 4
+        return load(source.at[chip, :, SPARE : SPARE + 128], spare_ref.at[n], 16 + n)
+
+    for n in range(4):
+        same = facts_ref[NAMED + n // 2] % 2 == col
+        pl.when(same)(spare(mine_ref, n).start)
+        pl.when(jnp.logical_not(same))(spare(theirs_ref, n).start)
 
     lane = pl.multiple_of(512 + 512 * col, 512)
     lefts = []
@@ -315,9 +328,11 @@
             stores.append(store)
     for store in stores:
         store.wait()
-
-
-def rotate(place, block, mine, theirs, first, second):
+    for n in range(4):
+        spare(mine_ref, n).wait()
+
+
+def rotate(facts, block, mine, theirs, first, second):
     half = first.shape[0]
     block, first, second = (
         pltpu.with_memory_space_constraint(value, pltpu.HBM) for value in (block, first, second)
@@ -325,25 +340,26 @@
     return pl.pallas_call(
         rotate_kernel,
         in_specs=[whole(pltpu.SMEM)] + [whole(pl.ANY)] * 5,
-        out_specs=[whole(pl.ANY), whole(pl.ANY), whole()],
+        out_specs=[whole(pl.ANY), whole(pl.ANY), whole(), whole(pl.ANY)],
         out_shape=[
             jax.ShapeDtypeStruct((half, half), jnp.float32),
             jax.ShapeDtypeStruct((half, half), jnp.float32),
             jax.ShapeDtypeStruct((half, half), jnp.bfloat16),
+            pltpu.HBM((4, SUB, 128), jnp.bfloat16),
         ],
         scratch_shapes=[
             pltpu.VMEM((1024, 1024), jnp.bfloat16),
             pltpu.VMEM((CHIPS, 2, SUB, 512), jnp.bfloat16),
             pltpu.VMEM((CHIPS, 2, SUB, 512), jnp.bfloat16),
             pltpu.VMEM((2, half, half), jnp.float32),
-            pltpu.SemaphoreType.DMA((16,)),
+            pltpu.SemaphoreType.DMA((20,)),
         ],
         compiler_params=pltpu.CompilerParams(vmem_limit_bytes=20 * 2**20),
         cost_estimate=pl.CostEstimate(
             flops=16 * 10**8, bytes_accessed=10**7, transcendentals=10**6
         ),
         name="rotate",
-    )(place, block, mine, theirs, first, second)
+    )(facts, block, mine, theirs, first, second)
 
 
 def back_kernel(
@@ -415,6 +431,40 @@
     )(place, own, side, mine, theirs)
 
 
+def finish_kernel(keep_ref, other_ref, out_ref, sum_ref, sems):
+    parts = sems.shape[0]
+    rows = sum_ref.shape[0] // parts
+    stores = []
+    for part in range(parts):
+        span = slice(rows * part, rows * (part + 1))
+        sum_ref[span] = keep_ref[span] + other_ref[span].astype(jnp.float32)
+        stores.append(pltpu.make_async_copy(sum_ref.at[span], out_ref.at[span], sems.at[part]))
+        stores[part].start()
+    for store in stores:
+        store.wait()
+
+
+def finish(keep, other):
+    keep, other = (
+        pltpu.with_memory_space_constraint(value, pltpu.VMEM) for value in (keep, other)
+    )
+    return pl.pallas_call(
+        finish_kernel,
+        in_specs=[whole()] * 2,
+        out_specs=whole(pl.ANY),
+        out_shape=pltpu.HBM(keep.shape, keep.dtype),
+        scratch_shapes=[
+            pltpu.VMEM(keep.shape, keep.dtype),
+            pltpu.SemaphoreType.DMA((4,)),
+        ],
+        compiler_params=pltpu.CompilerParams(vmem_limit_bytes=8 * 2**20),
+        cost_estimate=pl.CostEstimate(
+            flops=3 * 10**5, bytes_accessed=2 * 10**6, transcendentals=0
+        ),
+        name="finish",
+    )(keep, other)
+
+
 def settle_kernel(factor_ref, out_ref, strips_ref, sems):
     count = strips_ref.shape[0]
     loads = [
@@ -458,12 +508,11 @@
 
 
 def factor_kernel(
-    facts_ref, factor_ref, got_ref, out_ref, strips_ref, held_ref, sems
+    facts_ref, factor_ref, got_ref, spare_ref, out_ref, strips_ref, held_ref, diagonal_ref, sems
 ):
     slots = factor_ref.shape[0]
     count = 4 * slots
     spans = [slice(2 * WIDTH * slot, 2 * WIDTH * (slot + 1)) for slot in range(slots)]
-    spans.append(slice(2 * WIDTH * slots, got_ref.shape[3]))
     pieces = [
         pltpu.make_async_copy(
             got_ref.at[:, :, :, span], held_ref.at[:, :, :, span], sems.at[2 * count + n]
@@ -478,13 +527,13 @@
         pltpu.make_async_copy(strips_ref.at[n], out_ref.at[strip_of(n)], sems.at[count + n])
         for n in range(count)
     ]
+    diagonals = pltpu.make_async_copy(spare_ref, diagonal_ref, sems.at[9 * slots])
+    diagonals.start()
     for slot in range(slots):
 
         @pl.when(facts_ref[LIVE + slot] != 0)
         def _(slot=slot):
             pieces[slot].start()
-            if slot == 0:
-                pieces[slots].start()
             for n in range(4 * slot, 4 * (slot + 1)):
                 loads[n].start()
 
@@ -508,10 +557,7 @@
         r, c = grid_positions()
         if row % 2 == 0:
             return jnp.where(r <= c, value, value.T)
-        item = facts_ref[NAMED + slot]
-        block = item // 2
-        source = (block // 4 * 2 + row // 2) * 8 + block % 4 * 2 + item % 2
-        tile = held_ref[source // 4, source % 4, :, 4 * WIDTH :].astype(jnp.float32)
+        tile = diagonal_ref[2 * slot + row // 2].astype(jnp.float32)
         diagonal = jnp.concatenate([tile[0:1], tile[1:2]], axis=1)
         return jnp.where(r > c, value, jnp.where(r < c, value.T, diagonal))
 
@@ -523,14 +569,13 @@
                 1.0 - shampoo_beta
             ) * sub_block(slot, row, col)
 
+    diagonals.wait()
     for n in range(count):
 
         @pl.when(facts_ref[LIVE + n // 4] != 0)
         def _(n=n):
             if n % 4 == 0:
                 pieces[n // 4].wait()
-            if n == 0:
-                pieces[slots].wait()
             loads[n].wait()
             mix(n)
             stores[n].start()
@@ -539,17 +584,18 @@
         pl.when(facts_ref[LIVE + n // 4] != 0)(stores[n].wait)
 
 
-def update_factors(facts, factors, got):
+def update_factors(facts, factors, got, spare):
     slots, size, _ = factors.shape
     got = got.reshape(32, 4, SUB, got.shape[2])
     return pl.pallas_call(
         factor_kernel,
-        in_specs=[whole(pltpu.SMEM)] + [whole(pl.ANY)] * 2,
+        in_specs=[whole(pltpu.SMEM)] + [whole(pl.ANY)] * 3,
         out_specs=whole(pl.ANY),
         out_shape=pltpu.HBM(factors.shape, factors.dtype),
         scratch_shapes=[
             pltpu.VMEM((4 * slots, GB, size), jnp.float32),
             pltpu.VMEM(got.shape, got.dtype),
+            pltpu.VMEM(spare.shape, spare.dtype),
             pltpu.SemaphoreType.DMA((9 * slots + 1,)),
         ],
         input_output_aliases={1: 0},
@@ -558,7 +604,7 @@
             flops=4 * 10**6, bytes_accessed=2 * 10**7, transcendentals=0
         ),
         name="update_factors",
-    )(facts, pltpu.with_memory_space_constraint(factors, pltpu.HBM), got)
+    )(facts, pltpu.with_memory_space_constraint(factors, pltpu.HBM), got, spare)
 
 
 def shards(gradient, first_moment, second_moment, factors, eigen_bases, owners):
@@ -596,7 +642,7 @@
     kept_gram = kept_gram.reshape(CHIPS, SUB, WIDTH)
 
     second_parts = second_operand(
-        facts, first_got.reshape(devices * slots, SUB, size), kept_gram, other_gram
+        facts, first_got.reshape(devices * slots, SUB, size), kept_gram, other_gram, diagonal
     )
     same_core = [[2 * chip + core for chip in range(CHIPS)] for core in range(2)]
     mine = lax.all_to_all(
@@ -604,16 +650,16 @@
     )
     theirs = swap_neighbour(mine, "rep")
 
-    third_parts = third_operand(facts, mine, diagonal)
+    third_parts = third_operand(facts, mine)
     third_got = lax.all_to_all(third_parts, BOTH, 0, 0, tiled=True)
 
-    new_first, new_second, direction = rotate(
-        place, block, mine, theirs, first_moment, second_moment
+    new_first, new_second, direction, spare = rotate(
+        facts, block, mine, theirs, first_moment, second_moment
     )
     other = swap_neighbour(direction, "rep")
     keep, give = back(place, direction, other, mine, theirs)
-    update = keep + swap_neighbour(give, "fsdp").astype(jnp.float32)
-    new_factors = update_factors(facts, settled, third_got)
+    update = finish(keep, swap_neighbour(give, "fsdp"))
+    new_factors = update_factors(facts, settled, third_got, spare)
     return (update, new_first, new_second, new_factors)
 
 

time: 155 us -> 153 us (0.987)
  waiting for transfers between devices: 66.4 us -> 63.2 us
  blocking collectives: 32.4 us -> 34.6 us
    all_to_all x1, waiting for transfers between devices: 13.6 us -> 10.8 us  [shards(): third_got = lax.all_to_all(third_parts, BOTH, 0, 0, tiled=True)]
    all_to_all x1, blocking collectives: 32.4 us -> 34.6 us  [shards(): lax.all_to_all(second_parts, BOTH, 0, 0, axis_index_groups=same_core, til...]
  transfers between devices with their start and end apart: 9 -> 9, of which waited for: 7 -> 7; matrix products, arithmetic and copies ran while one was open for 0% -> 0% of each run, Pallas kernels for 16% -> 17%
where the time goes in v4:
time: 153 us; the launch traced here: 151 us
  waiting for transfers between devices  63.2 us (41%)
  blocking collectives  34.6 us (23%)
  Pallas kernels  27.9 us (18%)
  starting transfers between devices  23.5 us (15%)
    all_to_all x1, waiting for transfers between devices, shards(): first_got = lax.all_to_all(first_parts, BOTH, 0, 0, tiled=True)  44.6 us
    all_to_all x1, blocking collectives, shards(): lax.all_to_all(second_parts, BOTH, 0, 0, axis_index_groups=same_core, til...  34.6 us
    all_to_all x1, starting transfers between devices, shards(): first_got = lax.all_to_all(first_parts, BOTH, 0, 0, tiled=True)  11.1 us
    all_to_all x1, waiting for transfers between devices, shards(): third_got = lax.all_to_all(third_parts, BOTH, 0, 0, tiled=True)  10.8 us
    ppermute x7, waiting for transfers between devices, swap_neighbour(): return lax.ppermute(value, axis, pairs)  7.85 us
    ppermute x7, starting transfers between devices, swap_neighbour(): return lax.ppermute(value, axis, pairs)  7.66 us
    pallas_call x1, Pallas kernels, settle(): pl.pallas_call(settle_kernel, in_specs=[whole(pl.ANY)], out_specs=whole(p...  6.42 us
    pallas_call x1, Pallas kernels, rotate(): pl.pallas_call(rotate_kernel, in_specs=[whole(pltpu.SMEM)] + [whole(pl.AN...  5.83 us
  transfers between devices with their start and end apart: 9, of which 7 were waited for; matrix products, arithmetic and copies ran while one was open for 0% of the time, Pallas kernels for 17%

profile of v4, /device:TPU:1, one launch (start us, length us, event | category | flops | bytes accessed | tf_op | source)
XLA Modules:
  0.0 150.7 jit_solution(5523919611223141625)
XLA Ops:
  0.6 2.2 %collective-permute-start.1 = (bf16[512,512]{1,0:T(8,128)(2,1)}, bf16[512,512]{1,0:T(8,128)(2,1)S(1)}, u32[]{:S(2)}, u32[]{:S(2)}) collective-permute-start(bf16[512,512]{1,0:T(8,128)(2,1)} %own_ref.1), channel_id=1, source_target_pairs={{0,8},{8,0},{16,24},{24,16},{32,40},{40,32},{48,56},{56,48},{64,72... | collective-permute-start | bytes 1572872 | tf_op jit(solution)/shard_map/ppermute | solution.py:29
  2.8 3.3 %interleave.1 = bf16[128,2,8,1024]{3,2,1,0:T(8,128)(2,1)} custom-call(bf16[2,128,8,1024]{3,2,1,0:T(8,128)(2,1)} %bitcast.10), custom_call_target="tpu_custom_call" | custom-call | bytes 8000000 | tf_op jit(solution)/shard_map/interleave/pallas_call | solution.py:72
  6.2 11.1 %all-to-all-start = ((bf16[128,2,8,1024]{3,2,1,0:T(8,128)(2,1)}), bf16[128,2,8,1024]{3,2,1,0:T(8,128)(2,1)}, u32[]{:S(2)}, u32[]{:S(2)}) async-start(bf16[128,2,8,1024]{3,2,1,0:T(8,128)(2,1)} %interleave.1), calls=%async_computation | async-start | bytes 8388608 | tf_op jit(solution)/shard_map/all_to_all | solution.py:623
  17.3 1.2 collective-permute-start
  18.9 1.2 collective-permute-done.side_ref
  20.1 0.7 collective-permute-done.2.cross_ref
  20.8 3.0 %gram_pieces.1 = (bf16[32,2,8,256]{3,2,1,0:T(8,128)(2,1)S(1)}, bf16[32,2,8,256]{3,2,1,0:T(8,128)(2,1)S(1)}, bf16[8,128]{1,0:T(8,128)(2,1)S(1)}, bf16[1024,1024]{1,0:T(8,128)(2,1)}) custom-call(s32[2]{0:T(128)S(1)} %pad_add_fusion.place_ref, bf16[512,512]{1,0:T(8,128)(2,1)S(1)} %copy-done.1, bf16[512,512]{1,0:T(8,128)(2,1)S(1)} %collective-permute-done.side_ref, ...), custom_call_target="tpu_custom_call" | custom-call | flops 32000000000 | bytes 3000000 | tf_op jit(solution)/shard_map/gram_pieces/pallas_call | solution.py:144
  24.4 0.9 collective-permute-done.3.other_ref
  25.3 44.6 %all-to-all-done = bf16[128,2,8,1024]{3,2,1,0:T(8,128)(2,1)} async-done(((bf16[128,2,8,1024]{3,2,1,0:T(8,128)(2,1)}), bf16[128,2,8,1024]{3,2,1,0:T(8,128)(2,1)}, u32[]{:S(2)}, u32[]{:S(2)}) %all-to-all-start) | async-done | bytes 4194336 | tf_op jit(solution)/shard_map/all_to_all | solution.py:623
  69.9 1.8 %second_operand.1 = bf16[64,8,2176]{2,1,0:T(8,128)(2,1)S(1)} custom-call(s32[71]{0:T(128)S(1)} %concatenate.4.facts_ref, bf16[256,8,1024]{2,1,0:T(8,128)(2,1)} %bitcast.4.rows_ref, bf16[64,8,256]{2,1,0:T(8,128)(2,1)S(1)} %bitcast.8, bf16[64,8,256]{2,1,0:T(8,128)(2,1)S(1)} %collective-permute-done.3.other_ref, bf16[8,128]{1,0:T(8,128)(2,1)S(1)} %get-tuple-element.17.diagonal_ref), custom_call_target="tpu_custom_call" | custom-call | bytes 8000000 | tf_op jit(solution)/shard_map/second_operand/pallas_call | solution.py:213
  71.8 34.6 %all_to_all.15.mine_ref.got_ref = bf16[64,8,2176]{2,1,0:T(8,128)(2,1)S(1)} all-to-all(bf16[64,8,2176]{2,1,0:T(8,128)(2,1)S(1)} %second_operand.1), channel_id=1, replica_groups={{0,2,4,6,8,10,12,14,16,18,20,22,24,26,28,30,32,34,36,38,40,42,44,46,48,..., dimensions={0} | all-to-all | bytes 4456448 | tf_op jit(solution)/shard_map/all_to_all | solution.py:648
  106.3 2.0 %collective-permute-start.4 = (bf16[64,8,2176]{2,1,0:T(8,128)(2,1)S(1)}, bf16[64,8,2176]{2,1,0:T(8,128)(2,1)}, u32[]{:S(2)}, u32[]{:S(2)}) collective-permute-start(bf16[64,8,2176]{2,1,0:T(8,128)(2,1)S(1)} %all_to_all.15.mine_ref.got_ref), channel_id=1, source_target_pairs={{0,1},{1,0},{2,3},{3,2},{4,5},{5,4},{6,7},{7,6},{8,9},{9,8},{10,11... | collective-permute-start | bytes 6684680 | tf_op jit(solution)/shard_map/ppermute | solution.py:29
  108.4 1.8 %third_operand.1 = bf16[128,8,1024]{2,1,0:T(8,128)(2,1)} custom-call(s32[71]{0:T(128)S(1)} %concatenate.4.facts_ref, bf16[64,8,2176]{2,1,0:T(8,128)(2,1)S(1)} %all_to_all.15.mine_ref.got_ref), custom_call_target="tpu_custom_call" | custom-call | bytes 4000000 | tf_op jit(solution)/shard_map/third_operand/pallas_call | solution.py:248
  110.2 4.7 %all-to-all-start.2 = ((bf16[128,8,1024]{2,1,0:T(8,128)(2,1)}), bf16[128,8,1024]{2,1,0:T(8,128)(2,1)}, u32[]{:S(2)}, u32[]{:S(2)}) async-start(bf16[128,8,1024]{2,1,0:T(8,128)(2,1)} %third_operand.1), calls=%async_computation.2 | async-start | bytes 4194304 | tf_op jit(solution)/shard_map/all_to_all | solution.py:654
  114.9 5.8 %rotate.1 = (f32[512,512]{1,0:T(8,128)}, f32[512,512]{1,0:T(8,128)}, bf16[512,512]{1,0:T(8,128)(2,1)S(1)}, bf16[4,8,128]{2,1,0:T(8,128)(2,1)}) custom-call(s32[71]{0:T(128)S(1)} %concatenate.4.facts_ref, bf16[1024,1024]{1,0:T(8,128)(2,1)} %get-tuple-element.14.block_ref, bf16[64,8,2176]{2,1,0:T(8,128)(2,1)S(1)} %all_to_all.15.mine_ref.got_ref, ...), custom_call_target="tpu_custom_call" | custom-call | flops 1600000000 | bytes 10000000 | tf_op jit(solution)/shard_map/rotate/pallas_call | solution.py:340
  120.8 1.1 collective-permute-start.5
  121.9 1.5 %collective-permute-done.5.side_ref = bf16[512,512]{1,0:T(8,128)(2,1)S(1)} collective-permute-done((bf16[512,512]{1,0:T(8,128)(2,1)S(1)}, bf16[512,512]{1,0:T(8,128)(2,1)S(1)}, u32[]{:S(2)}, u32[]{:S(2)}) %collective-permute-start.5) | collective-permute-done | bytes 524320 | tf_op jit(solution)/shard_map/ppermute | solution.py:29
  123.4 3.7 %back.1 = (f32[512,512]{1,0:T(8,128)S(1)}, bf16[512,512]{1,0:T(8,128)(2,1)}) custom-call(s32[2]{0:T(128)S(1)} %pad_add_fusion.place_ref, bf16[512,512]{1,0:T(8,128)(2,1)S(1)} %get-tuple-element.18.own_ref, bf16[512,512]{1,0:T(8,128)(2,1)S(1)} %collective-permute-done.5.side_ref, bf16[64,8,2176]{2,1,0:T(8,128)(2,1)S(1)} %all_to_all.15.mine_ref.got_ref, ...), custom_call_target="tpu_custom_call" | custom-call | flops 1100000000 | bytes 6000000 | tf_op jit(solution)/shard_map/back/pallas_call | solution.py:412
  127.2 0.6 collective-permute-start.6
  127.8 6.4 %settle.1.factor_ref = f32[2,1024,1024]{2,1,0:T(8,128)} custom-call(f32[2,1024,1024]{2,1,0:T(8,128)} %factor_ref.1), custom_call_target="tpu_custom_call" | custom-call | bytes 16000000 | tf_op jit(solution)/shard_map/settle/pallas_call | solution.py:489
  134.2 10.8 %all-to-all-done.2 = bf16[128,8,1024]{2,1,0:T(8,128)(2,1)} async-done(((bf16[128,8,1024]{2,1,0:T(8,128)(2,1)}), bf16[128,8,1024]{2,1,0:T(8,128)(2,1)}, u32[]{:S(2)}, u32[]{:S(2)}) %all-to-all-start.2) | async-done | bytes 2097184 | tf_op jit(solution)/shard_map/all_to_all | solution.py:654
  145.0 1.0 update_factors.1
  146.0 3.5 %collective-permute-done.6.other_ref = bf16[512,512]{1,0:T(8,128)(2,1)S(1)} collective-permute-done((bf16[512,512]{1,0:T(8,128)(2,1)}, bf16[512,512]{1,0:T(8,128)(2,1)S(1)}, u32[]{:S(2)}, u32[]{:S(2)}) %collective-permute-start.6) | collective-permute-done | bytes 524320 | tf_op jit(solution)/shard_map/ppermute | solution.py:29
  149.5 1.0 finish.1
  (16 shorter events, 1.0 us)
Async XLA Ops:
  0.6 17.9 %collective-permute-start.1 = (bf16[512,512]{1,0:T(8,128)(2,1)}, bf16[512,512]{1,0:T(8,128)(2,1)S(1)}, u32[]{:S(2)}, u32[]{:S(2)}) collective-permute-start(bf16[512,512]{1,0:T(8,128)(2,1)} %own_ref.1), channel_id=1, source_target_pairs={{0,8},{8,0},{16,24},{24,16},{32,40},{40,32},{48,56},{56,48},{64,72... | collective-permute-start | bytes 1572872 | tf_op jit(solution)/shard_map/ppermute | solution.py:29
  6.1 11.2 %copy-start.1 = (bf16[512,512]{1,0:T(8,128)(2,1)S(1)}, bf16[512,512]{1,0:T(8,128)(2,1)}, u32[]{:S(2)}) copy-start(bf16[512,512]{1,0:T(8,128)(2,1)} %own_ref.1) | copy-start | bytes 1572868
  6.2 12.6 %copy-start.2 = (s32[64]{0:T(128)S(1)}, s32[64]{0:T(128)}, u32[]{:S(2)}) copy-start(s32[64]{0:T(128)} %param.11) | copy-start | bytes 772
  6.2 63.8 %all-to-all-start = ((bf16[128,2,8,1024]{3,2,1,0:T(8,128)(2,1)}), bf16[128,2,8,1024]{3,2,1,0:T(8,128)(2,1)}, u32[]{:S(2)}, u32[]{:S(2)}) async-start(bf16[128,2,8,1024]{3,2,1,0:T(8,128)(2,1)} %interleave.1), calls=%async_computation | async-start | bytes 8388608 | tf_op jit(solution)/shard_map/all_to_all | solution.py:623
  17.3 2.8 %collective-permute-start = (bf16[512,512]{1,0:T(8,128)(2,1)S(1)}, bf16[512,512]{1,0:T(8,128)(2,1)S(1)}, u32[]{:S(2)}, u32[]{:S(2)}) collective-permute-start(bf16[512,512]{1,0:T(8,128)(2,1)S(1)} %copy-done.1), channel_id=1, source_target_pairs={{0,1},{1,0},{2,3},{3,2},{4,5},{5,4},{6,7},{7,6},{8,9},{9,8},{10,11... | collective-permute-start | bytes 1572872 | tf_op jit(solution)/shard_map/ppermute | solution.py:29
  18.5 2.3 %collective-permute-start.2 = (bf16[512,512]{1,0:T(8,128)(2,1)S(1)}, bf16[512,512]{1,0:T(8,128)(2,1)S(1)}, u32[]{:S(2)}, u32[]{:S(2)}) collective-permute-start(bf16[512,512]{1,0:T(8,128)(2,1)S(1)} %collective-permute-done.1.below_ref), channel_id=1, source_target_pairs={{0,1},{1,0},{2,3},{3,2},{4,5},{5,4},{6,7},{7,6},{8,9},{9,8},{10,11... | collective-permute-start | bytes 1572872 | tf_op jit(solution)/shard_map/ppermute | solution.py:29
  23.8 1.5 %collective-permute-start.3 = (bf16[64,8,256]{2,1,0:T(8,128)(2,1)S(1)}, bf16[64,8,256]{2,1,0:T(8,128)(2,1)S(1)}, u32[]{:S(2)}, u32[]{:S(2)}) collective-permute-start(bf16[64,8,256]{2,1,0:T(8,128)(2,1)S(1)} %bitcast.9), channel_id=1, source_target_pairs={{0,1},{1,0},{2,3},{3,2},{4,5},{5,4},{6,7},{7,6},{8,9},{9,8},{10,11... | collective-permute-start | bytes 786440 | tf_op jit(solution)/shard_map/ppermute | solution.py:29
  106.3 8.6 %collective-permute-start.4 = (bf16[64,8,2176]{2,1,0:T(8,128)(2,1)S(1)}, bf16[64,8,2176]{2,1,0:T(8,128)(2,1)}, u32[]{:S(2)}, u32[]{:S(2)}) collective-permute-start(bf16[64,8,2176]{2,1,0:T(8,128)(2,1)S(1)} %all_to_all.15.mine_ref.got_ref), channel_id=1, source_target_pairs={{0,1},{1,0},{2,3},{3,2},{4,5},{5,4},{6,7},{7,6},{8,9},{9,8},{10,11... | collective-permute-start | bytes 6684680 | tf_op jit(solution)/shard_map/ppermute | solution.py:29
  110.2 34.8 %all-to-all-start.2 = ((bf16[128,8,1024]{2,1,0:T(8,128)(2,1)}), bf16[128,8,1024]{2,1,0:T(8,128)(2,1)}, u32[]{:S(2)}, u32[]{:S(2)}) async-start(bf16[128,8,1024]{2,1,0:T(8,128)(2,1)} %third_operand.1), calls=%async_computation.2 | async-start | bytes 4194304 | tf_op jit(solution)/shard_map/all_to_all | solution.py:654
  120.8 2.7 %collective-permute-start.5 = (bf16[512,512]{1,0:T(8,128)(2,1)S(1)}, bf16[512,512]{1,0:T(8,128)(2,1)S(1)}, u32[]{:S(2)}, u32[]{:S(2)}) collective-permute-start(bf16[512,512]{1,0:T(8,128)(2,1)S(1)} %get-tuple-element.18.own_ref), channel_id=1, source_target_pairs={{0,1},{1,0},{2,3},{3,2},{4,5},{5,4},{6,7},{7,6},{8,9},{9,8},{10,11... | collective-permute-start | bytes 1572872 | tf_op jit(solution)/shard_map/ppermute | solution.py:29
  127.2 17.8 %copy-start = (bf16[4,8,128]{2,1,0:T(8,128)(2,1)S(1)}, bf16[4,8,128]{2,1,0:T(8,128)(2,1)}, u32[]{:S(2)}) copy-start(bf16[4,8,128]{2,1,0:T(8,128)(2,1)} %get-tuple-element.23.spare_ref) | copy-start | bytes 24580
  127.2 22.3 %collective-permute-start.6 = (bf16[512,512]{1,0:T(8,128)(2,1)}, bf16[512,512]{1,0:T(8,128)(2,1)S(1)}, u32[]{:S(2)}, u32[]{:S(2)}) collective-permute-start(bf16[512,512]{1,0:T(8,128)(2,1)} %get-tuple-element.20), channel_id=1, source_target_pairs={{0,8},{8,0},{16,24},{24,16},{32,40},{40,32},{48,56},{56,48},{64,72... | collective-permute-start | bytes 1572872 | tf_op jit(solution)/shard_map/ppermute | solution.py:29

commit v5 on v4

--- a/solution.py
+++ b/solution.py
@@ -17,6 +17,7 @@
 ABOVE = (((0, 1), (0, 2), (0, 3)), ((1, 2), (1, 3), (2, 3)))
 WIDTH = 2 * 128
 CHIPS = 64
+READY = 1
 ROW, COL, MINE, LIVE, NAMED = 64, 65, 66, 67, 69
 BASES = 512 + 1024
 SPARE = BASES + 2 * WIDTH
@@ -465,7 +466,7 @@
     )(keep, other)
 
 
-def settle_kernel(factor_ref, out_ref, strips_ref, sems):
+def settle_kernel(factor_ref, out_ref, ready_ref, strips_ref, sems):
     count = strips_ref.shape[0]
     loads = [
         pltpu.make_async_copy(factor_ref.at[strip_of(n)], strips_ref.at[n], sems.at[0, n])
@@ -477,9 +478,11 @@
     ]
     for load in loads:
         load.start()
-    for load, store in zip(loads, stores):
-        load.wait()
-        store.start()
+    for n in range(count):
+        loads[n].wait()
+        stores[n].start()
+        if n < READY:
+            ready_ref[n] = shampoo_beta * strips_ref[n]
     for store in stores:
         store.wait()
 
@@ -489,8 +492,11 @@
     return pl.pallas_call(
         settle_kernel,
         in_specs=[whole(pl.ANY)],
-        out_specs=whole(pl.ANY),
-        out_shape=pltpu.HBM(factors.shape, factors.dtype),
+        out_specs=[whole(pl.ANY), whole()],
+        out_shape=[
+            pltpu.HBM(factors.shape, factors.dtype),
+            pltpu.VMEM((READY, GB, size), factors.dtype),
+        ],
         scratch_shapes=[
             pltpu.VMEM((4 * slots, GB, size), jnp.float32),
             pltpu.SemaphoreType.DMA((2, 4 * slots)),
@@ -508,7 +514,16 @@
 
 
 def factor_kernel(
-    facts_ref, factor_ref, got_ref, spare_ref, out_ref, strips_ref, held_ref, diagonal_ref, sems
+    facts_ref,
+    ready_ref,
+    factor_ref,
+    got_ref,
+    spare_ref,
+    out_ref,
+    strips_ref,
+    held_ref,
+    diagonal_ref,
+    sems,
 ):
     slots = factor_ref.shape[0]
     count = 4 * slots
@@ -519,10 +534,10 @@
         )
         for n, span in enumerate(spans)
     ]
-    loads = [
-        pltpu.make_async_copy(out_ref.at[strip_of(n)], strips_ref.at[n], sems.at[n])
-        for n in range(count)
-    ]
+    loads = {
+        n: pltpu.make_async_copy(out_ref.at[strip_of(n)], strips_ref.at[n], sems.at[n])
+        for n in range(READY, count)
+    }
     stores = [
         pltpu.make_async_copy(strips_ref.at[n], out_ref.at[strip_of(n)], sems.at[count + n])
         for n in range(count)
@@ -534,7 +549,7 @@
         @pl.when(facts_ref[LIVE + slot] != 0)
         def _(slot=slot):
             pieces[slot].start()
-            for n in range(4 * slot, 4 * (slot + 1)):
+            for n in range(max(READY, 4 * slot), 4 * (slot + 1)):
                 loads[n].start()
 
     def piece(slot, which, n):
@@ -565,9 +580,11 @@
         slot, row = n // 4, n % 4
         for col in range(4):
             span = slice(col * GB, (col + 1) * GB)
-            strips_ref[n, :, span] = shampoo_beta * strips_ref[n, :, span] + (
-                1.0 - shampoo_beta
-            ) * sub_block(slot, row, col)
+            if n < READY:
+                decayed = ready_ref[n, :, span]
+            else:
+                decayed = shampoo_beta * strips_ref[n, :, span]
+            strips_ref[n, :, span] = decayed + (1.0 - shampoo_beta) * sub_block(slot, row, col)
 
     diagonals.wait()
     for n in range(count):
@@ -576,7 +593,8 @@
         def _(n=n):
             if n % 4 == 0:
                 pieces[n // 4].wait()
-            loads[n].wait()
+            if n >= READY:
+                loads[n].wait()
             mix(n)
             stores[n].start()
 
@@ -584,12 +602,12 @@
         pl.when(facts_ref[LIVE + n // 4] != 0)(stores[n].wait)
 
 
-def update_factors(facts, factors, got, spare):
+def update_factors(facts, ready, factors, got, spare):
     slots, size, _ = factors.shape
     got = got.reshape(32, 4, SUB, got.shape[2])
     return pl.pallas_call(
         factor_kernel,
-        in_specs=[whole(pltpu.SMEM)] + [whole(pl.ANY)] * 3,
+        in_specs=[whole(pltpu.SMEM), whole()] + [whole(pl.ANY)] * 3,
         out_specs=whole(pl.ANY),
         out_shape=pltpu.HBM(factors.shape, factors.dtype),
         scratch_shapes=[
@@ -598,13 +616,19 @@
             pltpu.VMEM(spare.shape, spare.dtype),
             pltpu.SemaphoreType.DMA((9 * slots + 1,)),
         ],
-        input_output_aliases={1: 0},
+        input_output_aliases={2: 0},
         compiler_params=pltpu.CompilerParams(vmem_limit_bytes=20 * 2**20),
         cost_estimate=pl.CostEstimate(
             flops=4 * 10**6, bytes_accessed=2 * 10**7, transcendentals=0
         ),
         name="update_factors",
-    )(facts, pltpu.with_memory_space_constraint(factors, pltpu.HBM), got, spare)
+    )(
+        facts,
+        pltpu.with_memory_space_constraint(ready, pltpu.VMEM),
+        pltpu.with_memory_space_constraint(factors, pltpu.HBM),
+        got,
+        spare,
+    )
 
 
 def shards(gradient, first_moment, second_moment, factors, eigen_bases, owners):
@@ -636,7 +660,7 @@
     side = swap_neighbour(gradient, "rep")
     cross = swap_neighbour(below, "rep")
     quads = (gradient, side, below, cross)
-    settled = settle(factors)
+    settled, ready = settle(factors)
     kept_gram, given_gram, diagonal, block = gram_pieces(place, quads)
     other_gram = swap_neighbour(given_gram.reshape(CHIPS, SUB, WIDTH), "rep")
     kept_gram = kept_gram.reshape(CHIPS, SUB, WIDTH)
@@ -659,7 +683,7 @@
     other = swap_neighbour(direction, "rep")
     keep, give = back(place, direction, other, mine, theirs)
     update = finish(keep, swap_neighbour(give, "fsdp"))
-    new_factors = update_factors(facts, settled, third_got, spare)
+    new_factors = update_factors(facts, ready, settled, third_got, spare)
     return (update, new_first, new_second, new_factors)
 
 

time: 153 us -> 151 us (0.987); the launches traced: 151 us -> 151 us
  Pallas kernels: 27.9 us -> 31.1 us
  waiting for transfers between devices: 63.2 us -> 60 us
    pallas_call x2, Pallas kernels: 7.43 us -> 10.6 us  [the longest x1 6.42 us: settle(): pl.pallas_call(settle_kernel, in_specs=[whole(pl.ANY)], out_specs=[whole(...]
    ppermute x7, waiting for transfers between devices: 7.85 us -> 4.65 us  [swap_neighbour(): return lax.ppermute(value, axis, pairs)]
  transfers between devices with their start and end apart: 9 -> 9, of which waited for: 7 -> 7; matrix products, arithmetic and copies ran while one was open for 0% -> 0% of each run, Pallas kernels for 17% -> 19%
where the time goes in v5:
time: 151 us
  waiting for transfers between devices  60 us (40%)
  blocking collectives  34.6 us (23%)
  Pallas kernels  31.1 us (21%)
  starting transfers between devices  23.5 us (16%)
    all_to_all x1, waiting for transfers between devices, shards(): first_got = lax.all_to_all(first_parts, BOTH, 0, 0, tiled=True)  44.6 us
    all_to_all x1, blocking collectives, shards(): lax.all_to_all(second_parts, BOTH, 0, 0, axis_index_groups=same_core, til...  34.6 us
    all_to_all x1, starting transfers between devices, shards(): first_got = lax.all_to_all(first_parts, BOTH, 0, 0, tiled=True)  11.1 us
    all_to_all x1, waiting for transfers between devices, shards(): third_got = lax.all_to_all(third_parts, BOTH, 0, 0, tiled=True)  10.7 us
    ppermute x7, starting transfers between devices, swap_neighbour(): return lax.ppermute(value, axis, pairs)  7.68 us
    pallas_call x1, Pallas kernels, settle(): pl.pallas_call(settle_kernel, in_specs=[whole(pl.ANY)], out_specs=[whole(...  6.42 us
    pallas_call x1, Pallas kernels, rotate(): pl.pallas_call(rotate_kernel, in_specs=[whole(pltpu.SMEM)] + [whole(pl.AN...  5.84 us
    all_to_all x1, starting transfers between devices, shards(): third_got = lax.all_to_all(third_parts, BOTH, 0, 0, tiled=True)  4.73 us
  transfers between devices with their start and end apart: 9, of which 7 were waited for; matrix products, arithmetic and copies ran while one was open for 0% of the time, Pallas kernels for 19%

profile of v5, /device:TPU:1, one launch (start us, length us, event | category | flops | bytes accessed | tf_op | source)
XLA Modules:
  0.0 150.7 jit_solution(11105317415011671626)
XLA Ops:
  0.6 2.2 %collective-permute-start.1 = (bf16[512,512]{1,0:T(8,128)(2,1)}, bf16[512,512]{1,0:T(8,128)(2,1)S(1)}, u32[]{:S(2)}, u32[]{:S(2)}) collective-permute-start(bf16[512,512]{1,0:T(8,128)(2,1)} %own_ref.1), channel_id=1, source_target_pairs={{0,8},{8,0},{16,24},{24,16},{32,40},{40,32},{48,56},{56,48},{64,72... | collective-permute-start | bytes 1572872 | tf_op jit(solution)/shard_map/ppermute | solution.py:30
  2.8 3.3 %interleave.1 = bf16[128,2,8,1024]{3,2,1,0:T(8,128)(2,1)} custom-call(bf16[2,128,8,1024]{3,2,1,0:T(8,128)(2,1)} %bitcast.10), custom_call_target="tpu_custom_call" | custom-call | bytes 8000000 | tf_op jit(solution)/shard_map/interleave/pallas_call | solution.py:73
  6.2 11.1 %all-to-all-start = ((bf16[128,2,8,1024]{3,2,1,0:T(8,128)(2,1)}), bf16[128,2,8,1024]{3,2,1,0:T(8,128)(2,1)}, u32[]{:S(2)}, u32[]{:S(2)}) async-start(bf16[128,2,8,1024]{3,2,1,0:T(8,128)(2,1)} %interleave.1), calls=%async_computation | async-start | bytes 8388608 | tf_op jit(solution)/shard_map/all_to_all | solution.py:647
  17.3 1.2 collective-permute-start
  18.9 1.2 collective-permute-done.side_ref
  20.1 0.7 collective-permute-done.2.cross_ref
  20.8 3.0 %gram_pieces.1 = (bf16[32,2,8,256]{3,2,1,0:T(8,128)(2,1)S(1)}, bf16[32,2,8,256]{3,2,1,0:T(8,128)(2,1)S(1)}, bf16[8,128]{1,0:T(8,128)(2,1)S(1)}, bf16[1024,1024]{1,0:T(8,128)(2,1)}) custom-call(s32[2]{0:T(128)S(1)} %pad_add_fusion.place_ref, bf16[512,512]{1,0:T(8,128)(2,1)S(1)} %copy-done.1, bf16[512,512]{1,0:T(8,128)(2,1)S(1)} %collective-permute-done.side_ref, ...), custom_call_target="tpu_custom_call" | custom-call | flops 32000000000 | bytes 3000000 | tf_op jit(solution)/shard_map/gram_pieces/pallas_call | solution.py:145
  23.8 0.3 collective-permute-start.3
  24.4 0.9 collective-permute-done.3.other_ref
  25.3 44.6 %all-to-all-done = bf16[128,2,8,1024]{3,2,1,0:T(8,128)(2,1)} async-done(((bf16[128,2,8,1024]{3,2,1,0:T(8,128)(2,1)}), bf16[128,2,8,1024]{3,2,1,0:T(8,128)(2,1)}, u32[]{:S(2)}, u32[]{:S(2)}) %all-to-all-start) | async-done | bytes 4194336 | tf_op jit(solution)/shard_map/all_to_all | solution.py:647
  69.9 1.8 %second_operand.1 = bf16[64,8,2176]{2,1,0:T(8,128)(2,1)S(1)} custom-call(s32[71]{0:T(128)S(1)} %concatenate.4.facts_ref, bf16[256,8,1024]{2,1,0:T(8,128)(2,1)} %bitcast.4.rows_ref, bf16[64,8,256]{2,1,0:T(8,128)(2,1)S(1)} %bitcast.8, bf16[64,8,256]{2,1,0:T(8,128)(2,1)S(1)} %collective-permute-done.3.other_ref, bf16[8,128]{1,0:T(8,128)(2,1)S(1)} %get-tuple-element.19.diagonal_ref), custom_call_target="tpu_custom_call" | custom-call | bytes 8000000 | tf_op jit(solution)/shard_map/second_operand/pallas_call | solution.py:214
  71.8 34.6 %all_to_all.15.mine_ref.got_ref = bf16[64,8,2176]{2,1,0:T(8,128)(2,1)S(1)} all-to-all(bf16[64,8,2176]{2,1,0:T(8,128)(2,1)S(1)} %second_operand.1), channel_id=1, replica_groups={{0,2,4,6,8,10,12,14,16,18,20,22,24,26,28,30,32,34,36,38,40,42,44,46,48,..., dimensions={0} | all-to-all | bytes 4456448 | tf_op jit(solution)/shard_map/all_to_all | solution.py:672
  106.3 2.0 %collective-permute-start.4 = (bf16[64,8,2176]{2,1,0:T(8,128)(2,1)S(1)}, bf16[64,8,2176]{2,1,0:T(8,128)(2,1)}, u32[]{:S(2)}, u32[]{:S(2)}) collective-permute-start(bf16[64,8,2176]{2,1,0:T(8,128)(2,1)S(1)} %all_to_all.15.mine_ref.got_ref), channel_id=1, source_target_pairs={{0,1},{1,0},{2,3},{3,2},{4,5},{5,4},{6,7},{7,6},{8,9},{9,8},{10,11... | collective-permute-start | bytes 6684680 | tf_op jit(solution)/shard_map/ppermute | solution.py:30
  108.4 1.8 %third_operand.1 = bf16[128,8,1024]{2,1,0:T(8,128)(2,1)} custom-call(s32[71]{0:T(128)S(1)} %concatenate.4.facts_ref, bf16[64,8,2176]{2,1,0:T(8,128)(2,1)S(1)} %all_to_all.15.mine_ref.got_ref), custom_call_target="tpu_custom_call" | custom-call | bytes 4000000 | tf_op jit(solution)/shard_map/third_operand/pallas_call | solution.py:249
  110.2 4.7 %all-to-all-start.2 = ((bf16[128,8,1024]{2,1,0:T(8,128)(2,1)}), bf16[128,8,1024]{2,1,0:T(8,128)(2,1)}, u32[]{:S(2)}, u32[]{:S(2)}) async-start(bf16[128,8,1024]{2,1,0:T(8,128)(2,1)} %third_operand.1), calls=%async_computation.2 | async-start | bytes 4194304 | tf_op jit(solution)/shard_map/all_to_all | solution.py:678
  114.9 5.8 %rotate.1 = (f32[512,512]{1,0:T(8,128)}, f32[512,512]{1,0:T(8,128)}, bf16[512,512]{1,0:T(8,128)(2,1)S(1)}, bf16[4,8,128]{2,1,0:T(8,128)(2,1)}) custom-call(s32[71]{0:T(128)S(1)} %concatenate.4.facts_ref, bf16[1024,1024]{1,0:T(8,128)(2,1)} %get-tuple-element.16.block_ref, bf16[64,8,2176]{2,1,0:T(8,128)(2,1)S(1)} %all_to_all.15.mine_ref.got_ref, ...), custom_call_target="tpu_custom_call" | custom-call | flops 1600000000 | bytes 10000000 | tf_op jit(solution)/shard_map/rotate/pallas_call | solution.py:341
  120.8 1.2 collective-permute-start.5
  121.9 1.5 %collective-permute-done.5.side_ref = bf16[512,512]{1,0:T(8,128)(2,1)S(1)} collective-permute-done((bf16[512,512]{1,0:T(8,128)(2,1)S(1)}, bf16[512,512]{1,0:T(8,128)(2,1)S(1)}, u32[]{:S(2)}, u32[]{:S(2)}) %collective-permute-start.5) | collective-permute-done | bytes 524320 | tf_op jit(solution)/shard_map/ppermute | solution.py:30
  123.5 3.7 %back.1 = (f32[512,512]{1,0:T(8,128)S(1)}, bf16[512,512]{1,0:T(8,128)(2,1)}) custom-call(s32[2]{0:T(128)S(1)} %pad_add_fusion.place_ref, bf16[512,512]{1,0:T(8,128)(2,1)S(1)} %get-tuple-element.20.own_ref, bf16[512,512]{1,0:T(8,128)(2,1)S(1)} %collective-permute-done.5.side_ref, bf16[64,8,2176]{2,1,0:T(8,128)(2,1)S(1)} %all_to_all.15.mine_ref.got_ref, ...), custom_call_target="tpu_custom_call" | custom-call | flops 1100000000 | bytes 6000000 | tf_op jit(solution)/shard_map/back/pallas_call | solution.py:413
  127.2 0.6 collective-permute-start.6
  127.8 6.4 %settle.1 = (f32[2,1024,1024]{2,1,0:T(8,128)}, f32[1,256,1024]{2,1,0:T(8,128)S(1)}) custom-call(f32[2,1024,1024]{2,1,0:T(8,128)} %factor_ref.1), custom_call_target="tpu_custom_call" | custom-call | bytes 16000000 | tf_op jit(solution)/shard_map/settle/pallas_call | solution.py:492
  134.3 10.7 %all-to-all-done.2 = bf16[128,8,1024]{2,1,0:T(8,128)(2,1)} async-done(((bf16[128,8,1024]{2,1,0:T(8,128)(2,1)}), bf16[128,8,1024]{2,1,0:T(8,128)(2,1)}, u32[]{:S(2)}, u32[]{:S(2)}) %all-to-all-start.2) | async-done | bytes 2097184 | tf_op jit(solution)/shard_map/all_to_all | solution.py:678
  145.0 4.2 %update_factors.1 = f32[2,1024,1024]{2,1,0:T(8,128)} custom-call(s32[71]{0:T(128)S(1)} %concatenate.4.facts_ref, f32[1,256,1024]{2,1,0:T(8,128)S(1)} %get-tuple-element.25.ready_ref, f32[2,1024,1024]{2,1,0:T(8,128)} %get-tuple-element.26.factor_ref, bf16[32,4,8,1024]{3,2,1,0:T(8,128)(2,1)} %bitcast.7.got_ref, ...), custom_call_target="tpu_custom_call", output_to_operand_aliasing={{}: (2, {})} | custom-call | flops 4000000 | bytes 20000000 | tf_op jit(solution)/shard_map/update_factors/pallas_call | solution.py:608
  149.5 1.0 finish.1
  (16 shorter events, 0.9 us)
Async XLA Ops:
  0.6 17.9 %collective-permute-start.1 = (bf16[512,512]{1,0:T(8,128)(2,1)}, bf16[512,512]{1,0:T(8,128)(2,1)S(1)}, u32[]{:S(2)}, u32[]{:S(2)}) collective-permute-start(bf16[512,512]{1,0:T(8,128)(2,1)} %own_ref.1), channel_id=1, source_target_pairs={{0,8},{8,0},{16,24},{24,16},{32,40},{40,32},{48,56},{56,48},{64,72... | collective-permute-start | bytes 1572872 | tf_op jit(solution)/shard_map/ppermute | solution.py:30
  6.1 11.2 %copy-start.1 = (bf16[512,512]{1,0:T(8,128)(2,1)S(1)}, bf16[512,512]{1,0:T(8,128)(2,1)}, u32[]{:S(2)}) copy-start(bf16[512,512]{1,0:T(8,128)(2,1)} %own_ref.1) | copy-start | bytes 1572868
  6.2 12.6 %copy-start.2 = (s32[64]{0:T(128)S(1)}, s32[64]{0:T(128)}, u32[]{:S(2)}) copy-start(s32[64]{0:T(128)} %param.11) | copy-start | bytes 772
  6.2 63.8 %all-to-all-start = ((bf16[128,2,8,1024]{3,2,1,0:T(8,128)(2,1)}), bf16[128,2,8,1024]{3,2,1,0:T(8,128)(2,1)}, u32[]{:S(2)}, u32[]{:S(2)}) async-start(bf16[128,2,8,1024]{3,2,1,0:T(8,128)(2,1)} %interleave.1), calls=%async_computation | async-start | bytes 8388608 | tf_op jit(solution)/shard_map/all_to_all | solution.py:647
  17.3 2.8 %collective-permute-start = (bf16[512,512]{1,0:T(8,128)(2,1)S(1)}, bf16[512,512]{1,0:T(8,128)(2,1)S(1)}, u32[]{:S(2)}, u32[]{:S(2)}) collective-permute-start(bf16[512,512]{1,0:T(8,128)(2,1)S(1)} %copy-done.1), channel_id=1, source_target_pairs={{0,1},{1,0},{2,3},{3,2},{4,5},{5,4},{6,7},{7,6},{8,9},{9,8},{10,11... | collective-permute-start | bytes 1572872 | tf_op jit(solution)/shard_map/ppermute | solution.py:30
  18.5 2.3 %collective-permute-start.2 = (bf16[512,512]{1,0:T(8,128)(2,1)S(1)}, bf16[512,512]{1,0:T(8,128)(2,1)S(1)}, u32[]{:S(2)}, u32[]{:S(2)}) collective-permute-start(bf16[512,512]{1,0:T(8,128)(2,1)S(1)} %collective-permute-done.1.below_ref), channel_id=1, source_target_pairs={{0,1},{1,0},{2,3},{3,2},{4,5},{5,4},{6,7},{7,6},{8,9},{9,8},{10,11... | collective-permute-start | bytes 1572872 | tf_op jit(solution)/shard_map/ppermute | solution.py:30
  23.8 1.5 %collective-permute-start.3 = (bf16[64,8,256]{2,1,0:T(8,128)(2,1)S(1)}, bf16[64,8,256]{2,1,0:T(8,128)(2,1)S(1)}, u32[]{:S(2)}, u32[]{:S(2)}) collective-permute-start(bf16[64,8,256]{2,1,0:T(8,128)(2,1)S(1)} %bitcast.9), channel_id=1, source_target_pairs={{0,1},{1,0},{2,3},{3,2},{4,5},{5,4},{6,7},{7,6},{8,9},{9,8},{10,11... | collective-permute-start | bytes 786440 | tf_op jit(solution)/shard_map/ppermute | solution.py:30
  106.3 8.6 %collective-permute-start.4 = (bf16[64,8,2176]{2,1,0:T(8,128)(2,1)S(1)}, bf16[64,8,2176]{2,1,0:T(8,128)(2,1)}, u32[]{:S(2)}, u32[]{:S(2)}) collective-permute-start(bf16[64,8,2176]{2,1,0:T(8,128)(2,1)S(1)} %all_to_all.15.mine_ref.got_ref), channel_id=1, source_target_pairs={{0,1},{1,0},{2,3},{3,2},{4,5},{5,4},{6,7},{7,6},{8,9},{9,8},{10,11... | collective-permute-start | bytes 6684680 | tf_op jit(solution)/shard_map/ppermute | solution.py:30
  110.2 34.8 %all-to-all-start.2 = ((bf16[128,8,1024]{2,1,0:T(8,128)(2,1)}), bf16[128,8,1024]{2,1,0:T(8,128)(2,1)}, u32[]{:S(2)}, u32[]{:S(2)}) async-start(bf16[128,8,1024]{2,1,0:T(8,128)(2,1)} %third_operand.1), calls=%async_computation.2 | async-start | bytes 4194304 | tf_op jit(solution)/shard_map/all_to_all | solution.py:678
  120.8 2.7 %collective-permute-start.5 = (bf16[512,512]{1,0:T(8,128)(2,1)S(1)}, bf16[512,512]{1,0:T(8,128)(2,1)S(1)}, u32[]{:S(2)}, u32[]{:S(2)}) collective-permute-start(bf16[512,512]{1,0:T(8,128)(2,1)S(1)} %get-tuple-element.20.own_ref), channel_id=1, source_target_pairs={{0,1},{1,0},{2,3},{3,2},{4,5},{5,4},{6,7},{7,6},{8,9},{9,8},{10,11... | collective-permute-start | bytes 1572872 | tf_op jit(solution)/shard_map/ppermute | solution.py:30
  127.2 17.8 %copy-start = (bf16[4,8,128]{2,1,0:T(8,128)(2,1)S(1)}, bf16[4,8,128]{2,1,0:T(8,128)(2,1)}, u32[]{:S(2)}) copy-start(bf16[4,8,128]{2,1,0:T(8,128)(2,1)} %get-tuple-element.27.spare_ref) | copy-start | bytes 24580
  127.2 22.3 %collective-permute-start.6 = (bf16[512,512]{1,0:T(8,128)(2,1)}, bf16[512,512]{1,0:T(8,128)(2,1)S(1)}, u32[]{:S(2)}, u32[]{:S(2)}) collective-permute-start(bf16[512,512]{1,0:T(8,128)(2,1)} %get-tuple-element.22), channel_id=1, source_target_pairs={{0,8},{8,0},{16,24},{24,16},{32,40},{40,32},{48,56},{56,48},{64,72... | collective-permute-start | bytes 1572872 | tf_op jit(solution)/shard_map/ppermute | solution.py:30
